TPU v7x, 32 devices: a whole 2x2x4 slice. The times are simulated.
32 devices in a mesh: grp: 2 (over y), row: 4 (over z), col: 4 (over x, core).
Axes of the slice: x: 2, y: 2, z: 4, core: 2. Of those that a mesh axis runs over, the one named last changes fastest.
Arguments:
- frames: bfloat16 [16, 24576], P(None, ('grp', 'row', 'col')), parts along dimension 1, may hold values from -6 to 6
- vectors: bfloat16 [16, 24576], P(None, ('grp', 'row', 'col')), parts along dimension 1, may hold values from -8 to 8
- degrees: float32 [24576], P(('grp', 'row', 'col')), parts along dimension 0, may hold values from 1 to 10
- tile_table: int32 [16, 8, 2], replicated, may hold values from -1 to 15, as said below
Outputs:
- basis: float32 [16, 24576], P(None, ('grp', 'row', 'col')), parts along dimension 1
- ritz: float32 [32, 16], P('grp'), parts along dimension 0
There are 2 independent parts, one for each index of `grp`. A program takes and returns all parts, laid end to end along the dimension named above; an argument that names none is the same for every part. Nothing has to cross between parts.
Inputs may be any that keep to these rules, and one draw needn't show every extreme that they name: `tile_table`: row d lists the tiles computed by device d of row+col (index row * 4 + col): pairs (I, J) of frame blocks with I <= J, filled from the front, the remaining slots -1 in both entries. Every pair (I, I) is listed once, every other pair at most once, 76 pairs in all. Some device has all 8 slots filled.
All inputs are finite; a program needn't handle non-finite values.
Results may differ from a plain program's by a relative error of at most 0.0047.
Values may be sent and summed in bfloat16 or wider, within the bound.
No kernel may reach another device: no remote copies, remote signals or barrier semaphores. Data moves between devices by JAX's collectives and lax.ppermute only.
A program may use at most 64 MiB of HBM per device.

v0:
```python
import math

import jax
import jax.numpy as jnp
from jax import lax
from jax.sharding import PartitionSpec as P

kernel_width = 4.0


def tile_terms(frames_all, scaled_all, first, second, rows):
    left_x = lax.dynamic_slice_in_dim(frames_all, first * rows, rows, 1)
    right_x = lax.dynamic_slice_in_dim(frames_all, second * rows, rows, 1)
    left_v = lax.dynamic_slice_in_dim(scaled_all, first * rows, rows, 1)
    right_v = lax.dynamic_slice_in_dim(scaled_all, second * rows, rows, 1)
    left_sq = jnp.sum(jnp.square(left_x.astype(jnp.float32)), axis=0)
    right_sq = jnp.sum(jnp.square(right_x.astype(jnp.float32)), axis=0)
    cross = lax.dot_general(
        left_x, right_x, (((0,), (0,)), ((), ())), preferred_element_type=jnp.float32
    )
    dist = left_sq[:, None] + right_sq[None, :] - 2.0 * cross
    kern = jnp.exp(-dist / kernel_width).astype(jnp.bfloat16)
    to_left = lax.dot_general(
        right_v, kern, (((1,), (1,)), ((), ())), preferred_element_type=jnp.float32
    )
    to_right = lax.dot_general(
        left_v, kern, (((1,), (0,)), ((), ())), preferred_element_type=jnp.float32
    )
    return (to_left, to_right)


def add_block(image, term, start):
    old = lax.dynamic_slice_in_dim(image, start, term.shape[1], 1)
    return lax.dynamic_update_slice_in_dim(image, old + term, start, 1)


def per_device(frames, vectors, degrees, tile_table):
    rows = frames.shape[1]
    devices = lax.axis_size("row") * lax.axis_size("col")
    total_frames = rows * devices
    scale_root = lax.rsqrt(degrees)
    scaled = (vectors.astype(jnp.float32) * scale_root[None, :]).astype(jnp.bfloat16)
    vector_local = jnp.dot(vectors, vectors.T, preferred_element_type=jnp.float32)
    vector_gram = lax.psum(vector_local, ("row", "col"))
    frames_all, scaled_all = (
        lax.all_gather(frames, ("row", "col"), axis=1, tiled=True),
        lax.all_gather(scaled, ("row", "col"), axis=1, tiled=True),
    )
    device_index = lax.axis_index(("row", "col"))
    own_rows = lax.dynamic_index_in_dim(tile_table, device_index, 0, keepdims=False)
    count = jnp.sum((own_rows[:, 0] >= 0).astype(jnp.int32))

    def pick(step):
        return own_rows[step]

    def visit(step, image):
        pair = pick(step)
        first = pair[0]
        second = pair[1]
        to_left, to_right = tile_terms(frames_all, scaled_all, first, second, rows)
        image = add_block(image, to_left, first * rows)
        weight = (first != second).astype(jnp.float32)
        return add_block(image, to_right * weight, second * rows)

    image = lax.fori_loop(0, count, visit, jnp.zeros((vectors.shape[0], total_frames), jnp.float32))
    image_own = lax.psum_scatter(image, ("row", "col"), scatter_dimension=1, tiled=True)
    applied = image_own * scale_root[None, :]
    image_local = jnp.dot(applied, applied.T, precision=lax.Precision.HIGHEST)
    cross_local = jnp.dot(vectors.astype(jnp.float32), applied.T, precision=lax.Precision.HIGHEST)
    image_gram, cross_gram = lax.psum((image_local, cross_local), ("row", "col"))
    image_factor = jnp.linalg.cholesky(image_gram)
    basis = jax.scipy.linalg.solve_triangular(image_factor, applied, lower=True) * math.sqrt(
        total_frames
    )
    vector_factor = jnp.linalg.cholesky(vector_gram)
    half = jax.scipy.linalg.solve_triangular(vector_factor, cross_gram, lower=True)
    ritz = jax.scipy.linalg.solve_triangular(vector_factor, half.T, lower=True).T
    return (basis, ritz)


def solution(mesh):
    return jax.shard_map(
        per_device,
        mesh=mesh,
        in_specs=(
            P(None, ("grp", "row", "col")),
            P(None, ("grp", "row", "col")),
            P(("grp", "row", "col")),
            P(),
        ),
        out_specs=(P(None, ("grp", "row", "col")), P("grp", None)),
        check_vma=False,
    )
```

profile of v0, /device:TPU:0, one launch (start us, length us, event | category | flops | bytes accessed | tf_op | source)
XLA Modules:
  0.0 230.0 jit_solution(10784557413882215366)
XLA Ops:
  7.2 0.6 copy-done
  8.0 0.6 fusion.24
  8.7 0.7 rsqrt.3
  9.4 0.7 multiply_convert_fusion
  10.1 24.1 %all_gather.6 = bf16[16,12288]{1,0:T(8,128)(2,1)S(1)} all-gather(bf16[16,768]{1,0:T(8,128)(2,1)S(1)} %multiply_convert_fusion), channel_id=1, replica_groups=mesh['grp'=2,'row'=4,'col'=4] {'row','col'}, dimensions={1}, use_global_device_ids=true | all-gather | bytes 417792 | tf_op jit(solution)/shard_map/all_gather | solution.py:47
  34.2 18.7 %all_gather.7 = bf16[16,12288]{1,0:T(8,128)(2,1)S(1)} all-gather(bf16[16,768]{1,0:T(8,128)(2,1)} %param.9), channel_id=1, replica_groups=mesh['grp'=2,'row'=4,'col'=4] {'row','col'}, dimensions={1}, use_global_device_ids=true | all-gather | bytes 417792 | tf_op jit(solution)/shard_map/all_gather | solution.py:46
  53.0 22.1 %while.10 = (s32[]{:T(128)}, f32[16,12288]{1,0:T(8,128)S(1)}, s32[]{:T(128)}, s32[8,2]{0,1:T(2,128)S(1)}, bf16[16,12288]{1,0:T(8,128)(2,1)S(1)}, /*index=5*/bf16...) while((s32[]{:T(128)}, f32[16,12288]{1,0:T(8,128)S(1)}, ...), condition=%wide.region_4.0_spmd, body=%wide.region_1.4_spmd.sunk | while | flops 60271116 | bytes 3897665 | solution.py:65
  53.8 0.6 fusion.49
  55.7 0.7 exponential_convert_fusion.2
  56.4 0.4 fusion.50
  59.1 0.6 fusion.49
  61.1 0.7 exponential_convert_fusion.2
  64.5 0.6 fusion.49
  66.4 0.7 exponential_convert_fusion.2
  67.1 0.4 fusion.50
  69.9 0.6 fusion.49
  71.8 0.7 exponential_convert_fusion.2
  75.2 0.9 copy-done.1
  76.2 76.3 %reduce-scatter.2.cloned.1.call-done = f32[16,768]{1,0:T(8,128)} async-done(((f32[16,12288]{1,0:T(8,128)}), f32[16,768]{1,0:T(8,128)}) %reduce-scatter.2.cloned.1.call-update) | async-done | bytes 49168 | tf_op jit(solution)/shard_map/reduce_scatter | solution.py:66
  152.5 0.9 convolution_bitcast_fusion.2
  153.4 1.1 fusion.12
  154.5 57.7 %all-reduce = (f32[16,16]{0,1:T(8,128)S(1)}, f32[16,16]{0,1:T(8,128)S(1)}, f32[16,16]{0,1:T(8,128)S(1)}) all-reduce(f32[16,16]{0,1:T(8,128)S(1)} %fusion.12, f32[16,16]{0,1:T(8,128)S(1)} %convolution_bitcast_fusion.2, f32[16,16]{0,1:T(8,128)S(1)} %fusion.26), channel_id=1, replica_groups=mesh['grp'=2,'row'=4,'col'=4] {'row','col'}, use_global_device_ids=true, to_apply=%region_6.7 | all-reduce | flops 768 | bytes 6144 | tf_op jit(solution)/shard_map/psum | solution.py:70
  212.3 1.5 cholesky.55
  213.8 0.6 compare_reduce_fusion
  214.5 0.6 fusion.18
  215.1 1.2 custom-call.12
  216.8 0.7 copy.11
  217.5 1.4 cholesky.44
  218.9 0.6 compare_reduce_fusion.1
  219.6 0.6 fusion.17
  220.2 1.2 custom-call.9
  221.5 1.7 convolution_multiply_fusion.1
  (31 shorter events, 3.4 us)
Async XLA Ops:
  7.2 0.7 copy-start
  7.2 145.3 %reduce-scatter.2.cloned.1.call-start = ((), (), s32[]{:S(2)}) async-start(), calls=%async_computation.1 | async-start | bytes 835584 | tf_op jit(solution)/shard_map/reduce_scatter | solution.py:66
  53.0 23.0 %copy-start.2 = (bf16[16,768]{1,0:T(8,128)(2,1)S(1)}, bf16[16,768]{1,0:T(8,128)(2,1)}, u32[]{:S(2)}) copy-start(bf16[16,768]{1,0:T(8,128)(2,1)} %param.10) | copy-start | bytes 73732
  75.1 0.9 copy-start.1
Sparse Core Ops, SparseCore 0:
  76.2 76.3 reduce-scatter.1
where the time goes:
time: 230 us
  blocking collectives  101 us (44%)
  waiting for transfers between devices  76.4 us (33%)
  between operations  14.1 us (6%)
  loops' own time  13.7 us (6%)
  matrix products  9.8 us (4%)
  other arithmetic  9.53 us (4%)
  local copies, waits for them, and re-layouts  5.95 us (3%)
    reduce_scatter x1, waiting for transfers between devices, per_device(): lax.psum_scatter(image, ('row', 'col'), scatter_dimension=1, tiled=True)  76.3 us
    psum x1, blocking collectives, per_device(): lax.psum((image_local, cross_local), ('row', 'col'))  57.7 us
    all_gather x1, blocking collectives, per_device(): lax.all_gather(scaled, ('row', 'col'), axis=1, tiled=True)  24.1 us
    all_gather x1, blocking collectives, per_device(): lax.all_gather(frames, ('row', 'col'), axis=1, tiled=True)  18.7 us
    another operation x1, loops' own time, per_device(): lax.fori_loop(0, count, visit, jnp.zeros((vectors.shape[0], total_frames)...  13.7 us
  transfers between devices with their start and end apart: 1, of which 1 were waited for; matrix products, arithmetic and copies ran while one was open for 0% of the time, Pallas kernels for 0%

commit v1 on v0

v1 whole, which is shorter than its diff:
```python
import functools
import math

import jax
import jax.numpy as jnp
from jax import lax
from jax.experimental import pallas as pl
from jax.experimental.pallas import tpu as pltpu
from jax.sharding import PartitionSpec as P

unit = -math.log2(math.e) / 4.0

NT = (((1,), (1,)), ((), ()))
TN = (((0,), (0,)), ((), ()))


def split3(x):
    high = x.astype(jnp.bfloat16).astype(jnp.float32)
    rest = x - high
    mid = rest.astype(jnp.bfloat16).astype(jnp.float32)
    low = (rest - mid).astype(jnp.bfloat16).astype(jnp.float32)
    return high, mid, low


def pack_kernel(frames_ref, vectors_ref, degrees_ref, out_ref):
    ncv = frames_ref.shape[0]
    root = lax.rsqrt(degrees_ref[...])
    out_ref[:ncv, :] = frames_ref[...]
    out_ref[ncv:, :] = (vectors_ref[...].astype(jnp.float32) * root).astype(jnp.bfloat16)


def edge_rows(square, ones_first):
    high, mid, low = split3(square * unit)
    shape = (16, square.shape[1])
    row = lax.broadcasted_iota(jnp.int32, shape, 0)
    base = 3 if ones_first else 0
    ones_at = 0 if ones_first else 3
    block = jnp.where((row >= ones_at) & (row < ones_at + 3), 1.0, 0.0)
    block = jnp.where(row == base, high, block)
    block = jnp.where(row == base + 1, mid, block)
    block = jnp.where(row == base + 2, low, block)
    return block.astype(jnp.bfloat16)


def image_kernel(
    list_ref, count_ref, all_ref, own_ref, vectors_ref, degrees_ref,
    applied_ref, gram_ref, left_ref, image_ref,
):
    ncv = own_ref.shape[0]
    own = own_ref[...].astype(jnp.float32)
    high, mid, low = split3(own * (-2.0 * unit))
    square = jnp.sum(own * own, axis=0, keepdims=True)
    edge = edge_rows(square, True).astype(jnp.float32)
    left = jnp.concatenate([high, mid, low, edge], axis=0)
    left_ref[...] = left.T.astype(jnp.bfloat16)
    image_ref[...] = jnp.zeros_like(image_ref)

    def visit(step, _):
        block = list_ref[step]
        x = all_ref[block, :ncv, :]
        v = all_ref[block, ncv:, :]
        wide = x.astype(jnp.float32)
        edge = edge_rows(jnp.sum(wide * wide, axis=0, keepdims=True), False)
        right = jnp.concatenate([x, x, x, edge], axis=0)
        power = jnp.dot(left_ref[...], right, preferred_element_type=jnp.float32)
        kern = jnp.exp2(power).astype(jnp.bfloat16)
        image_ref[...] += lax.dot_general(kern, v, NT, preferred_element_type=jnp.float32)
        return 0

    lax.fori_loop(0, count_ref[0], visit, 0)
    applied = image_ref[...].T * lax.rsqrt(degrees_ref[...])
    applied_ref[...] = applied
    both = jnp.concatenate([applied, vectors_ref[...].astype(jnp.float32)], axis=0)
    gram_ref[...] = lax.dot_general(
        both, both, NT, precision=lax.Precision.HIGHEST, preferred_element_type=jnp.float32
    )


def inverse_factor(gram):
    n = gram.shape[0]
    shape = (n, 2 * n)
    row = lax.broadcasted_iota(jnp.int32, shape, 0)
    lane = lax.broadcasted_iota(jnp.int32, shape, 1)
    work = jnp.concatenate([gram, (row == lane).astype(jnp.float32)[:, :n]], axis=1)
    for k in range(n - 1):
        column = jnp.broadcast_to(work[:, k : k + 1], shape)
        factor = jnp.where(row > k, column / column[k : k + 1, :], 0.0)
        work = work - factor * work[k : k + 1, :]
    pivot = jnp.sum(jnp.where(row == lane, work, 0.0), axis=1, keepdims=True)
    return work[:, n:] * lax.rsqrt(pivot)


def finish_kernel(total_frames, grams_ref, applied_ref, basis_ref, ritz_ref):
    gram = jnp.sum(grams_ref[...], axis=0)
    n = applied_ref.shape[0]
    exact = functools.partial(
        lax.dot_general, precision=lax.Precision.HIGHEST, preferred_element_type=jnp.float32
    )
    plain = (((1,), (0,)), ((), ()))
    image_inverse = inverse_factor(gram[:n, :n])
    vector_inverse = inverse_factor(gram[n:, n:])
    basis_ref[...] = exact(image_inverse * math.sqrt(total_frames), applied_ref[...], plain)
    half = exact(vector_inverse, gram[n:, :n], plain)
    ritz_ref[...] = exact(half, vector_inverse, NT)


def per_device(frames, vectors, degrees, tile_table):
    ncv, rows = frames.shape
    nvec = vectors.shape[0]
    axes = ("row", "col")
    devices = lax.axis_size("row") * lax.axis_size("col")
    me = lax.axis_index(axes)
    degrees = degrees[None, :]
    vmem = pl.BlockSpec(memory_space=pltpu.VMEM)
    smem = pl.BlockSpec(memory_space=pltpu.SMEM)
    params = pltpu.CompilerParams(vmem_limit_bytes=48 * 1024 * 1024)

    packed = pl.pallas_call(
        pack_kernel,
        out_shape=jax.ShapeDtypeStruct((ncv + nvec, rows), jnp.bfloat16),
        in_specs=[vmem] * 3,
        out_specs=vmem,
        name="pack",
    )(frames, vectors, degrees)
    everything = lax.all_gather(packed, axes, axis=0)

    first, second = tile_table[..., 0].reshape(-1), tile_table[..., 1].reshape(-1)
    blocks = jnp.arange(devices, dtype=jnp.int32)
    linked = jnp.any(
        ((first == me)[None, :] & (second[None, :] == blocks[:, None]))
        | ((second == me)[None, :] & (first[None, :] == blocks[:, None])),
        axis=1,
    ).astype(jnp.int32)
    place = jnp.sum(jnp.where(blocks[None, :] < blocks[:, None], linked[None, :], 0), axis=1)
    chosen = (place[None, :] == blocks[:, None]) & (linked[None, :] == 1)
    order = jnp.sum(jnp.where(chosen, blocks[None, :], 0), axis=1)
    count = jnp.sum(linked)[None]

    applied, gram = pl.pallas_call(
        image_kernel,
        out_shape=(
            jax.ShapeDtypeStruct((nvec, rows), jnp.float32),
            jax.ShapeDtypeStruct((2 * nvec, 2 * nvec), jnp.float32),
        ),
        in_specs=[smem, smem, vmem, vmem, vmem, vmem],
        out_specs=(vmem, vmem),
        scratch_shapes=[
            pltpu.VMEM((rows, 3 * ncv + 16), jnp.bfloat16),
            pltpu.VMEM((rows, nvec), jnp.float32),
        ],
        compiler_params=params,
        name="image",
    )(order, count, everything, frames, vectors, degrees)

    grams = lax.all_gather(gram, axes, axis=0)
    basis, ritz = pl.pallas_call(
        functools.partial(finish_kernel, rows * devices),
        out_shape=(
            jax.ShapeDtypeStruct((nvec, rows), jnp.float32),
            jax.ShapeDtypeStruct((nvec, nvec), jnp.float32),
        ),
        in_specs=[vmem, vmem],
        out_specs=(vmem, vmem),
        name="finish",
    )(grams, applied)
    return (basis, ritz)


def solution(mesh):
    split = P(None, ("grp", "row", "col"))
    return jax.shard_map(
        per_device,
        mesh=mesh,
        in_specs=(split, split, P(("grp", "row", "col")), P()),
        out_specs=(split, P("grp", None)),
        check_vma=False,
    )
```

time: 230 us -> 64.9 us (0.28)
  waiting for transfers between devices: 76.4 us -> 0 us
  blocking collectives: 101 us -> 47.1 us
  Pallas kernels: 0 us -> 14.6 us
  loops' own time: 13.7 us -> 0 us
  between operations: 14.1 us -> 0.7 us
  matrix products: 9.8 us -> 0 us
  other arithmetic: 9.53 us -> 1.08 us
  local copies, waits for them, and re-layouts: 5.95 us -> 1.6 us
    reduce_scatter x1 -> x0, waiting for transfers between devices: 76.3 us -> none  [per_device(): lax.psum_scatter(image, ('row', 'col'), scatter_dimension=1, tiled=True)]
    psum x1 -> x0, blocking collectives: 57.7 us -> none  [per_device(): lax.psum((image_local, cross_local), ('row', 'col'))]
    pallas_call x0 -> x3, Pallas kernels: none -> 14.6 us  [the longest x1 7.83 us: per_device(): pl.pallas_call(image_kernel, out_shape=(jax.ShapeDtypeStruct((nvec, rows)...]
    another operation x1 -> x0, loops' own time: 13.7 us -> none  [per_device(): lax.fori_loop(0, count, visit, jnp.zeros((vectors.shape[0], total_frames)...]
    another operation x10 -> x0, other arithmetic: 8.01 us -> none  [the longest x3 2.13 us: per_device(): vector_factor = jnp.linalg.cholesky(vector_gram)]
    dot_general x15 -> x0, matrix products: 7.72 us -> none  [the longest x4 2.8 us: tile_terms(): lax.dot_general(left_x, right_x, (((0,), (0,)), ((), ())), preferred_elem...]
    all_gather x2, blocking collectives: 42.9 us -> 47.1 us  [the longest x1 25.8 us: per_device(): everything = lax.all_gather(packed, axes, axis=0)]
  transfers between devices with their start and end apart: 1 -> 0, of which waited for: 1 -> 0; matrix products, arithmetic and copies ran while one was open for 0% -> 0% of each run, Pallas kernels for 0% -> 0%
where the time goes in v1:
time: 64.9 us; the launch traced here: 65.1 us
  blocking collectives  47.1 us (73%)
  Pallas kernels  14.6 us (22%)
  local copies, waits for them, and re-layouts  1.6 us (2%)
  other arithmetic  1.08 us (2%)
  between operations  0.7 us (1%)
    all_gather x1, blocking collectives, per_device(): everything = lax.all_gather(packed, axes, axis=0)  25.8 us
    all_gather x1, blocking collectives, per_device(): grams = lax.all_gather(gram, axes, axis=0)  21.3 us
    pallas_call x1, Pallas kernels, per_device(): pl.pallas_call(image_kernel, out_shape=(jax.ShapeDtypeStruct((nvec, rows)...  7.83 us
    pallas_call x1, Pallas kernels, per_device(): pl.pallas_call(functools.partial(finish_kernel, rows * devices), out_shap...  5.38 us
    pallas_call x1, Pallas kernels, per_device(): pl.pallas_call(pack_kernel, out_shape=jax.ShapeDtypeStruct((ncv + nvec, r...  1.4 us

profile of v1, /device:TPU:0, one launch (start us, length us, event | category | flops | bytes accessed | tf_op | source)
XLA Modules:
  0.0 65.1 jit_solution(15256983680337697251)
XLA Ops:
  0.6 0.0 copy-start.5
  0.6 0.0 copy-start.4
  0.7 0.7 %copy-done.5 = f32[768]{0:T(1024)S(1)} copy-done((f32[768]{0:T(1024)S(1)}, f32[768]{0:T(1024)}, u32[]{:S(2)}) %copy-start.5) | copy-done | bytes 3096
  1.3 0.6 broadcast_in_dim.36.degrees_ref
  1.9 0.0 copy-done.4
  1.9 0.1 copy.11
  2.0 0.1 eq.67
  2.1 0.1 copy.10
  2.1 0.1 reshape_squeeze.4
  2.3 0.1 fusion.3
  2.4 0.7 %convert_reduce_fusion = s32[]{:T(128)} fusion(pred[16]{0:T(512)(128)(4,1)S(1)} %fusion.3), kind=kLoop, calls=%fused_computation.14 | loop fusion | flops 31 | bytes 20 | tf_op jit(solution)/shard_map/reduce_sum | solution.py:137
  3.1 0.1 select_reduce_fusion.1
  3.2 0.1 select_reduce_fusion.list_ref
  3.3 1.4 %pack.1 = bf16[32,768]{1,0:T(8,128)(2,1)} custom-call(bf16[16,768]{1,0:T(8,128)(2,1)} %own_ref.1, bf16[16,768]{1,0:T(8,128)(2,1)} %vectors_ref.3, f32[1,768]{1,0:T(1,128)} %broadcast_in_dim.36.degrees_ref), custom_call_target="tpu_custom_call" | custom-call | tf_op jit(solution)/shard_map/pack/pallas_call | solution.py:118
  4.7 0.0 copy-start
  4.7 0.0 copy-start.1
  4.7 0.0 copy-start.3
  4.7 25.8 %all-gather = bf16[512,768]{1,0:T(8,128)(2,1)S(1)} all-gather(bf16[32,768]{1,0:T(8,128)(2,1)} %pack.1), channel_id=2, replica_groups=mesh['grp'=2,'row'=4,'col'=4] {'row','col'}, dimensions={0}, use_global_device_ids=true | all-gather | bytes 835584 | tf_op jit(solution)/shard_map/all_gather | solution.py:125
  30.5 0.0 copy-done
  30.5 0.0 copy-done.1
  30.5 0.0 copy-done.3
  30.5 7.8 %image.1 = (f32[16,768]{1,0:T(8,128)S(1)}, f32[32,32]{1,0:T(8,128)S(1)}) custom-call(s32[16]{0:T(128)S(1)} %select_reduce_fusion.list_ref, s32[1]{0:T(128)} %bitcast.count_ref, bf16[16,32,768]{2,1,0:T(8,128)(2,1)S(1)} %bitcast.7, bf16[16,768]{1,0:T(8,128)(2,1)S(1)} %copy-done, bf16[16,768]{1,0:T(8,128)(2,1)S(1)} %copy-done.1, f32[1,768]{1,0:T(1,128)S(1)} %copy-done.3), custom_call_target="tpu_custom_call" | custom-call | tf_op jit(solution)/shard_map/image/pallas_call | solution.py:139
  38.4 0.0 copy-start.2
  38.4 21.3 %all-gather.1 = f32[512,32]{1,0:T(8,128)} all-gather(f32[32,32]{1,0:T(8,128)S(1)} %get-tuple-element.4), channel_id=3, replica_groups=mesh['grp'=2,'row'=4,'col'=4] {'row','col'}, dimensions={0}, use_global_device_ids=true | all-gather | bytes 69632 | tf_op jit(solution)/shard_map/all_gather | solution.py:155
  59.7 0.0 copy-done.2
  59.7 5.4 %finish.1 = (f32[16,768]{1,0:T(8,128)}, f32[16,16]{1,0:T(8,128)}) custom-call(f32[16,32,32]{2,1,0:T(8,128)} %bitcast.8, f32[16,768]{1,0:T(8,128)} %copy-done.2), custom_call_target="tpu_custom_call" | custom-call | tf_op jit(solution)/shard_map/finish/pallas_call | solution.py:156
  (3 shorter events, 0.0 us)
Async XLA Ops:
  0.6 0.7 %copy-start.5 = (f32[768]{0:T(1024)S(1)}, f32[768]{0:T(1024)}, u32[]{:S(2)}) copy-start(f32[768]{0:T(1024)} %param.6) | copy-start | bytes 9220
  0.6 1.3 %copy-start.4 = (s32[16,8,2]{0,2,1:T(2,128)S(1)}, s32[16,8,2]{0,2,1:T(2,128)}, u32[]{:S(2)}) copy-start(s32[16,8,2]{0,2,1:T(2,128)} %param.7) | copy-start | bytes 3076
  4.7 25.8 %copy-start = (bf16[16,768]{1,0:T(8,128)(2,1)S(1)}, bf16[16,768]{1,0:T(8,128)(2,1)}, u32[]{:S(2)}) copy-start(bf16[16,768]{1,0:T(8,128)(2,1)} %own_ref.1) | copy-start | bytes 73732
  4.7 25.8 %copy-start.1 = (bf16[16,768]{1,0:T(8,128)(2,1)S(1)}, bf16[16,768]{1,0:T(8,128)(2,1)}, u32[]{:S(2)}) copy-start(bf16[16,768]{1,0:T(8,128)(2,1)} %vectors_ref.3) | copy-start | bytes 73732
  4.7 25.8 %copy-start.3 = (f32[1,768]{1,0:T(1,128)S(1)}, f32[1,768]{1,0:T(1,128)}, u32[]{:S(2)}) copy-start(f32[1,768]{1,0:T(1,128)} %broadcast_in_dim.36.degrees_ref) | copy-start | bytes 9220
  38.4 21.3 %copy-start.2 = (f32[16,768]{1,0:T(8,128)}, f32[16,768]{1,0:T(8,128)S(1)}, u32[]{:S(2)}) copy-start(f32[16,768]{1,0:T(8,128)S(1)} %get-tuple-element.5.applied_ref) | copy-start | bytes 147460

commit v2 on v1

v2 whole, which is shorter than its diff:
```python
import functools
import math

import jax
import jax.numpy as jnp
from jax import lax
from jax.experimental import pallas as pl
from jax.experimental.pallas import tpu as pltpu
from jax.sharding import PartitionSpec as P

unit = -math.log2(math.e) / 4.0

NT = (((1,), (1,)), ((), ()))
MIB = 1024 * 1024


def split3(x):
    high = x.astype(jnp.bfloat16).astype(jnp.float32)
    rest = x - high
    mid = rest.astype(jnp.bfloat16).astype(jnp.float32)
    low = (rest - mid).astype(jnp.bfloat16).astype(jnp.float32)
    return high, mid, low


def pack_kernel(frames_ref, vectors_ref, degrees_ref, out_ref):
    ncv = frames_ref.shape[0]
    root = lax.rsqrt(degrees_ref[...])[None, :]
    out_ref[:ncv, :] = frames_ref[...]
    out_ref[ncv:, :] = (vectors_ref[...].astype(jnp.float32) * root).astype(jnp.bfloat16)


def edge_rows(square, ones_first):
    high, mid, low = split3(square * unit)
    row = lax.broadcasted_iota(jnp.int32, (16, square.shape[1]), 0)
    base = 3 if ones_first else 0
    ones_at = 0 if ones_first else 3
    block = jnp.where((row >= ones_at) & (row < ones_at + 3), 1.0, 0.0)
    block = jnp.where(row == base, high, block)
    block = jnp.where(row == base + 1, mid, block)
    return jnp.where(row == base + 2, low, block)


def own_side(own):
    own = own.astype(jnp.float32)
    high, mid, low = split3(own * (-2.0 * unit))
    edge = edge_rows(jnp.sum(own * own, axis=0, keepdims=True), True)
    return jnp.concatenate([high, mid, low, edge], axis=0).T.astype(jnp.bfloat16)


def tile_image(left, x, v):
    wide = x.astype(jnp.float32)
    edge = edge_rows(jnp.sum(wide * wide, axis=0, keepdims=True), False).astype(jnp.bfloat16)
    right = jnp.concatenate([x, x, x, edge], axis=0)
    power = jnp.dot(left, right, preferred_element_type=jnp.float32)
    kern = jnp.exp2(power).astype(jnp.bfloat16)
    return lax.dot_general(kern, v, NT, preferred_element_type=jnp.float32)


def own_kernel(packed_ref, left_ref, image_ref):
    ncv = packed_ref.shape[0] // 2
    x = packed_ref[:ncv, :]
    left_ref[...] = own_side(x)
    image_ref[...] = tile_image(left_ref[...], x, packed_ref[ncv:, :])


def add_blocks(part, sizes, table_ref, left_ref, blocks_ref, image_ref):
    n_row, n_col = sizes
    ncv = blocks_ref.shape[1] // 2
    my_row, my_col = lax.axis_index("row"), lax.axis_index("col")
    me = my_row * n_col + my_col
    first, second = table_ref[:, 0, :], table_ref[:, 1, :]
    other = jnp.where(first == me, second, jnp.where(second == me, first, -1))
    words = []
    for start in range(0, n_row * n_col, 16):
        bit = jnp.zeros(other.shape, jnp.float32)
        for b in range(16):
            bit = jnp.where(other == start + b, float(1 << b), bit)
        words.append(jnp.sum(bit).astype(jnp.int32))
    lane_col = my_col ^ 1 if part in ("core", "far") else my_col

    def visit(step, _):
        shift = step // n_row + 1 if part in ("across", "far") else 0
        from_row = (my_row - step % n_row + n_row) % n_row
        from_col = (lane_col - 2 * shift + 2 * n_col) % n_col
        block = from_row * n_col + from_col
        word = words[0]
        for w in range(1, len(words)):
            word = jnp.where(block // 16 == w, words[w], word)

        @pl.when(((word >> (block % 16)) & 1) == 1)
        def _():
            image_ref[...] += tile_image(
                left_ref[...], blocks_ref[step, :ncv, :], blocks_ref[step, ncv:, :]
            )

        return 0

    lax.fori_loop(1 if part == "line" else 0, blocks_ref.shape[0], visit, 0)


def part_kernel(part, sizes, table_ref, left_ref, blocks_ref, before_ref, image_ref):
    image_ref[...] = before_ref[...]
    add_blocks(part, sizes, table_ref, left_ref, blocks_ref, image_ref)


def last_kernel(
    sizes, table_ref, left_ref, blocks_ref, before_ref, vectors_ref, degrees_ref,
    applied_ref, gram_ref, image_ref,
):
    image_ref[...] = before_ref[...]
    add_blocks("far", sizes, table_ref, left_ref, blocks_ref, image_ref)
    n = vectors_ref.shape[0]
    applied = image_ref[...].T * lax.rsqrt(degrees_ref[...])[None, :]
    applied_ref[...] = applied
    both = jnp.concatenate([applied, vectors_ref[...].astype(jnp.float32)], axis=0)
    gram = lax.dot_general(
        both, both, NT, precision=lax.Precision.HIGHEST, preferred_element_type=jnp.float32
    )
    wide = jnp.concatenate(
        [gram[:n, :n], gram[n:, :], jnp.zeros((n, n), jnp.float32)], axis=1
    )
    tile = jnp.concatenate([wide[: n // 2, :], wide[n // 2 :, :]], axis=1)
    for device in range(gram_ref.shape[0]):
        gram_ref[device] = tile


def inverse_factors(grams):
    n = grams[0].shape[0]
    half = 64
    tiles = range(n // 8)
    shape = (8, 2 * half)
    row = lax.broadcasted_iota(jnp.int32, shape, 0)
    lane = lax.broadcasted_iota(jnp.int32, shape, 1)
    columns = [
        [
            jnp.where(
                lane < half,
                jnp.broadcast_to(grams[0][8 * t : 8 * t + 8, j : j + 1], shape),
                jnp.broadcast_to(grams[1][8 * t : 8 * t + 8, j : j + 1], shape),
            )
            for t in tiles
        ]
        for j in range(n)
    ]
    right = [jnp.where(lane % half == row + 8 * t, 1.0, 0.0) for t in tiles]
    pivots = [jnp.ones(shape, jnp.float32) for t in tiles]
    for k in range(n):
        top, at = k // 8, k % 8
        pivot = columns[k][top][at : at + 1, :]
        pivots[top] = jnp.where(row == at, pivot, pivots[top])
        if k == n - 1:
            break
        scale = 1.0 / pivot
        factor = {t: columns[k][t] * scale for t in tiles if t >= top}
        factor[top] = jnp.where(row > at, factor[top], 0.0)
        for column in columns[k + 1 :] + [right]:
            line = column[top][at : at + 1, :]
            for t in factor:
                column[t] = column[t] - factor[t] * line
    result = jnp.concatenate([r * lax.rsqrt(p) for r, p in zip(right, pivots)], axis=0)
    return result[:, :n], result[:, half : half + n]


def finish_kernel(total_frames, grams_ref, applied_ref, basis_ref, ritz_ref):
    tile = grams_ref[0]
    for device in range(1, grams_ref.shape[0]):
        tile += grams_ref[device]
    n = applied_ref.shape[0]
    gram = jnp.concatenate([tile[:, : 4 * n], tile[:, 4 * n :]], axis=0)
    exact = functools.partial(
        lax.dot_general, precision=lax.Precision.HIGHEST, preferred_element_type=jnp.float32
    )
    plain = (((1,), (0,)), ((), ()))
    image_inverse, vector_inverse = inverse_factors([gram[:, :n], gram[:, 2 * n : 3 * n]])
    basis_ref[...] = exact(image_inverse * math.sqrt(total_frames), applied_ref[...], plain)
    half = exact(vector_inverse, gram[:, n : 2 * n], plain)
    ritz_ref[...] = exact(half, vector_inverse, NT)


def shifted(x, axis, step):
    size = lax.axis_size(axis)
    return lax.ppermute(x, axis, [(i, (i + step) % size) for i in range(size)])


def swapped(x):
    return lax.ppermute(x, "col", [(i, i ^ 1) for i in range(lax.axis_size("col"))])


def per_device(frames, vectors, degrees, tile_table):
    ncv, rows = frames.shape
    nvec = vectors.shape[0]
    n_row, n_col = lax.axis_size("row"), lax.axis_size("col")
    devices = n_row * n_col
    sizes = (n_row, n_col)
    vmem = pl.BlockSpec(memory_space=pltpu.VMEM)

    def call(kernel, name, outs, *args, limit=16, tiles=0, **keywords):
        shapes = [jax.ShapeDtypeStruct(*out) for out in outs]
        keywords["cost_estimate"] = pl.CostEstimate(
            flops=tiles * rows * rows * 2 * (4 * ncv + nvec),
            transcendentals=tiles * rows * rows,
            bytes_accessed=sum(a.size * a.dtype.itemsize for a in args),
        )
        return pl.pallas_call(
            kernel,
            out_shape=shapes,
            in_specs=[vmem] * len(args),
            out_specs=[vmem] * len(outs),
            compiler_params=pltpu.CompilerParams(vmem_limit_bytes=limit * MIB),
            name=name,
            **keywords,
        )(*args)

    table = tile_table.transpose(1, 2, 0)
    image_type = ((rows, nvec), jnp.float32)

    (packed,) = call(
        pack_kernel, "pack", [((ncv + nvec, rows), jnp.bfloat16)], frames, vectors, degrees
    )
    line = jnp.stack([packed] + [shifted(packed, "row", s) for s in range(1, n_row)])
    left, image = call(own_kernel, "own", [((rows, 3 * ncv + 16), jnp.bfloat16), image_type], packed, tiles=1)

    def add(part, blocks, image):
        (image,) = call(
            functools.partial(part_kernel, part, sizes),
            "add_" + part,
            [image_type],
            table,
            left,
            blocks,
            image,
            tiles=blocks.shape[0] // 2,
            input_output_aliases={3: 0},
        )
        return image

    line, image = lax.optimization_barrier((line, image))
    across = [shifted(line, "col", 2 * t) for t in range(1, n_col // 2)]
    across = across[0] if len(across) == 1 else jnp.concatenate(across)
    core = swapped(line)
    image = add("line", line, image)
    image = add("core", core, image)
    across, image = lax.optimization_barrier((across, image))
    far = swapped(across)
    image = add("across", across, image)
    applied, gram = call(
        functools.partial(last_kernel, sizes),
        "add_far",
        [((nvec, rows), jnp.float32), ((devices, nvec // 2, 8 * nvec), jnp.float32)],
        table,
        left,
        far,
        image,
        vectors,
        degrees,
        tiles=far.shape[0] // 2,
        scratch_shapes=[pltpu.VMEM(*image_type)],
    )
    grams = lax.all_to_all(gram, ("row", "col"), 0, 0)
    basis, ritz = call(
        functools.partial(finish_kernel, rows * devices),
        "finish",
        [((nvec, rows), jnp.float32), ((nvec, nvec), jnp.float32)],
        grams,
        applied,
    )
    return (basis, ritz)


def solution(mesh):
    split = P(None, ("grp", "row", "col"))
    return jax.shard_map(
        per_device,
        mesh=mesh,
        in_specs=(split, split, P(("grp", "row", "col")), P()),
        out_specs=(split, P("grp", None)),
        check_vma=False,
    )
```

time: 64.9 us -> 38.7 us (0.60)
  blocking collectives: 47.1 us -> 11.5 us
  starting transfers between devices: 0 us -> 7.74 us
  waiting for transfers between devices: 0 us -> 5.57 us
  Pallas kernels: 14.6 us -> 10.7 us
  other arithmetic: 1.08 us -> 0.03 us
    all_gather x2 -> x0, blocking collectives: 47.1 us -> none  [the longest x1 25.8 us: per_device(): everything = lax.all_gather(packed, axes, axis=0)]
    all_to_all x0 -> x1, blocking collectives: none -> 11.5 us  [per_device(): grams = lax.all_to_all(gram, ('row', 'col'), 0, 0)]
    ppermute x0 -> x6, starting transfers between devices: none -> 7.74 us  [the longest x4 7.67 us: shifted(): return lax.ppermute(x, axis, [(i, (i + step) % size) for i in range(size)])]
    ppermute x0 -> x6, waiting for transfers between devices: none -> 5.57 us  [the longest x4 5.22 us: shifted(): return lax.ppermute(x, axis, [(i, (i + step) % size) for i in range(size)])]
    pallas_call x3 -> x7, Pallas kernels: 14.6 us -> 10.7 us  [call(): pl.pallas_call(kernel, out_shape=shapes, in_specs=[vmem] * len(args), out...]
    unnamed x12, local copies, waits for them, and re-layouts: 0.69 us -> 2.17 us
    reduce_sum x3 -> x0, other arithmetic: 0.95 us -> none  [the longest x1 0.72 us: per_device(): count = jnp.sum(linked)[None]]
  transfers between devices with their start and end apart: 0 -> 6, of which waited for: 0 -> 5; matrix products, arithmetic and copies ran while one was open for 0% -> 0% of each run, Pallas kernels for 0% -> 17%
where the time goes in v2:
time: 38.7 us; the launch traced here: 38.4 us
  blocking collectives  11.5 us (30%)
  Pallas kernels  10.7 us (28%)
  starting transfers between devices  7.74 us (20%)
  waiting for transfers between devices  5.57 us (14%)
  local copies, waits for them, and re-layouts  2.17 us (6%)
  between operations  0.72 us (2%)
    all_to_all x1, blocking collectives, per_device(): grams = lax.all_to_all(gram, ('row', 'col'), 0, 0)  11.5 us
    pallas_call x7, Pallas kernels, call(): pl.pallas_call(kernel, out_shape=shapes, in_specs=[vmem] * len(args), out...  10.7 us
    ppermute x4, starting transfers between devices, shifted(): return lax.ppermute(x, axis, [(i, (i + step) % size) for i in range(size)])  7.67 us
    ppermute x4, waiting for transfers between devices, shifted(): return lax.ppermute(x, axis, [(i, (i + step) % size) for i in range(size)])  5.22 us
    unnamed x12, local copies, waits for them, and re-layouts  2.17 us
  transfers between devices with their start and end apart: 6, of which 5 were waited for; matrix products, arithmetic and copies ran while one was open for 0% of the time, Pallas kernels for 17%

profile of v2, /device:TPU:0, one launch (start us, length us, event | category | flops | bytes accessed | tf_op | source)
XLA Modules:
  0.0 38.4 jit_solution(11463184185447026023)
XLA Ops:
  0.6 0.0 copy-start
  0.6 0.7 %copy-done = bf16[16,768]{1,0:T(8,128)(2,1)S(1)} copy-done((bf16[16,768]{1,0:T(8,128)(2,1)S(1)}, bf16[16,768]{1,0:T(8,128)(2,1)}, u32[]{:S(2)}) %copy-start) | copy-done | bytes 24600
  1.4 0.0 copy-start.1
  1.4 0.7 %copy-done.1 = bf16[16,768]{1,0:T(8,128)(2,1)S(1)} copy-done((bf16[16,768]{1,0:T(8,128)(2,1)S(1)}, bf16[16,768]{1,0:T(8,128)(2,1)}, u32[]{:S(2)}) %copy-start.1) | copy-done | bytes 24600
  2.1 0.0 copy-start.3
  2.1 0.7 %copy-done.3 = f32[768]{0:T(1024)S(1)} copy-done((f32[768]{0:T(1024)S(1)}, f32[768]{0:T(1024)}, u32[]{:S(2)}) %copy-start.3) | copy-done | bytes 3096
  2.8 5.1 %collective-permute-start.2 = (bf16[32,768]{1,0:T(8,128)(2,1)S(1)}, bf16[32,768]{1,0:T(8,128)(2,1)S(1)}, u32[]{:S(2)}, u32[]{:S(2)}) collective-permute-start(bf16[32,768]{1,0:T(8,128)(2,1)S(1)} %pack.1.packed_ref), channel_id=1, source_target_pairs={{0,12},{4,0},{8,4},{12,8},{1,13},{5,1},{9,5},{13,9},{2,14},{6,2},{... | collective-permute-start | bytes 147464 | tf_op jit(solution)/shard_map/ppermute | solution.py:182
  7.9 0.0 collective-permute-start.1
  7.9 1.0 %collective-permute-start = (bf16[32,768]{1,0:T(8,128)(2,1)S(1)}, bf16[32,768]{1,0:T(8,128)(2,1)S(1)}, u32[]{:S(2)}, u32[]{:S(2)}) collective-permute-start(bf16[32,768]{1,0:T(8,128)(2,1)S(1)} %pack.1.packed_ref), channel_id=1, source_target_pairs={{0,4},{4,8},{8,12},{12,0},{1,5},{5,9},{9,13},{13,1},{2,6},{6,10},{... | collective-permute-start | bytes 147464 | tf_op jit(solution)/shard_map/ppermute | solution.py:182
  8.9 0.9 %own.1 = (bf16[768,64]{1,0:T(8,128)(2,1)S(1)}, f32[768,16]{1,0:T(8,128)S(1)}) custom-call(bf16[32,768]{1,0:T(8,128)(2,1)S(1)} %pack.1.packed_ref), custom_call_target="tpu_custom_call" | custom-call | flops 94371840 | bytes 49152 | tf_op jit(solution)/shard_map/own/pallas_call | solution.py:204
  9.9 0.1 collective-permute-done.2
  10.0 2.9 %collective-permute-done.1 = bf16[32,768]{1,0:T(8,128)(2,1)S(1)} collective-permute-done((bf16[32,768]{1,0:T(8,128)(2,1)S(1)}, bf16[32,768]{1,0:T(8,128)(2,1)S(1)}, u32[]{:S(2)}, u32[]{:S(2)}) %collective-permute-start.1) | collective-permute-done | bytes 49184 | tf_op jit(solution)/shard_map/ppermute | solution.py:182
  12.9 0.9 %collective-permute-done = bf16[32,768]{1,0:T(8,128)(2,1)S(1)} collective-permute-done((bf16[32,768]{1,0:T(8,128)(2,1)S(1)}, bf16[32,768]{1,0:T(8,128)(2,1)S(1)}, u32[]{:S(2)}, u32[]{:S(2)}) %collective-permute-start) | collective-permute-done | bytes 49184 | tf_op jit(solution)/shard_map/ppermute | solution.py:182
  13.8 0.0 copy-start.5
  13.8 0.1 collective-permute-start.4
  13.9 1.6 %collective-permute-start.3 = (bf16[4,32,768]{2,1,0:T(8,128)(2,1)S(1)}, bf16[4,32,768]{2,1,0:T(8,128)(2,1)S(1)}, u32[]{:S(2)}, u32[]{:S(2)}) collective-permute-start(bf16[4,32,768]{2,1,0:T(8,128)(2,1)S(1)} %pad_maximum_fusion.blocks_ref), channel_id=1, source_target_pairs={{0,2},{1,3},{2,0},{3,1},{4,6},{5,7},{6,4},{7,5},{8,10},{9,11},{10,... | collective-permute-start | bytes 589832 | tf_op jit(solution)/shard_map/ppermute | solution.py:182
  15.5 0.0 copy-done.5
  15.5 1.8 %add_line.1.before_ref = f32[768,16]{1,0:T(8,128)S(1)} custom-call(s32[8,2,16]{2,1,0:T(2,128)S(1)} %bitcast.6, bf16[768,64]{1,0:T(8,128)(2,1)S(1)} %get-tuple-element.10.left_ref, bf16[4,32,768]{2,1,0:T(8,128)(2,1)S(1)} %pad_maximum_fusion.blocks_ref, f32[768,16]{1,0:T(8,128)S(1)} %get-tuple-element.13.before_ref), custom_call_target="tpu_custom_call", output_to_operand_aliasing={{}: (3, {})} | custom-call | flops 188743680 | bytes 345088 | tf_op jit(solution)/shard_map/add_line/pallas_call | solution.py:204
  17.3 0.0 collective-permute-done.4.blocks_ref
  17.3 2.6 %add_core.1.before_ref = f32[768,16]{1,0:T(8,128)S(1)} custom-call(s32[8,2,16]{2,1,0:T(2,128)S(1)} %bitcast.7, bf16[768,64]{1,0:T(8,128)(2,1)S(1)} %get-tuple-element.10.left_ref, bf16[4,32,768]{2,1,0:T(8,128)(2,1)S(1)} %collective-permute-done.4.blocks_ref, f32[768,16]{1,0:T(8,128)S(1)} %add_line.1.before_ref), custom_call_target="tpu_custom_call", output_to_operand_aliasing={{}: (3, {})} | custom-call | flops 188743680 | bytes 345088 | tf_op jit(solution)/shard_map/add_core/pallas_call | solution.py:204
  19.9 0.0 copy-start.2
  19.9 0.0 copy-start.4
  19.9 1.3 %collective-permute-done.3.blocks_ref = bf16[4,32,768]{2,1,0:T(8,128)(2,1)S(1)} collective-permute-done((bf16[4,32,768]{2,1,0:T(8,128)(2,1)S(1)}, bf16[4,32,768]{2,1,0:T(8,128)(2,1)S(1)}, u32[]{:S(2)}, u32[]{:S(2)}) %collective-permute-start.3) | collective-permute-done | bytes 196640 | tf_op jit(solution)/shard_map/ppermute | solution.py:182
  21.2 0.0 collective-permute-start.5
  21.2 1.1 %add_across.1.before_ref = f32[768,16]{1,0:T(8,128)S(1)} custom-call(s32[8,2,16]{2,1,0:T(2,128)S(1)} %bitcast.8, bf16[768,64]{1,0:T(8,128)(2,1)S(1)} %get-tuple-element.10.left_ref, bf16[4,32,768]{2,1,0:T(8,128)(2,1)S(1)} %collective-permute-done.3.blocks_ref, f32[768,16]{1,0:T(8,128)S(1)} %add_core.1.before_ref), custom_call_target="tpu_custom_call", output_to_operand_aliasing={{}: (3, {})} | custom-call | flops 188743680 | bytes 345088 | tf_op jit(solution)/shard_map/add_across/pallas_call | solution.py:204
  22.3 0.3 collective-permute-done.5.blocks_ref
  22.7 0.0 copy-done.2
  22.7 0.0 copy-done.4
  22.7 3.0 %add_far.1 = (f32[16,768]{1,0:T(8,128)S(1)}, f32[16,8,128]{2,1,0:T(8,128)S(1)}) custom-call(s32[8,2,16]{2,1,0:T(2,128)S(1)} %bitcast.9, bf16[768,64]{1,0:T(8,128)(2,1)S(1)} %get-tuple-element.10.left_ref, bf16[4,32,768]{2,1,0:T(8,128)(2,1)S(1)} %collective-permute-done.5.blocks_ref, f32[768,16]{1,0:T(8,128)S(1)} %add_across.1.before_ref, ...), custom_call_target="tpu_custom_call" | custom-call | flops 188743680 | bytes 372736 | tf_op jit(solution)/shard_map/add_far/pallas_call | solution.py:204
  25.7 11.5 %all_to_all.5.grams_ref = f32[16,8,128]{2,1,0:T(8,128)S(1)} all-to-all(f32[16,8,128]{2,1,0:T(8,128)S(1)} %get-tuple-element.16), channel_id=1, replica_groups=mesh['grp'=2,'row'=4,'col'=4] {'row','col'}, dimensions={0} | all-to-all | bytes 131072 | tf_op jit(solution)/shard_map/all_to_all | solution.py:259
  37.2 1.3 %finish.1 = (f32[16,768]{1,0:T(8,128)}, f32[16,16]{1,0:T(8,128)}) custom-call(f32[16,8,128]{2,1,0:T(8,128)S(1)} %all_to_all.5.grams_ref, f32[16,768]{1,0:T(8,128)S(1)} %get-tuple-element.17.applied_ref), custom_call_target="tpu_custom_call" | custom-call | bytes 114688 | tf_op jit(solution)/shard_map/finish/pallas_call | solution.py:204
  (2 shorter events, 0.0 us)
Async XLA Ops:
  0.6 0.7 %copy-start = (bf16[16,768]{1,0:T(8,128)(2,1)S(1)}, bf16[16,768]{1,0:T(8,128)(2,1)}, u32[]{:S(2)}) copy-start(bf16[16,768]{1,0:T(8,128)(2,1)} %frames_ref.1) | copy-start | bytes 73732
  1.4 0.7 %copy-start.1 = (bf16[16,768]{1,0:T(8,128)(2,1)S(1)}, bf16[16,768]{1,0:T(8,128)(2,1)}, u32[]{:S(2)}) copy-start(bf16[16,768]{1,0:T(8,128)(2,1)} %vectors_ref.3) | copy-start | bytes 73732
  2.1 0.7 %copy-start.3 = (f32[768]{0:T(1024)S(1)}, f32[768]{0:T(1024)}, u32[]{:S(2)}) copy-start(f32[768]{0:T(1024)} %degrees_ref.3) | copy-start | bytes 9220
  2.8 7.2 %collective-permute-start.2 = (bf16[32,768]{1,0:T(8,128)(2,1)S(1)}, bf16[32,768]{1,0:T(8,128)(2,1)S(1)}, u32[]{:S(2)}, u32[]{:S(2)}) collective-permute-start(bf16[32,768]{1,0:T(8,128)(2,1)S(1)} %pack.1.packed_ref), channel_id=1, source_target_pairs={{0,12},{4,0},{8,4},{12,8},{1,13},{5,1},{9,5},{13,9},{2,14},{6,2},{... | collective-permute-start | bytes 147464 | tf_op jit(solution)/shard_map/ppermute | solution.py:182
  7.9 5.0 %collective-permute-start.1 = (bf16[32,768]{1,0:T(8,128)(2,1)S(1)}, bf16[32,768]{1,0:T(8,128)(2,1)S(1)}, u32[]{:S(2)}, u32[]{:S(2)}) collective-permute-start(bf16[32,768]{1,0:T(8,128)(2,1)S(1)} %pack.1.packed_ref), channel_id=1, source_target_pairs={{0,8},{4,12},{8,0},{12,4},{1,9},{5,13},{9,1},{13,5},{2,10},{6,14},... | collective-permute-start | bytes 147464 | tf_op jit(solution)/shard_map/ppermute | solution.py:182
  7.9 5.9 %collective-permute-start = (bf16[32,768]{1,0:T(8,128)(2,1)S(1)}, bf16[32,768]{1,0:T(8,128)(2,1)S(1)}, u32[]{:S(2)}, u32[]{:S(2)}) collective-permute-start(bf16[32,768]{1,0:T(8,128)(2,1)S(1)} %pack.1.packed_ref), channel_id=1, source_target_pairs={{0,4},{4,8},{8,12},{12,0},{1,5},{5,9},{9,13},{13,1},{2,6},{6,10},{... | collective-permute-start | bytes 147464 | tf_op jit(solution)/shard_map/ppermute | solution.py:182
  13.8 1.7 %copy-start.5 = (s32[16,8,2]{0,2,1:T(2,128)S(1)}, s32[16,8,2]{0,2,1:T(2,128)}, u32[]{:S(2)}) copy-start(s32[16,8,2]{0,2,1:T(2,128)} %param.7) | copy-start | bytes 3076
  13.8 3.5 %collective-permute-start.4 = (bf16[4,32,768]{2,1,0:T(8,128)(2,1)S(1)}, bf16[4,32,768]{2,1,0:T(8,128)(2,1)S(1)}, u32[]{:S(2)}, u32[]{:S(2)}) collective-permute-start(bf16[4,32,768]{2,1,0:T(8,128)(2,1)S(1)} %pad_maximum_fusion.blocks_ref), channel_id=1, source_target_pairs={{0,1},{1,0},{2,3},{3,2},{4,5},{5,4},{6,7},{7,6},{8,9},{9,8},{10,11... | collective-permute-start | bytes 589832 | tf_op jit(solution)/shard_map/ppermute | solution.py:186
  13.9 7.3 %collective-permute-start.3 = (bf16[4,32,768]{2,1,0:T(8,128)(2,1)S(1)}, bf16[4,32,768]{2,1,0:T(8,128)(2,1)S(1)}, u32[]{:S(2)}, u32[]{:S(2)}) collective-permute-start(bf16[4,32,768]{2,1,0:T(8,128)(2,1)S(1)} %pad_maximum_fusion.blocks_ref), channel_id=1, source_target_pairs={{0,2},{1,3},{2,0},{3,1},{4,6},{5,7},{6,4},{7,5},{8,10},{9,11},{10,... | collective-permute-start | bytes 589832 | tf_op jit(solution)/shard_map/ppermute | solution.py:182
  19.9 2.8 %copy-start.2 = (bf16[16,768]{1,0:T(8,128)(2,1)S(1)}, bf16[16,768]{1,0:T(8,128)(2,1)}, u32[]{:S(2)}) copy-start(bf16[16,768]{1,0:T(8,128)(2,1)} %vectors_ref.3) | copy-start | bytes 73732
  19.9 2.7 %copy-start.4 = (f32[768]{0:T(1024)S(1)}, f32[768]{0:T(1024)}, u32[]{:S(2)}) copy-start(f32[768]{0:T(1024)} %degrees_ref.3) | copy-start | bytes 9220
  21.2 1.4 %collective-permute-start.5 = (bf16[4,32,768]{2,1,0:T(8,128)(2,1)S(1)}, bf16[4,32,768]{2,1,0:T(8,128)(2,1)S(1)}, u32[]{:S(2)}, u32[]{:S(2)}) collective-permute-start(bf16[4,32,768]{2,1,0:T(8,128)(2,1)S(1)} %collective-permute-done.3.blocks_ref), channel_id=1, source_target_pairs={{0,1},{1,0},{2,3},{3,2},{4,5},{5,4},{6,7},{7,6},{8,9},{9,8},{10,11... | collective-permute-start | bytes 589832 | tf_op jit(solution)/shard_map/ppermute | solution.py:186

commit v3 on v2

--- a/solution.py
+++ b/solution.py
@@ -22,11 +22,20 @@
     return high, mid, low
 
 
-def pack_kernel(frames_ref, vectors_ref, degrees_ref, out_ref):
+def pack_kernel(frames_ref, vectors_ref, degrees_ref, out_ref, raw_ref, degree_ref, sems):
     ncv = frames_ref.shape[0]
-    root = lax.rsqrt(degrees_ref[...])[None, :]
-    out_ref[:ncv, :] = frames_ref[...]
-    out_ref[ncv:, :] = (vectors_ref[...].astype(jnp.float32) * root).astype(jnp.bfloat16)
+    copies = [
+        pltpu.make_async_copy(vectors_ref, raw_ref, sems.at[0]),
+        pltpu.make_async_copy(degrees_ref, degree_ref, sems.at[1]),
+        pltpu.make_async_copy(frames_ref, out_ref.at[pl.ds(0, ncv)], sems.at[2]),
+    ]
+    for copy in copies:
+        copy.start()
+    copies[0].wait()
+    copies[1].wait()
+    root = lax.rsqrt(degree_ref[...])[None, :]
+    out_ref[ncv:, :] = (raw_ref[...].astype(jnp.float32) * root).astype(jnp.bfloat16)
+    copies[2].wait()
 
 
 def edge_rows(square, ones_first):
@@ -47,20 +56,25 @@
     return jnp.concatenate([high, mid, low, edge], axis=0).T.astype(jnp.bfloat16)
 
 
-def tile_image(left, x, v):
+def tile_image(left_ref, x, v):
     wide = x.astype(jnp.float32)
     edge = edge_rows(jnp.sum(wide * wide, axis=0, keepdims=True), False).astype(jnp.bfloat16)
     right = jnp.concatenate([x, x, x, edge], axis=0)
-    power = jnp.dot(left, right, preferred_element_type=jnp.float32)
-    kern = jnp.exp2(power).astype(jnp.bfloat16)
-    return lax.dot_general(kern, v, NT, preferred_element_type=jnp.float32)
+    chunk = 256
+    parts = []
+    for start in range(0, x.shape[1], chunk):
+        left = left_ref[start : start + chunk, :]
+        power = jnp.dot(left, right, preferred_element_type=jnp.float32)
+        kern = jnp.exp2(power).astype(jnp.bfloat16)
+        parts.append(lax.dot_general(v, kern, NT, preferred_element_type=jnp.float32))
+    return jnp.concatenate(parts, axis=1)
 
 
 def own_kernel(packed_ref, left_ref, image_ref):
     ncv = packed_ref.shape[0] // 2
     x = packed_ref[:ncv, :]
     left_ref[...] = own_side(x)
-    image_ref[...] = tile_image(left_ref[...], x, packed_ref[ncv:, :])
+    image_ref[...] = tile_image(left_ref, x, packed_ref[ncv:, :])
 
 
 def add_blocks(part, sizes, table_ref, left_ref, blocks_ref, image_ref):
@@ -90,7 +104,7 @@
         @pl.when(((word >> (block % 16)) & 1) == 1)
         def _():
             image_ref[...] += tile_image(
-                left_ref[...], blocks_ref[step, :ncv, :], blocks_ref[step, ncv:, :]
+                left_ref, blocks_ref[step, :ncv, :], blocks_ref[step, ncv:, :]
             )
 
         return 0
@@ -110,7 +124,7 @@
     image_ref[...] = before_ref[...]
     add_blocks("far", sizes, table_ref, left_ref, blocks_ref, image_ref)
     n = vectors_ref.shape[0]
-    applied = image_ref[...].T * lax.rsqrt(degrees_ref[...])[None, :]
+    applied = image_ref[...] * lax.rsqrt(degrees_ref[...])[None, :]
     applied_ref[...] = applied
     both = jnp.concatenate([applied, vectors_ref[...].astype(jnp.float32)], axis=0)
     gram = lax.dot_general(
@@ -194,7 +208,7 @@
     sizes = (n_row, n_col)
     vmem = pl.BlockSpec(memory_space=pltpu.VMEM)
 
-    def call(kernel, name, outs, *args, limit=16, tiles=0, **keywords):
+    def call(kernel, name, outs, *args, limit=16, tiles=0, where=vmem, **keywords):
         shapes = [jax.ShapeDtypeStruct(*out) for out in outs]
         keywords["cost_estimate"] = pl.CostEstimate(
             flops=tiles * rows * rows * 2 * (4 * ncv + nvec),
@@ -204,7 +218,7 @@
         return pl.pallas_call(
             kernel,
             out_shape=shapes,
-            in_specs=[vmem] * len(args),
+            in_specs=[where] * len(args),
             out_specs=[vmem] * len(outs),
             compiler_params=pltpu.CompilerParams(vmem_limit_bytes=limit * MIB),
             name=name,
@@ -212,10 +226,19 @@
         )(*args)
 
     table = tile_table.transpose(1, 2, 0)
-    image_type = ((rows, nvec), jnp.float32)
+    image_type = ((nvec, rows), jnp.float32)
 
     (packed,) = call(
-        pack_kernel, "pack", [((ncv + nvec, rows), jnp.bfloat16)], frames, vectors, degrees
+        pack_kernel,
+        "pack",
+        [((ncv + nvec, rows), jnp.bfloat16)],
+        *(pltpu.with_memory_space_constraint(x, pltpu.HBM) for x in (frames, vectors, degrees)),
+        where=pl.BlockSpec(memory_space=pltpu.HBM),
+        scratch_shapes=[
+            pltpu.VMEM(vectors.shape, vectors.dtype),
+            pltpu.VMEM(degrees.shape, degrees.dtype),
+            pltpu.SemaphoreType.DMA((3,)),
+        ],
     )
     line = jnp.stack([packed] + [shifted(packed, "row", s) for s in range(1, n_row)])
     left, image = call(own_kernel, "own", [((rows, 3 * ncv + 16), jnp.bfloat16), image_type], packed, tiles=1)
@@ -246,7 +269,7 @@
     applied, gram = call(
         functools.partial(last_kernel, sizes),
         "add_far",
-        [((nvec, rows), jnp.float32), ((devices, nvec // 2, 8 * nvec), jnp.float32)],
+        [((nvec, rows), jnp.float32), ((n_row, nvec // 2, 8 * nvec), jnp.float32)],
         table,
         left,
         far,
@@ -256,7 +279,9 @@
         tiles=far.shape[0] // 2,
         scratch_shapes=[pltpu.VMEM(*image_type)],
     )
-    grams = lax.all_to_all(gram, ("row", "col"), 0, 0)
+    grams = lax.all_to_all(gram, "row", 0, 0)
+    gram = jnp.broadcast_to(jnp.sum(grams, axis=0), (n_col, nvec // 2, 8 * nvec))
+    grams = lax.all_to_all(gram, "col", 0, 0)
     basis, ritz = call(
         functools.partial(finish_kernel, rows * devices),
         "finish",

time: 38.7 us -> 41.2 us (1.065); the launches traced: 38.4 us -> 40.5 us
  blocking collectives: 11.5 us -> 16.4 us
  Pallas kernels: 10.7 us -> 7.69 us
  waiting for transfers between devices: 5.57 us -> 7.89 us
  local copies, waits for them, and re-layouts: 2.17 us -> 0.02 us
    all_to_all x1 -> x2, blocking collectives: 11.5 us -> 16.4 us  [the longest x1 10.2 us: per_device(): grams = lax.all_to_all(gram, 'row', 0, 0)]
    pallas_call x7, Pallas kernels: 10.7 us -> 7.69 us  [call(): pl.pallas_call(kernel, out_shape=shapes, in_specs=[where] * len(args), ou...]
    ppermute x4, waiting for transfers between devices: 5.22 us -> 7.54 us  [shifted(): return lax.ppermute(x, axis, [(i, (i + step) % size) for i in range(size)])]
    unnamed x12 -> x6, local copies, waits for them, and re-layouts: 2.17 us -> 0.01 us
  transfers between devices with their start and end apart: 6 -> 6, of which waited for: 5 -> 5; matrix products, arithmetic and copies ran while one was open for 0% -> 0% of each run, Pallas kernels for 17% -> 10%
where the time goes in v3:
time: 41.2 us; the launch traced here: 40.5 us
  blocking collectives  16.4 us (40%)
  waiting for transfers between devices  7.89 us (19%)
  starting transfers between devices  7.74 us (19%)
  Pallas kernels  7.69 us (19%)
  between operations  0.66 us (2%)
    all_to_all x1, blocking collectives, per_device(): grams = lax.all_to_all(gram, 'row', 0, 0)  10.2 us
    pallas_call x7, Pallas kernels, call(): pl.pallas_call(kernel, out_shape=shapes, in_specs=[where] * len(args), ou...  7.69 us
    ppermute x4, starting transfers between devices, shifted(): return lax.ppermute(x, axis, [(i, (i + step) % size) for i in range(size)])  7.67 us
    ppermute x4, waiting for transfers between devices, shifted(): return lax.ppermute(x, axis, [(i, (i + step) % size) for i in range(size)])  7.54 us
    all_to_all x1, blocking collectives, per_device(): grams = lax.all_to_all(gram, 'col', 0, 0)  6.19 us
  transfers between devices with their start and end apart: 6, of which 5 were waited for; matrix products, arithmetic and copies ran while one was open for 0% of the time, Pallas kernels for 10%

profile of v3, /device:TPU:0, one launch (start us, length us, event | category | flops | bytes accessed | tf_op | source)
XLA Modules:
  0.0 40.5 jit_solution(3622788884313742516)
XLA Ops:
  0.6 0.8 %pack.1.packed_ref = bf16[32,768]{1,0:T(8,128)(2,1)S(1)} custom-call(bf16[16,768]{1,0:T(8,128)(2,1)} %frames_ref.1, bf16[16,768]{1,0:T(8,128)(2,1)} %vectors_ref.3, f32[768]{0:T(1024)} %degrees_ref.3), custom_call_target="tpu_custom_call" | custom-call | bytes 52224 | tf_op jit(solution)/shard_map/pack/pallas_call | solution.py:218
  1.4 5.1 %collective-permute-start.2 = (bf16[32,768]{1,0:T(8,128)(2,1)S(1)}, bf16[32,768]{1,0:T(8,128)(2,1)S(1)}, u32[]{:S(2)}, u32[]{:S(2)}) collective-permute-start(bf16[32,768]{1,0:T(8,128)(2,1)S(1)} %pack.1.packed_ref), channel_id=1, source_target_pairs={{0,12},{4,0},{8,4},{12,8},{1,13},{5,1},{9,5},{13,9},{2,14},{6,2},{... | collective-permute-start | bytes 147464 | tf_op jit(solution)/shard_map/ppermute | solution.py:196
  6.5 0.0 collective-permute-start.1
  6.5 1.0 %collective-permute-start = (bf16[32,768]{1,0:T(8,128)(2,1)S(1)}, bf16[32,768]{1,0:T(8,128)(2,1)S(1)}, u32[]{:S(2)}, u32[]{:S(2)}) collective-permute-start(bf16[32,768]{1,0:T(8,128)(2,1)S(1)} %pack.1.packed_ref), channel_id=1, source_target_pairs={{0,4},{4,8},{8,12},{12,0},{1,5},{5,9},{9,13},{13,1},{2,6},{6,10},{... | collective-permute-start | bytes 147464 | tf_op jit(solution)/shard_map/ppermute | solution.py:196
  7.6 0.9 %own.1 = (bf16[768,64]{1,0:T(8,128)(2,1)S(1)}, f32[16,768]{1,0:T(8,128)S(1)}) custom-call(bf16[32,768]{1,0:T(8,128)(2,1)S(1)} %pack.1.packed_ref), custom_call_target="tpu_custom_call" | custom-call | flops 94371840 | bytes 49152 | tf_op jit(solution)/shard_map/own/pallas_call | solution.py:218
  8.5 0.1 collective-permute-done.2
  8.6 2.9 %collective-permute-done.1 = bf16[32,768]{1,0:T(8,128)(2,1)S(1)} collective-permute-done((bf16[32,768]{1,0:T(8,128)(2,1)S(1)}, bf16[32,768]{1,0:T(8,128)(2,1)S(1)}, u32[]{:S(2)}, u32[]{:S(2)}) %collective-permute-start.1) | collective-permute-done | bytes 49184 | tf_op jit(solution)/shard_map/ppermute | solution.py:196
  11.5 0.9 %collective-permute-done = bf16[32,768]{1,0:T(8,128)(2,1)S(1)} collective-permute-done((bf16[32,768]{1,0:T(8,128)(2,1)S(1)}, bf16[32,768]{1,0:T(8,128)(2,1)S(1)}, u32[]{:S(2)}, u32[]{:S(2)}) %collective-permute-start) | collective-permute-done | bytes 49184 | tf_op jit(solution)/shard_map/ppermute | solution.py:196
  12.4 0.0 copy-start.2
  12.5 0.1 collective-permute-start.4
  12.5 1.6 %collective-permute-start.3 = (bf16[4,32,768]{2,1,0:T(8,128)(2,1)S(1)}, bf16[4,32,768]{2,1,0:T(8,128)(2,1)S(1)}, u32[]{:S(2)}, u32[]{:S(2)}) collective-permute-start(bf16[4,32,768]{2,1,0:T(8,128)(2,1)S(1)} %pad_maximum_fusion.blocks_ref), channel_id=1, source_target_pairs={{0,2},{1,3},{2,0},{3,1},{4,6},{5,7},{6,4},{7,5},{8,10},{9,11},{10,... | collective-permute-start | bytes 589832 | tf_op jit(solution)/shard_map/ppermute | solution.py:196
  14.1 0.0 copy-done.2
  14.1 1.1 %add_line.1.before_ref = f32[16,768]{1,0:T(8,128)S(1)} custom-call(s32[8,2,16]{2,1,0:T(2,128)S(1)} %bitcast.6, bf16[768,64]{1,0:T(8,128)(2,1)S(1)} %get-tuple-element.10.left_ref, bf16[4,32,768]{2,1,0:T(8,128)(2,1)S(1)} %pad_maximum_fusion.blocks_ref, f32[16,768]{1,0:T(8,128)S(1)} %get-tuple-element.13.before_ref), custom_call_target="tpu_custom_call", output_to_operand_aliasing={{}: (3, {})} | custom-call | flops 188743680 | bytes 345088 | tf_op jit(solution)/shard_map/add_line/pallas_call | solution.py:218
  15.2 0.0 collective-permute-done.4.blocks_ref
  15.2 1.1 %add_core.1.before_ref = f32[16,768]{1,0:T(8,128)S(1)} custom-call(s32[8,2,16]{2,1,0:T(2,128)S(1)} %bitcast.7, bf16[768,64]{1,0:T(8,128)(2,1)S(1)} %get-tuple-element.10.left_ref, bf16[4,32,768]{2,1,0:T(8,128)(2,1)S(1)} %collective-permute-done.4.blocks_ref, f32[16,768]{1,0:T(8,128)S(1)} %add_line.1.before_ref), custom_call_target="tpu_custom_call", output_to_operand_aliasing={{}: (3, {})} | custom-call | flops 188743680 | bytes 345088 | tf_op jit(solution)/shard_map/add_core/pallas_call | solution.py:218
  16.2 0.0 copy-start
  16.2 0.0 copy-start.1
  16.2 3.6 %collective-permute-done.3.blocks_ref = bf16[4,32,768]{2,1,0:T(8,128)(2,1)S(1)} collective-permute-done((bf16[4,32,768]{2,1,0:T(8,128)(2,1)S(1)}, bf16[4,32,768]{2,1,0:T(8,128)(2,1)S(1)}, u32[]{:S(2)}, u32[]{:S(2)}) %collective-permute-start.3) | collective-permute-done | bytes 196640 | tf_op jit(solution)/shard_map/ppermute | solution.py:196
  19.9 0.0 collective-permute-start.5
  19.9 1.1 %add_across.1.before_ref = f32[16,768]{1,0:T(8,128)S(1)} custom-call(s32[8,2,16]{2,1,0:T(2,128)S(1)} %bitcast.8, bf16[768,64]{1,0:T(8,128)(2,1)S(1)} %get-tuple-element.10.left_ref, bf16[4,32,768]{2,1,0:T(8,128)(2,1)S(1)} %collective-permute-done.3.blocks_ref, f32[16,768]{1,0:T(8,128)S(1)} %add_core.1.before_ref), custom_call_target="tpu_custom_call", output_to_operand_aliasing={{}: (3, {})} | custom-call | flops 188743680 | bytes 345088 | tf_op jit(solution)/shard_map/add_across/pallas_call | solution.py:218
  21.0 0.3 collective-permute-done.5.blocks_ref
  21.3 0.0 copy-done
  21.3 0.0 copy-done.1
  21.3 1.5 %add_far.1 = (f32[16,768]{1,0:T(8,128)S(1)}, f32[4,8,128]{2,1,0:T(8,128)S(1)}) custom-call(s32[8,2,16]{2,1,0:T(2,128)S(1)} %bitcast.9, bf16[768,64]{1,0:T(8,128)(2,1)S(1)} %get-tuple-element.10.left_ref, bf16[4,32,768]{2,1,0:T(8,128)(2,1)S(1)} %collective-permute-done.5.blocks_ref, f32[16,768]{1,0:T(8,128)S(1)} %add_across.1.before_ref, ...), custom_call_target="tpu_custom_call" | custom-call | flops 188743680 | bytes 372736 | tf_op jit(solution)/shard_map/add_far/pallas_call | solution.py:218
  22.8 10.2 %all_to_all.10 = f32[4,8,128]{2,1,0:T(8,128)S(1)} all-to-all(f32[4,8,128]{2,1,0:T(8,128)S(1)} %get-tuple-element.16), channel_id=1, replica_groups=mesh['grp'=2,'row'=4,'col'=4] {'row'}, dimensions={0} | all-to-all | bytes 32768 | tf_op jit(solution)/shard_map/all_to_all | solution.py:282
  33.0 6.2 %all_to_all.11.grams_ref = f32[4,8,128]{2,1,0:T(8,128)S(1)} all-to-all(f32[4,8,128]{2,1,0:T(8,128)S(1)} %broadcast_in_dim.3), channel_id=1, replica_groups=mesh['grp'=2,'row'=4,'col'=4] {'col'}, dimensions={0} | all-to-all | bytes 32768 | tf_op jit(solution)/shard_map/all_to_all | solution.py:284
  39.2 1.3 %finish.1 = (f32[16,768]{1,0:T(8,128)}, f32[16,16]{1,0:T(8,128)}) custom-call(f32[4,8,128]{2,1,0:T(8,128)S(1)} %all_to_all.11.grams_ref, f32[16,768]{1,0:T(8,128)S(1)} %get-tuple-element.17.applied_ref), custom_call_target="tpu_custom_call" | custom-call | bytes 65536 | tf_op jit(solution)/shard_map/finish/pallas_call | solution.py:218
  (3 shorter events, 0.0 us)
Async XLA Ops:
  1.4 7.2 %collective-permute-start.2 = (bf16[32,768]{1,0:T(8,128)(2,1)S(1)}, bf16[32,768]{1,0:T(8,128)(2,1)S(1)}, u32[]{:S(2)}, u32[]{:S(2)}) collective-permute-start(bf16[32,768]{1,0:T(8,128)(2,1)S(1)} %pack.1.packed_ref), channel_id=1, source_target_pairs={{0,12},{4,0},{8,4},{12,8},{1,13},{5,1},{9,5},{13,9},{2,14},{6,2},{... | collective-permute-start | bytes 147464 | tf_op jit(solution)/shard_map/ppermute | solution.py:196
  6.5 5.0 %collective-permute-start.1 = (bf16[32,768]{1,0:T(8,128)(2,1)S(1)}, bf16[32,768]{1,0:T(8,128)(2,1)S(1)}, u32[]{:S(2)}, u32[]{:S(2)}) collective-permute-start(bf16[32,768]{1,0:T(8,128)(2,1)S(1)} %pack.1.packed_ref), channel_id=1, source_target_pairs={{0,8},{4,12},{8,0},{12,4},{1,9},{5,13},{9,1},{13,5},{2,10},{6,14},... | collective-permute-start | bytes 147464 | tf_op jit(solution)/shard_map/ppermute | solution.py:196
  6.5 5.9 %collective-permute-start = (bf16[32,768]{1,0:T(8,128)(2,1)S(1)}, bf16[32,768]{1,0:T(8,128)(2,1)S(1)}, u32[]{:S(2)}, u32[]{:S(2)}) collective-permute-start(bf16[32,768]{1,0:T(8,128)(2,1)S(1)} %pack.1.packed_ref), channel_id=1, source_target_pairs={{0,4},{4,8},{8,12},{12,0},{1,5},{5,9},{9,13},{13,1},{2,6},{6,10},{... | collective-permute-start | bytes 147464 | tf_op jit(solution)/shard_map/ppermute | solution.py:196
  12.4 1.7 %copy-start.2 = (s32[16,8,2]{0,2,1:T(2,128)S(1)}, s32[16,8,2]{0,2,1:T(2,128)}, u32[]{:S(2)}) copy-start(s32[16,8,2]{0,2,1:T(2,128)} %param.7) | copy-start | bytes 3076
  12.5 2.7 %collective-permute-start.4 = (bf16[4,32,768]{2,1,0:T(8,128)(2,1)S(1)}, bf16[4,32,768]{2,1,0:T(8,128)(2,1)S(1)}, u32[]{:S(2)}, u32[]{:S(2)}) collective-permute-start(bf16[4,32,768]{2,1,0:T(8,128)(2,1)S(1)} %pad_maximum_fusion.blocks_ref), channel_id=1, source_target_pairs={{0,1},{1,0},{2,3},{3,2},{4,5},{5,4},{6,7},{7,6},{8,9},{9,8},{10,11... | collective-permute-start | bytes 589832 | tf_op jit(solution)/shard_map/ppermute | solution.py:200
  12.5 7.3 %collective-permute-start.3 = (bf16[4,32,768]{2,1,0:T(8,128)(2,1)S(1)}, bf16[4,32,768]{2,1,0:T(8,128)(2,1)S(1)}, u32[]{:S(2)}, u32[]{:S(2)}) collective-permute-start(bf16[4,32,768]{2,1,0:T(8,128)(2,1)S(1)} %pad_maximum_fusion.blocks_ref), channel_id=1, source_target_pairs={{0,2},{1,3},{2,0},{3,1},{4,6},{5,7},{6,4},{7,5},{8,10},{9,11},{10,... | collective-permute-start | bytes 589832 | tf_op jit(solution)/shard_map/ppermute | solution.py:196
  16.2 5.1 %copy-start = (bf16[16,768]{1,0:T(8,128)(2,1)S(1)}, bf16[16,768]{1,0:T(8,128)(2,1)}, u32[]{:S(2)}) copy-start(bf16[16,768]{1,0:T(8,128)(2,1)} %vectors_ref.3) | copy-start | bytes 73732
  16.2 5.1 %copy-start.1 = (f32[768]{0:T(1024)S(1)}, f32[768]{0:T(1024)}, u32[]{:S(2)}) copy-start(f32[768]{0:T(1024)} %degrees_ref.3) | copy-start | bytes 9220
  19.9 1.4 %collective-permute-start.5 = (bf16[4,32,768]{2,1,0:T(8,128)(2,1)S(1)}, bf16[4,32,768]{2,1,0:T(8,128)(2,1)S(1)}, u32[]{:S(2)}, u32[]{:S(2)}) collective-permute-start(bf16[4,32,768]{2,1,0:T(8,128)(2,1)S(1)} %collective-permute-done.3.blocks_ref), channel_id=1, source_target_pairs={{0,1},{1,0},{2,3},{3,2},{4,5},{5,4},{6,7},{7,6},{8,9},{9,8},{10,11... | collective-permute-start | bytes 589832 | tf_op jit(solution)/shard_map/ppermute | solution.py:200

commit v4 on v3

--- a/solution.py
+++ b/solution.py
@@ -66,8 +66,8 @@
         left = left_ref[start : start + chunk, :]
         power = jnp.dot(left, right, preferred_element_type=jnp.float32)
         kern = jnp.exp2(power).astype(jnp.bfloat16)
-        parts.append(lax.dot_general(v, kern, NT, preferred_element_type=jnp.float32))
-    return jnp.concatenate(parts, axis=1)
+        parts.append(lax.dot_general(kern, v, NT, preferred_element_type=jnp.float32))
+    return jnp.concatenate(parts, axis=0)
 
 
 def own_kernel(packed_ref, left_ref, image_ref):
@@ -124,7 +124,7 @@
     image_ref[...] = before_ref[...]
     add_blocks("far", sizes, table_ref, left_ref, blocks_ref, image_ref)
     n = vectors_ref.shape[0]
-    applied = image_ref[...] * lax.rsqrt(degrees_ref[...])[None, :]
+    applied = image_ref[...].T * lax.rsqrt(degrees_ref[...])[None, :]
     applied_ref[...] = applied
     both = jnp.concatenate([applied, vectors_ref[...].astype(jnp.float32)], axis=0)
     gram = lax.dot_general(
@@ -133,9 +133,7 @@
     wide = jnp.concatenate(
         [gram[:n, :n], gram[n:, :], jnp.zeros((n, n), jnp.float32)], axis=1
     )
-    tile = jnp.concatenate([wide[: n // 2, :], wide[n // 2 :, :]], axis=1)
-    for device in range(gram_ref.shape[0]):
-        gram_ref[device] = tile
+    gram_ref[...] = jnp.concatenate([wide[: n // 2, :], wide[n // 2 :, :]], axis=1)
 
 
 def inverse_factors(grams):
@@ -175,10 +173,8 @@
     return result[:, :n], result[:, half : half + n]
 
 
-def finish_kernel(total_frames, grams_ref, applied_ref, basis_ref, ritz_ref):
-    tile = grams_ref[0]
-    for device in range(1, grams_ref.shape[0]):
-        tile += grams_ref[device]
+def finish_kernel(total_frames, gram_ref, applied_ref, basis_ref, ritz_ref):
+    tile = gram_ref[...]
     n = applied_ref.shape[0]
     gram = jnp.concatenate([tile[:, : 4 * n], tile[:, 4 * n :]], axis=0)
     exact = functools.partial(
@@ -196,8 +192,16 @@
     return lax.ppermute(x, axis, [(i, (i + step) % size) for i in range(size)])
 
 
-def swapped(x):
-    return lax.ppermute(x, "col", [(i, i ^ 1) for i in range(lax.axis_size("col"))])
+def paired(x, axis, bit):
+    return lax.ppermute(x, axis, [(i, i ^ bit) for i in range(lax.axis_size(axis))])
+
+
+def summed(x, axis):
+    bit = 1
+    while bit < lax.axis_size(axis):
+        x = x + paired(x, axis, bit)
+        bit *= 2
+    return x
 
 
 def per_device(frames, vectors, degrees, tile_table):
@@ -226,7 +230,7 @@
         )(*args)
 
     table = tile_table.transpose(1, 2, 0)
-    image_type = ((nvec, rows), jnp.float32)
+    image_type = ((rows, nvec), jnp.float32)
 
     (packed,) = call(
         pack_kernel,
@@ -260,16 +264,16 @@
     line, image = lax.optimization_barrier((line, image))
     across = [shifted(line, "col", 2 * t) for t in range(1, n_col // 2)]
     across = across[0] if len(across) == 1 else jnp.concatenate(across)
-    core = swapped(line)
+    core = paired(line, "col", 1)
     image = add("line", line, image)
     image = add("core", core, image)
     across, image = lax.optimization_barrier((across, image))
-    far = swapped(across)
+    far = paired(across, "col", 1)
     image = add("across", across, image)
     applied, gram = call(
         functools.partial(last_kernel, sizes),
         "add_far",
-        [((nvec, rows), jnp.float32), ((n_row, nvec // 2, 8 * nvec), jnp.float32)],
+        [((nvec, rows), jnp.float32), ((nvec // 2, 8 * nvec), jnp.float32)],
         table,
         left,
         far,
@@ -279,14 +283,12 @@
         tiles=far.shape[0] // 2,
         scratch_shapes=[pltpu.VMEM(*image_type)],
     )
-    grams = lax.all_to_all(gram, "row", 0, 0)
-    gram = jnp.broadcast_to(jnp.sum(grams, axis=0), (n_col, nvec // 2, 8 * nvec))
-    grams = lax.all_to_all(gram, "col", 0, 0)
+    gram = summed(summed(gram, "col"), "row")
     basis, ritz = call(
         functools.partial(finish_kernel, rows * devices),
         "finish",
         [((nvec, rows), jnp.float32), ((nvec, nvec), jnp.float32)],
-        grams,
+        gram,
         applied,
     )
     return (basis, ritz)

time: 41.2 us -> 40.4 us (0.981)
  blocking collectives: 16.4 us -> 0 us
  starting transfers between devices: 7.74 us -> 15.2 us
  waiting for transfers between devices: 7.89 us -> 14.1 us
  Pallas kernels: 7.69 us -> 9.81 us
    all_to_all x2 -> x0, blocking collectives: 16.4 us -> none  [the longest x1 10.2 us: per_device(): grams = lax.all_to_all(gram, 'row', 0, 0)]
    ppermute x2 -> x6, starting transfers between devices: 0.07 us -> 7.54 us  [paired(): lax.ppermute(x, axis, [(i, i ^ bit) for i in range(lax.axis_size(axis))])]
    ppermute x2 -> x6, waiting for transfers between devices: 0.35 us -> 7.6 us  [paired(): lax.ppermute(x, axis, [(i, i ^ bit) for i in range(lax.axis_size(axis))])]
    pallas_call x7, Pallas kernels: 7.69 us -> 9.81 us  [call(): pl.pallas_call(kernel, out_shape=shapes, in_specs=[where] * len(args), ou...]
    ppermute x4, waiting for transfers between devices: 7.54 us -> 6.47 us  [shifted(): return lax.ppermute(x, axis, [(i, (i + step) % size) for i in range(size)])]
  transfers between devices with their start and end apart: 6 -> 10, of which waited for: 5 -> 9; matrix products, arithmetic and copies ran while one was open for 0% -> 0% of each run, Pallas kernels for 10% -> 13%
where the time goes in v4:
time: 40.4 us; the launch traced here: 39.9 us
  starting transfers between devices  15.2 us (38%)
  waiting for transfers between devices  14.1 us (35%)
  Pallas kernels  9.81 us (24%)
  between operations  0.72 us (2%)
    pallas_call x7, Pallas kernels, call(): pl.pallas_call(kernel, out_shape=shapes, in_specs=[where] * len(args), ou...  9.81 us
    ppermute x4, starting transfers between devices, shifted(): return lax.ppermute(x, axis, [(i, (i + step) % size) for i in range(size)])  7.67 us
    ppermute x6, waiting for transfers between devices, paired(): lax.ppermute(x, axis, [(i, i ^ bit) for i in range(lax.axis_size(axis))])  7.6 us
    ppermute x6, starting transfers between devices, paired(): lax.ppermute(x, axis, [(i, i ^ bit) for i in range(lax.axis_size(axis))])  7.54 us
    ppermute x4, waiting for transfers between devices, shifted(): return lax.ppermute(x, axis, [(i, (i + step) % size) for i in range(size)])  6.47 us
  transfers between devices with their start and end apart: 10, of which 9 were waited for; matrix products, arithmetic and copies ran while one was open for 0% of the time, Pallas kernels for 13%

profile of v4, /device:TPU:0, one launch (start us, length us, event | category | flops | bytes accessed | tf_op | source)
XLA Modules:
  0.0 39.9 jit_solution(11051753660638013831)
XLA Ops:
  0.6 0.8 %pack.1.packed_ref = bf16[32,768]{1,0:T(8,128)(2,1)S(1)} custom-call(bf16[16,768]{1,0:T(8,128)(2,1)} %frames_ref.1, bf16[16,768]{1,0:T(8,128)(2,1)} %vectors_ref.3, f32[768]{0:T(1024)} %degrees_ref.3), custom_call_target="tpu_custom_call" | custom-call | bytes 52224 | tf_op jit(solution)/shard_map/pack/pallas_call | solution.py:222
  1.4 5.1 %collective-permute-start.2 = (bf16[32,768]{1,0:T(8,128)(2,1)S(1)}, bf16[32,768]{1,0:T(8,128)(2,1)S(1)}, u32[]{:S(2)}, u32[]{:S(2)}) collective-permute-start(bf16[32,768]{1,0:T(8,128)(2,1)S(1)} %pack.1.packed_ref), channel_id=1, source_target_pairs={{0,12},{4,0},{8,4},{12,8},{1,13},{5,1},{9,5},{13,9},{2,14},{6,2},{... | collective-permute-start | bytes 147464 | tf_op jit(solution)/shard_map/ppermute | solution.py:192
  6.5 0.0 collective-permute-start.1
  6.5 1.0 %collective-permute-start = (bf16[32,768]{1,0:T(8,128)(2,1)S(1)}, bf16[32,768]{1,0:T(8,128)(2,1)S(1)}, u32[]{:S(2)}, u32[]{:S(2)}) collective-permute-start(bf16[32,768]{1,0:T(8,128)(2,1)S(1)} %pack.1.packed_ref), channel_id=1, source_target_pairs={{0,4},{4,8},{8,12},{12,0},{1,5},{5,9},{9,13},{13,1},{2,6},{6,10},{... | collective-permute-start | bytes 147464 | tf_op jit(solution)/shard_map/ppermute | solution.py:192
  7.6 0.9 %own.1 = (bf16[768,64]{1,0:T(8,128)(2,1)S(1)}, f32[768,16]{1,0:T(8,128)S(1)}) custom-call(bf16[32,768]{1,0:T(8,128)(2,1)S(1)} %pack.1.packed_ref), custom_call_target="tpu_custom_call" | custom-call | flops 94371840 | bytes 49152 | tf_op jit(solution)/shard_map/own/pallas_call | solution.py:222
  8.5 0.1 collective-permute-done.2
  8.6 2.9 %collective-permute-done.1 = bf16[32,768]{1,0:T(8,128)(2,1)S(1)} collective-permute-done((bf16[32,768]{1,0:T(8,128)(2,1)S(1)}, bf16[32,768]{1,0:T(8,128)(2,1)S(1)}, u32[]{:S(2)}, u32[]{:S(2)}) %collective-permute-start.1) | collective-permute-done | bytes 49184 | tf_op jit(solution)/shard_map/ppermute | solution.py:192
  11.5 0.9 %collective-permute-done = bf16[32,768]{1,0:T(8,128)(2,1)S(1)} collective-permute-done((bf16[32,768]{1,0:T(8,128)(2,1)S(1)}, bf16[32,768]{1,0:T(8,128)(2,1)S(1)}, u32[]{:S(2)}, u32[]{:S(2)}) %collective-permute-start) | collective-permute-done | bytes 49184 | tf_op jit(solution)/shard_map/ppermute | solution.py:192
  12.5 0.1 collective-permute-start.4
  12.5 1.6 %collective-permute-start.3 = (bf16[4,32,768]{2,1,0:T(8,128)(2,1)S(1)}, bf16[4,32,768]{2,1,0:T(8,128)(2,1)S(1)}, u32[]{:S(2)}, u32[]{:S(2)}) collective-permute-start(bf16[4,32,768]{2,1,0:T(8,128)(2,1)S(1)} %pad_maximum_fusion.blocks_ref), channel_id=1, source_target_pairs={{0,2},{1,3},{2,0},{3,1},{4,6},{5,7},{6,4},{7,5},{8,10},{9,11},{10,... | collective-permute-start | bytes 589832 | tf_op jit(solution)/shard_map/ppermute | solution.py:192
  14.1 0.0 copy-done.2
  14.1 2.0 %add_line.1.before_ref = f32[768,16]{1,0:T(8,128)S(1)} custom-call(s32[8,2,16]{2,1,0:T(2,128)S(1)} %bitcast.6, bf16[768,64]{1,0:T(8,128)(2,1)S(1)} %get-tuple-element.10.left_ref, bf16[4,32,768]{2,1,0:T(8,128)(2,1)S(1)} %pad_maximum_fusion.blocks_ref, f32[768,16]{1,0:T(8,128)S(1)} %get-tuple-element.13.before_ref), custom_call_target="tpu_custom_call", output_to_operand_aliasing={{}: (3, {})} | custom-call | flops 188743680 | bytes 345088 | tf_op jit(solution)/shard_map/add_line/pallas_call | solution.py:222
  16.1 0.0 collective-permute-done.4.blocks_ref
  16.1 1.2 %add_core.1.before_ref = f32[768,16]{1,0:T(8,128)S(1)} custom-call(s32[8,2,16]{2,1,0:T(2,128)S(1)} %bitcast.7, bf16[768,64]{1,0:T(8,128)(2,1)S(1)} %get-tuple-element.10.left_ref, bf16[4,32,768]{2,1,0:T(8,128)(2,1)S(1)} %collective-permute-done.4.blocks_ref, f32[768,16]{1,0:T(8,128)S(1)} %add_line.1.before_ref), custom_call_target="tpu_custom_call", output_to_operand_aliasing={{}: (3, {})} | custom-call | flops 188743680 | bytes 345088 | tf_op jit(solution)/shard_map/add_core/pallas_call | solution.py:222
  17.3 0.0 copy-start
  17.3 0.0 copy-start.1
  17.3 2.5 %collective-permute-done.3.blocks_ref = bf16[4,32,768]{2,1,0:T(8,128)(2,1)S(1)} collective-permute-done((bf16[4,32,768]{2,1,0:T(8,128)(2,1)S(1)}, bf16[4,32,768]{2,1,0:T(8,128)(2,1)S(1)}, u32[]{:S(2)}, u32[]{:S(2)}) %collective-permute-start.3) | collective-permute-done | bytes 196640 | tf_op jit(solution)/shard_map/ppermute | solution.py:192
  19.9 0.0 collective-permute-start.5
  19.9 1.2 %add_across.1.before_ref = f32[768,16]{1,0:T(8,128)S(1)} custom-call(s32[8,2,16]{2,1,0:T(2,128)S(1)} %bitcast.8, bf16[768,64]{1,0:T(8,128)(2,1)S(1)} %get-tuple-element.10.left_ref, bf16[4,32,768]{2,1,0:T(8,128)(2,1)S(1)} %collective-permute-done.3.blocks_ref, f32[768,16]{1,0:T(8,128)S(1)} %add_core.1.before_ref), custom_call_target="tpu_custom_call", output_to_operand_aliasing={{}: (3, {})} | custom-call | flops 188743680 | bytes 345088 | tf_op jit(solution)/shard_map/add_across/pallas_call | solution.py:222
  21.1 0.2 collective-permute-done.5.blocks_ref
  21.3 0.0 copy-done
  21.3 0.0 copy-done.1
  21.3 2.5 %add_far.1 = (f32[16,768]{1,0:T(8,128)S(1)}, f32[8,128]{1,0:T(8,128)S(1)}) custom-call(s32[8,2,16]{2,1,0:T(2,128)S(1)} %bitcast.9, bf16[768,64]{1,0:T(8,128)(2,1)S(1)} %get-tuple-element.10.left_ref, bf16[4,32,768]{2,1,0:T(8,128)(2,1)S(1)} %collective-permute-done.5.blocks_ref, f32[768,16]{1,0:T(8,128)S(1)} %add_across.1.before_ref, ...), custom_call_target="tpu_custom_call" | custom-call | flops 188743680 | bytes 372736 | tf_op jit(solution)/shard_map/add_far/pallas_call | solution.py:222
  23.8 0.3 collective-permute-start.6
  24.1 0.9 %collective-permute-done.6 = f32[8,128]{1,0:T(8,128)S(1)} collective-permute-done((f32[8,128]{1,0:T(8,128)S(1)}, f32[8,128]{1,0:T(8,128)S(1)}, u32[]{:S(2)}, u32[]{:S(2)}) %collective-permute-start.6) | collective-permute-done | bytes 4128 | tf_op jit(solution)/shard_map/ppermute | solution.py:196
  25.0 3.1 %collective-permute-start.7 = (f32[8,128]{1,0:T(8,128)S(1)}, f32[8,128]{1,0:T(8,128)S(1)}, u32[]{:S(2)}, u32[]{:S(2)}) collective-permute-start(f32[8,128]{1,0:T(8,128)S(1)} %add.12), channel_id=1, source_target_pairs={{0,2},{1,3},{2,0},{3,1},{4,6},{5,7},{6,4},{7,5},{8,10},{9,11},{10,... | collective-permute-start | bytes 12296 | tf_op jit(solution)/shard_map/ppermute | solution.py:196
  28.1 1.6 %collective-permute-done.7 = f32[8,128]{1,0:T(8,128)S(1)} collective-permute-done((f32[8,128]{1,0:T(8,128)S(1)}, f32[8,128]{1,0:T(8,128)S(1)}, u32[]{:S(2)}, u32[]{:S(2)}) %collective-permute-start.7) | collective-permute-done | bytes 4128 | tf_op jit(solution)/shard_map/ppermute | solution.py:196
  29.7 2.8 %collective-permute-start.8 = (f32[8,128]{1,0:T(8,128)S(1)}, f32[8,128]{1,0:T(8,128)S(1)}, u32[]{:S(2)}, u32[]{:S(2)}) collective-permute-start(f32[8,128]{1,0:T(8,128)S(1)} %add.13), channel_id=1, source_target_pairs={{0,4},{4,0},{8,12},{12,8},{1,5},{5,1},{9,13},{13,9},{2,6},{6,2},{1... | collective-permute-start | bytes 12296 | tf_op jit(solution)/shard_map/ppermute | solution.py:196
  32.5 1.6 %collective-permute-done.8 = f32[8,128]{1,0:T(8,128)S(1)} collective-permute-done((f32[8,128]{1,0:T(8,128)S(1)}, f32[8,128]{1,0:T(8,128)S(1)}, u32[]{:S(2)}, u32[]{:S(2)}) %collective-permute-start.8) | collective-permute-done | bytes 4128 | tf_op jit(solution)/shard_map/ppermute | solution.py:196
  34.1 1.2 %collective-permute-start.9 = (f32[8,128]{1,0:T(8,128)S(1)}, f32[8,128]{1,0:T(8,128)S(1)}, u32[]{:S(2)}, u32[]{:S(2)}) collective-permute-start(f32[8,128]{1,0:T(8,128)S(1)} %add.14), channel_id=1, source_target_pairs={{0,8},{4,12},{8,0},{12,4},{1,9},{5,13},{9,1},{13,5},{2,10},{6,14},... | collective-permute-start | bytes 12296 | tf_op jit(solution)/shard_map/ppermute | solution.py:196
  35.3 3.3 %collective-permute-done.9 = f32[8,128]{1,0:T(8,128)S(1)} collective-permute-done((f32[8,128]{1,0:T(8,128)S(1)}, f32[8,128]{1,0:T(8,128)S(1)}, u32[]{:S(2)}, u32[]{:S(2)}) %collective-permute-start.9) | collective-permute-done | bytes 4128 | tf_op jit(solution)/shard_map/ppermute | solution.py:196
  38.6 1.3 %finish.1 = (f32[16,768]{1,0:T(8,128)}, f32[16,16]{1,0:T(8,128)}) custom-call(f32[8,128]{1,0:T(8,128)S(1)} %add.15.gram_ref, f32[16,768]{1,0:T(8,128)S(1)} %get-tuple-element.17.applied_ref), custom_call_target="tpu_custom_call" | custom-call | bytes 53248 | tf_op jit(solution)/shard_map/finish/pallas_call | solution.py:222
  (6 shorter events, 0.0 us)
Async XLA Ops:
  1.4 7.2 %collective-permute-start.2 = (bf16[32,768]{1,0:T(8,128)(2,1)S(1)}, bf16[32,768]{1,0:T(8,128)(2,1)S(1)}, u32[]{:S(2)}, u32[]{:S(2)}) collective-permute-start(bf16[32,768]{1,0:T(8,128)(2,1)S(1)} %pack.1.packed_ref), channel_id=1, source_target_pairs={{0,12},{4,0},{8,4},{12,8},{1,13},{5,1},{9,5},{13,9},{2,14},{6,2},{... | collective-permute-start | bytes 147464 | tf_op jit(solution)/shard_map/ppermute | solution.py:192
  6.5 5.0 %collective-permute-start.1 = (bf16[32,768]{1,0:T(8,128)(2,1)S(1)}, bf16[32,768]{1,0:T(8,128)(2,1)S(1)}, u32[]{:S(2)}, u32[]{:S(2)}) collective-permute-start(bf16[32,768]{1,0:T(8,128)(2,1)S(1)} %pack.1.packed_ref), channel_id=1, source_target_pairs={{0,8},{4,12},{8,0},{12,4},{1,9},{5,13},{9,1},{13,5},{2,10},{6,14},... | collective-permute-start | bytes 147464 | tf_op jit(solution)/shard_map/ppermute | solution.py:192
  6.5 5.9 %collective-permute-start = (bf16[32,768]{1,0:T(8,128)(2,1)S(1)}, bf16[32,768]{1,0:T(8,128)(2,1)S(1)}, u32[]{:S(2)}, u32[]{:S(2)}) collective-permute-start(bf16[32,768]{1,0:T(8,128)(2,1)S(1)} %pack.1.packed_ref), channel_id=1, source_target_pairs={{0,4},{4,8},{8,12},{12,0},{1,5},{5,9},{9,13},{13,1},{2,6},{6,10},{... | collective-permute-start | bytes 147464 | tf_op jit(solution)/shard_map/ppermute | solution.py:192
  12.4 1.7 %copy-start.2 = (s32[16,8,2]{0,2,1:T(2,128)S(1)}, s32[16,8,2]{0,2,1:T(2,128)}, u32[]{:S(2)}) copy-start(s32[16,8,2]{0,2,1:T(2,128)} %param.7) | copy-start | bytes 3076
  12.5 3.6 %collective-permute-start.4 = (bf16[4,32,768]{2,1,0:T(8,128)(2,1)S(1)}, bf16[4,32,768]{2,1,0:T(8,128)(2,1)S(1)}, u32[]{:S(2)}, u32[]{:S(2)}) collective-permute-start(bf16[4,32,768]{2,1,0:T(8,128)(2,1)S(1)} %pad_maximum_fusion.blocks_ref), channel_id=1, source_target_pairs={{0,1},{1,0},{2,3},{3,2},{4,5},{5,4},{6,7},{7,6},{8,9},{9,8},{10,11... | collective-permute-start | bytes 589832 | tf_op jit(solution)/shard_map/ppermute | solution.py:196
  12.5 7.3 %collective-permute-start.3 = (bf16[4,32,768]{2,1,0:T(8,128)(2,1)S(1)}, bf16[4,32,768]{2,1,0:T(8,128)(2,1)S(1)}, u32[]{:S(2)}, u32[]{:S(2)}) collective-permute-start(bf16[4,32,768]{2,1,0:T(8,128)(2,1)S(1)} %pad_maximum_fusion.blocks_ref), channel_id=1, source_target_pairs={{0,2},{1,3},{2,0},{3,1},{4,6},{5,7},{6,4},{7,5},{8,10},{9,11},{10,... | collective-permute-start | bytes 589832 | tf_op jit(solution)/shard_map/ppermute | solution.py:192
  17.3 4.0 %copy-start = (bf16[16,768]{1,0:T(8,128)(2,1)S(1)}, bf16[16,768]{1,0:T(8,128)(2,1)}, u32[]{:S(2)}) copy-start(bf16[16,768]{1,0:T(8,128)(2,1)} %vectors_ref.3) | copy-start | bytes 73732
  17.3 4.0 %copy-start.1 = (f32[768]{0:T(1024)S(1)}, f32[768]{0:T(1024)}, u32[]{:S(2)}) copy-start(f32[768]{0:T(1024)} %degrees_ref.3) | copy-start | bytes 9220
  19.9 1.4 %collective-permute-start.5 = (bf16[4,32,768]{2,1,0:T(8,128)(2,1)S(1)}, bf16[4,32,768]{2,1,0:T(8,128)(2,1)S(1)}, u32[]{:S(2)}, u32[]{:S(2)}) collective-permute-start(bf16[4,32,768]{2,1,0:T(8,128)(2,1)S(1)} %collective-permute-done.3.blocks_ref), channel_id=1, source_target_pairs={{0,1},{1,0},{2,3},{3,2},{4,5},{5,4},{6,7},{7,6},{8,9},{9,8},{10,11... | collective-permute-start | bytes 589832 | tf_op jit(solution)/shard_map/ppermute | solution.py:196
  23.8 1.2 %collective-permute-start.6 = (f32[8,128]{1,0:T(8,128)S(1)}, f32[8,128]{1,0:T(8,128)S(1)}, u32[]{:S(2)}, u32[]{:S(2)}) collective-permute-start(f32[8,128]{1,0:T(8,128)S(1)} %get-tuple-element.16), channel_id=1, source_target_pairs={{0,1},{1,0},{2,3},{3,2},{4,5},{5,4},{6,7},{7,6},{8,9},{9,8},{10,11... | collective-permute-start | bytes 12296 | tf_op jit(solution)/shard_map/ppermute | solution.py:196
  25.0 4.7 %collective-permute-start.7 = (f32[8,128]{1,0:T(8,128)S(1)}, f32[8,128]{1,0:T(8,128)S(1)}, u32[]{:S(2)}, u32[]{:S(2)}) collective-permute-start(f32[8,128]{1,0:T(8,128)S(1)} %add.12), channel_id=1, source_target_pairs={{0,2},{1,3},{2,0},{3,1},{4,6},{5,7},{6,4},{7,5},{8,10},{9,11},{10,... | collective-permute-start | bytes 12296 | tf_op jit(solution)/shard_map/ppermute | solution.py:196
  29.7 4.4 %collective-permute-start.8 = (f32[8,128]{1,0:T(8,128)S(1)}, f32[8,128]{1,0:T(8,128)S(1)}, u32[]{:S(2)}, u32[]{:S(2)}) collective-permute-start(f32[8,128]{1,0:T(8,128)S(1)} %add.13), channel_id=1, source_target_pairs={{0,4},{4,0},{8,12},{12,8},{1,5},{5,1},{9,13},{13,9},{2,6},{6,2},{1... | collective-permute-start | bytes 12296 | tf_op jit(solution)/shard_map/ppermute | solution.py:196
  34.1 4.5 %collective-permute-start.9 = (f32[8,128]{1,0:T(8,128)S(1)}, f32[8,128]{1,0:T(8,128)S(1)}, u32[]{:S(2)}, u32[]{:S(2)}) collective-permute-start(f32[8,128]{1,0:T(8,128)S(1)} %add.14), channel_id=1, source_target_pairs={{0,8},{4,12},{8,0},{12,4},{1,9},{5,13},{9,1},{13,5},{2,10},{6,14},... | collective-permute-start | bytes 12296 | tf_op jit(solution)/shard_map/ppermute | solution.py:196

commit v5 on v3

--- a/solution.py
+++ b/solution.py
@@ -56,30 +56,25 @@
     return jnp.concatenate([high, mid, low, edge], axis=0).T.astype(jnp.bfloat16)
 
 
-def tile_image(left_ref, x, v):
+def tile_image(left_ref, blocks):
+    both = blocks[0] if len(blocks) == 1 else jnp.concatenate(blocks, axis=1)
+    ncv = both.shape[0] // 2
+    x, v = both[:ncv, :], both[ncv:, :]
     wide = x.astype(jnp.float32)
     edge = edge_rows(jnp.sum(wide * wide, axis=0, keepdims=True), False).astype(jnp.bfloat16)
     right = jnp.concatenate([x, x, x, edge], axis=0)
-    chunk = 256
-    parts = []
-    for start in range(0, x.shape[1], chunk):
-        left = left_ref[start : start + chunk, :]
-        power = jnp.dot(left, right, preferred_element_type=jnp.float32)
-        kern = jnp.exp2(power).astype(jnp.bfloat16)
-        parts.append(lax.dot_general(v, kern, NT, preferred_element_type=jnp.float32))
-    return jnp.concatenate(parts, axis=1)
+    power = jnp.dot(left_ref[...], right, preferred_element_type=jnp.float32)
+    kern = jnp.exp2(power).astype(jnp.bfloat16)
+    return lax.dot_general(kern, v, NT, preferred_element_type=jnp.float32)
 
 
 def own_kernel(packed_ref, left_ref, image_ref):
-    ncv = packed_ref.shape[0] // 2
-    x = packed_ref[:ncv, :]
-    left_ref[...] = own_side(x)
-    image_ref[...] = tile_image(left_ref, x, packed_ref[ncv:, :])
-
-
-def add_blocks(part, sizes, table_ref, left_ref, blocks_ref, image_ref):
+    left_ref[...] = own_side(packed_ref[: packed_ref.shape[0] // 2, :])
+    image_ref[...] = tile_image(left_ref, [packed_ref[...]])
+
+
+def add_blocks(places, sizes, table_ref, left_ref, blocks_ref, image_ref, list_ref):
     n_row, n_col = sizes
-    ncv = blocks_ref.shape[1] // 2
     my_row, my_col = lax.axis_index("row"), lax.axis_index("col")
     me = my_row * n_col + my_col
     first, second = table_ref[:, 0, :], table_ref[:, 1, :]
@@ -90,41 +85,43 @@
         for b in range(16):
             bit = jnp.where(other == start + b, float(1 << b), bit)
         words.append(jnp.sum(bit).astype(jnp.int32))
-    lane_col = my_col ^ 1 if part in ("core", "far") else my_col
-
-    def visit(step, _):
-        shift = step // n_row + 1 if part in ("across", "far") else 0
-        from_row = (my_row - step % n_row + n_row) % n_row
-        from_col = (lane_col - 2 * shift + 2 * n_col) % n_col
+
+    count = jnp.int32(0)
+    for step, (rows_back, chips_back, swap) in enumerate(places):
+        from_row = (my_row + n_row - rows_back) % n_row
+        from_col = ((my_col ^ swap) + n_col - 2 * chips_back) % n_col
         block = from_row * n_col + from_col
         word = words[0]
         for w in range(1, len(words)):
             word = jnp.where(block // 16 == w, words[w], word)
-
-        @pl.when(((word >> (block % 16)) & 1) == 1)
-        def _():
-            image_ref[...] += tile_image(
-                left_ref, blocks_ref[step, :ncv, :], blocks_ref[step, ncv:, :]
-            )
-
+        list_ref[count] = step
+        count += (word >> (block % 16)) & 1
+
+    def visit(pair, _):
+        blocks = [blocks_ref[list_ref[2 * pair]], blocks_ref[list_ref[2 * pair + 1]]]
+        image_ref[...] += tile_image(left_ref, blocks)
         return 0
 
-    lax.fori_loop(1 if part == "line" else 0, blocks_ref.shape[0], visit, 0)
-
-
-def part_kernel(part, sizes, table_ref, left_ref, blocks_ref, before_ref, image_ref):
+    lax.fori_loop(0, count // 2, visit, 0)
+
+    @pl.when(count % 2 == 1)
+    def _():
+        image_ref[...] += tile_image(left_ref, [blocks_ref[list_ref[count - 1]]])
+
+
+def part_kernel(places, sizes, table_ref, left_ref, blocks_ref, before_ref, image_ref, list_ref):
     image_ref[...] = before_ref[...]
-    add_blocks(part, sizes, table_ref, left_ref, blocks_ref, image_ref)
+    add_blocks(places, sizes, table_ref, left_ref, blocks_ref, image_ref, list_ref)
 
 
 def last_kernel(
-    sizes, table_ref, left_ref, blocks_ref, before_ref, vectors_ref, degrees_ref,
-    applied_ref, gram_ref, image_ref,
+    places, sizes, table_ref, left_ref, blocks_ref, before_ref, vectors_ref, degrees_ref,
+    applied_ref, gram_ref, image_ref, list_ref,
 ):
     image_ref[...] = before_ref[...]
-    add_blocks("far", sizes, table_ref, left_ref, blocks_ref, image_ref)
+    add_blocks(places, sizes, table_ref, left_ref, blocks_ref, image_ref, list_ref)
     n = vectors_ref.shape[0]
-    applied = image_ref[...] * lax.rsqrt(degrees_ref[...])[None, :]
+    applied = image_ref[...].T * lax.rsqrt(degrees_ref[...])[None, :]
     applied_ref[...] = applied
     both = jnp.concatenate([applied, vectors_ref[...].astype(jnp.float32)], axis=0)
     gram = lax.dot_general(
@@ -226,7 +223,7 @@
         )(*args)
 
     table = tile_table.transpose(1, 2, 0)
-    image_type = ((nvec, rows), jnp.float32)
+    image_type = ((rows, nvec), jnp.float32)
 
     (packed,) = call(
         pack_kernel,
@@ -240,48 +237,54 @@
             pltpu.SemaphoreType.DMA((3,)),
         ],
     )
-    line = jnp.stack([packed] + [shifted(packed, "row", s) for s in range(1, n_row)])
+    row_blocks = [shifted(packed, "row", s) for s in range(1, n_row)]
+    chip_blocks = [shifted(packed, "col", 2 * t) for t in range(1, n_col // 2)]
     left, image = call(own_kernel, "own", [((rows, 3 * ncv + 16), jnp.bfloat16), image_type], packed, tiles=1)
 
-    def add(part, blocks, image):
+    def add(name, places, blocks, image):
         (image,) = call(
-            functools.partial(part_kernel, part, sizes),
-            "add_" + part,
+            functools.partial(part_kernel, places, sizes),
+            name,
             [image_type],
             table,
             left,
             blocks,
             image,
-            tiles=blocks.shape[0] // 2,
+            tiles=len(places) // 2,
             input_output_aliases={3: 0},
+            scratch_shapes=[pltpu.SMEM((len(places) + 1,), jnp.int32)],
         )
         return image
 
-    line, image = lax.optimization_barrier((line, image))
-    across = [shifted(line, "col", 2 * t) for t in range(1, n_col // 2)]
+    near = jnp.stack(row_blocks + chip_blocks + [packed])
+    near, image = lax.optimization_barrier((near, image))
+    across = [shifted(near[: n_row - 1], "col", 2 * t) for t in range(1, n_col // 2)]
     across = across[0] if len(across) == 1 else jnp.concatenate(across)
-    core = swapped(line)
-    image = add("line", line, image)
-    image = add("core", core, image)
+    near_places = [(s, 0, 0) for s in range(1, n_row)] + [(0, t, 0) for t in range(1, n_col // 2)]
+    across_places = [(s, t, 0) for t in range(1, n_col // 2) for s in range(1, n_row)]
+    image = add("add_near", near_places, near, image)
+    core = swapped(near)
+    image = add("add_core", [(s, t, 1) for s, t, _ in near_places + [(0, 0, 0)]], core, image)
     across, image = lax.optimization_barrier((across, image))
     far = swapped(across)
-    image = add("across", across, image)
+    image = add("add_across", across_places, across, image)
     applied, gram = call(
-        functools.partial(last_kernel, sizes),
+        functools.partial(last_kernel, [(s, t, 1) for s, t, _ in across_places], sizes),
         "add_far",
-        [((nvec, rows), jnp.float32), ((n_row, nvec // 2, 8 * nvec), jnp.float32)],
+        [((nvec, rows), jnp.float32), ((devices, nvec // 2, 8 * nvec), jnp.float32)],
         table,
         left,
         far,
         image,
         vectors,
         degrees,
-        tiles=far.shape[0] // 2,
-        scratch_shapes=[pltpu.VMEM(*image_type)],
-    )
-    grams = lax.all_to_all(gram, "row", 0, 0)
-    gram = jnp.broadcast_to(jnp.sum(grams, axis=0), (n_col, nvec // 2, 8 * nvec))
-    grams = lax.all_to_all(gram, "col", 0, 0)
+        tiles=len(across_places) // 2,
+        scratch_shapes=[
+            pltpu.VMEM(*image_type),
+            pltpu.SMEM((len(across_places) + 1,), jnp.int32),
+        ],
+    )
+    grams = lax.all_to_all(gram, ("row", "col"), 0, 0)
     basis, ritz = call(
         functools.partial(finish_kernel, rows * devices),
         "finish",

time: 41.2 us -> 35.3 us (0.86); the launches traced: 40.5 us -> 35.1 us
  blocking collectives: 16.4 us -> 11 us
  waiting for transfers between devices: 7.89 us -> 7.08 us
  starting transfers between devices: 7.74 us -> 8.21 us
    all_to_all x2 -> x1, blocking collectives: 16.4 us -> 11 us  [per_device(): grams = lax.all_to_all(gram, ('row', 'col'), 0, 0)]
    ppermute x4 -> x5, waiting for transfers between devices: 7.54 us -> 6.43 us  [shifted(): return lax.ppermute(x, axis, [(i, (i + step) % size) for i in range(size)])]
    ppermute x4 -> x5, starting transfers between devices: 7.67 us -> 8.14 us  [shifted(): return lax.ppermute(x, axis, [(i, (i + step) % size) for i in range(size)])]
  transfers between devices with their start and end apart: 6 -> 7, of which waited for: 5 -> 3; matrix products, arithmetic and copies ran while one was open for 0% -> 0% of each run, Pallas kernels for 10% -> 12%
where the time goes in v5:
time: 35.3 us; the launch traced here: 35.1 us
  blocking collectives  11 us (31%)
  starting transfers between devices  8.21 us (23%)
  Pallas kernels  7.86 us (22%)
  waiting for transfers between devices  7.08 us (20%)
  between operations  0.79 us (2%)
    all_to_all x1, blocking collectives, per_device(): grams = lax.all_to_all(gram, ('row', 'col'), 0, 0)  11 us
    ppermute x5, starting transfers between devices, shifted(): return lax.ppermute(x, axis, [(i, (i + step) % size) for i in range(size)])  8.14 us
    pallas_call x7, Pallas kernels, call(): pl.pallas_call(kernel, out_shape=shapes, in_specs=[where] * len(args), ou...  7.86 us
    ppermute x5, waiting for transfers between devices, shifted(): return lax.ppermute(x, axis, [(i, (i + step) % size) for i in range(size)])  6.43 us
  transfers between devices with their start and end apart: 7, of which 3 were waited for; matrix products, arithmetic and copies ran while one was open for 0% of the time, Pallas kernels for 12%

profile of v5, /device:TPU:0, one launch (start us, length us, event | category | flops | bytes accessed | tf_op | source)
XLA Modules:
  0.0 35.1 jit_solution(2309159671065916149)
XLA Ops:
  0.6 0.8 %pack.1.packed_ref = bf16[32,768]{1,0:T(8,128)(2,1)S(1)} custom-call(bf16[16,768]{1,0:T(8,128)(2,1)} %frames_ref.1, bf16[16,768]{1,0:T(8,128)(2,1)} %vectors_ref.3, f32[768]{0:T(1024)} %degrees_ref.3), custom_call_target="tpu_custom_call" | custom-call | bytes 52224 | tf_op jit(solution)/shard_map/pack/pallas_call | solution.py:215
  1.4 3.1 %collective-permute-start = (bf16[32,768]{1,0:T(8,128)(2,1)S(1)}, bf16[32,768]{1,0:T(8,128)(2,1)S(1)}, u32[]{:S(2)}, u32[]{:S(2)}) collective-permute-start(bf16[32,768]{1,0:T(8,128)(2,1)S(1)} %pack.1.packed_ref), channel_id=1, source_target_pairs={{0,4},{4,8},{8,12},{12,0},{1,5},{5,9},{9,13},{13,1},{2,6},{6,10},{... | collective-permute-start | bytes 147464 | tf_op jit(solution)/shard_map/ppermute | solution.py:193
  4.5 1.5 %collective-permute-start.3 = (bf16[32,768]{1,0:T(8,128)(2,1)S(1)}, bf16[32,768]{1,0:T(8,128)(2,1)S(1)}, u32[]{:S(2)}, u32[]{:S(2)}) collective-permute-start(bf16[32,768]{1,0:T(8,128)(2,1)S(1)} %pack.1.packed_ref), channel_id=1, source_target_pairs={{0,2},{1,3},{2,0},{3,1},{4,6},{5,7},{6,4},{7,5},{8,10},{9,11},{10,... | collective-permute-start | bytes 147464 | tf_op jit(solution)/shard_map/ppermute | solution.py:193
  6.0 2.2 %collective-permute-start.2 = (bf16[32,768]{1,0:T(8,128)(2,1)S(1)}, bf16[32,768]{1,0:T(8,128)(2,1)S(1)}, u32[]{:S(2)}, u32[]{:S(2)}) collective-permute-start(bf16[32,768]{1,0:T(8,128)(2,1)S(1)} %pack.1.packed_ref), channel_id=1, source_target_pairs={{0,12},{4,0},{8,4},{12,8},{1,13},{5,1},{9,5},{13,9},{2,14},{6,2},{... | collective-permute-start | bytes 147464 | tf_op jit(solution)/shard_map/ppermute | solution.py:193
  8.3 0.8 %collective-permute-start.1 = (bf16[32,768]{1,0:T(8,128)(2,1)S(1)}, bf16[32,768]{1,0:T(8,128)(2,1)S(1)}, u32[]{:S(2)}, u32[]{:S(2)}) collective-permute-start(bf16[32,768]{1,0:T(8,128)(2,1)S(1)} %pack.1.packed_ref), channel_id=1, source_target_pairs={{0,8},{4,12},{8,0},{12,4},{1,9},{5,13},{9,1},{13,5},{2,10},{6,14},... | collective-permute-start | bytes 147464 | tf_op jit(solution)/shard_map/ppermute | solution.py:193
  9.0 0.9 %own.1 = (bf16[768,64]{1,0:T(8,128)(2,1)S(1)}, f32[768,16]{1,0:T(8,128)S(1)}) custom-call(bf16[32,768]{1,0:T(8,128)(2,1)S(1)} %pack.1.packed_ref), custom_call_target="tpu_custom_call" | custom-call | flops 94371840 | bytes 49152 | tf_op jit(solution)/shard_map/own/pallas_call | solution.py:215
  10.0 0.0 collective-permute-done
  10.0 3.2 %collective-permute-done.1 = bf16[32,768]{1,0:T(8,128)(2,1)S(1)} collective-permute-done((bf16[32,768]{1,0:T(8,128)(2,1)S(1)}, bf16[32,768]{1,0:T(8,128)(2,1)S(1)}, u32[]{:S(2)}, u32[]{:S(2)}) %collective-permute-start.1) | collective-permute-done | bytes 49184 | tf_op jit(solution)/shard_map/ppermute | solution.py:193
  13.2 0.0 collective-permute-done.2
  13.3 0.0 collective-permute-done.3
  13.3 0.0 copy-start.1
  13.3 0.1 collective-permute-start.5
  13.4 0.5 %collective-permute-start.4 = (bf16[3,32,768]{2,1,0:T(8,128)(2,1)S(1)}, bf16[3,32,768]{2,1,0:T(8,128)(2,1)S(1)}, u32[]{:S(2)}, u32[]{:S(2)}) collective-permute-start(bf16[3,32,768]{2,1,0:T(8,128)(2,1)S(1)} %slice.3), channel_id=1, source_target_pairs={{0,2},{1,3},{2,0},{3,1},{4,6},{5,7},{6,4},{7,5},{8,10},{9,11},{10,... | collective-permute-start | bytes 442376 | tf_op jit(solution)/shard_map/ppermute | solution.py:193
  13.9 0.1 copy-done.1
  14.0 0.2 add_near.1.before_ref
  14.2 0.7 %collective-permute-done.5.blocks_ref = bf16[5,32,768]{2,1,0:T(8,128)(2,1)S(1)} collective-permute-done((bf16[5,32,768]{2,1,0:T(8,128)(2,1)S(1)}, bf16[5,32,768]{2,1,0:T(8,128)(2,1)S(1)}, u32[]{:S(2)}, u32[]{:S(2)}) %collective-permute-start.5) | collective-permute-done | bytes 245792 | tf_op jit(solution)/shard_map/ppermute | solution.py:197
  14.9 1.6 %add_core.1.before_ref = f32[768,16]{1,0:T(8,128)S(1)} custom-call(s32[8,2,16]{2,1,0:T(2,128)S(1)} %bitcast.12, bf16[768,64]{1,0:T(8,128)(2,1)S(1)} %get-tuple-element.10.left_ref, bf16[5,32,768]{2,1,0:T(8,128)(2,1)S(1)} %collective-permute-done.5.blocks_ref, f32[768,16]{1,0:T(8,128)S(1)} %add_near.1.before_ref), custom_call_target="tpu_custom_call", output_to_operand_aliasing={{}: (3, {})} | custom-call | flops 188743680 | bytes 394240 | tf_op jit(solution)/shard_map/add_core/pallas_call | solution.py:215
  16.5 0.0 copy-start
  16.5 0.0 copy-start.2
  16.5 3.2 %collective-permute-done.4.blocks_ref = bf16[3,32,768]{2,1,0:T(8,128)(2,1)S(1)} collective-permute-done((bf16[3,32,768]{2,1,0:T(8,128)(2,1)S(1)}, bf16[3,32,768]{2,1,0:T(8,128)(2,1)S(1)}, u32[]{:S(2)}, u32[]{:S(2)}) %collective-permute-start.4) | collective-permute-done | bytes 147488 | tf_op jit(solution)/shard_map/ppermute | solution.py:193
  19.7 0.0 collective-permute-start.6
  19.7 1.6 %add_across.1.before_ref = f32[768,16]{1,0:T(8,128)S(1)} custom-call(s32[8,2,16]{2,1,0:T(2,128)S(1)} %bitcast.13, bf16[768,64]{1,0:T(8,128)(2,1)S(1)} %get-tuple-element.10.left_ref, bf16[3,32,768]{2,1,0:T(8,128)(2,1)S(1)} %collective-permute-done.4.blocks_ref, f32[768,16]{1,0:T(8,128)S(1)} %add_core.1.before_ref), custom_call_target="tpu_custom_call", output_to_operand_aliasing={{}: (3, {})} | custom-call | flops 94371840 | bytes 295936 | tf_op jit(solution)/shard_map/add_across/pallas_call | solution.py:215
  21.3 0.0 collective-permute-done.6.blocks_ref
  21.3 0.0 copy-done
  21.4 0.0 copy-done.2
  21.4 1.4 %add_far.1 = (f32[16,768]{1,0:T(8,128)S(1)}, f32[16,8,128]{2,1,0:T(8,128)S(1)}) custom-call(s32[8,2,16]{2,1,0:T(2,128)S(1)} %bitcast.14, bf16[768,64]{1,0:T(8,128)(2,1)S(1)} %get-tuple-element.10.left_ref, bf16[3,32,768]{2,1,0:T(8,128)(2,1)S(1)} %collective-permute-done.6.blocks_ref, f32[768,16]{1,0:T(8,128)S(1)} %add_across.1.before_ref, ...), custom_call_target="tpu_custom_call" | custom-call | flops 94371840 | bytes 323584 | tf_op jit(solution)/shard_map/add_far/pallas_call | solution.py:215
  22.8 11.0 %all_to_all.5.grams_ref = f32[16,8,128]{2,1,0:T(8,128)S(1)} all-to-all(f32[16,8,128]{2,1,0:T(8,128)S(1)} %get-tuple-element.16), channel_id=1, replica_groups=mesh['grp'=2,'row'=4,'col'=4] {'row','col'}, dimensions={0} | all-to-all | bytes 131072 | tf_op jit(solution)/shard_map/all_to_all | solution.py:287
  33.8 1.3 %finish.1 = (f32[16,768]{1,0:T(8,128)}, f32[16,16]{1,0:T(8,128)}) custom-call(f32[16,8,128]{2,1,0:T(8,128)S(1)} %all_to_all.5.grams_ref, f32[16,768]{1,0:T(8,128)S(1)} %get-tuple-element.17.applied_ref), custom_call_target="tpu_custom_call" | custom-call | bytes 114688 | tf_op jit(solution)/shard_map/finish/pallas_call | solution.py:215
  (6 shorter events, 0.0 us)
Async XLA Ops:
  1.4 8.6 %collective-permute-start = (bf16[32,768]{1,0:T(8,128)(2,1)S(1)}, bf16[32,768]{1,0:T(8,128)(2,1)S(1)}, u32[]{:S(2)}, u32[]{:S(2)}) collective-permute-start(bf16[32,768]{1,0:T(8,128)(2,1)S(1)} %pack.1.packed_ref), channel_id=1, source_target_pairs={{0,4},{4,8},{8,12},{12,0},{1,5},{5,9},{9,13},{13,1},{2,6},{6,10},{... | collective-permute-start | bytes 147464 | tf_op jit(solution)/shard_map/ppermute | solution.py:193
  4.5 8.8 %collective-permute-start.3 = (bf16[32,768]{1,0:T(8,128)(2,1)S(1)}, bf16[32,768]{1,0:T(8,128)(2,1)S(1)}, u32[]{:S(2)}, u32[]{:S(2)}) collective-permute-start(bf16[32,768]{1,0:T(8,128)(2,1)S(1)} %pack.1.packed_ref), channel_id=1, source_target_pairs={{0,2},{1,3},{2,0},{3,1},{4,6},{5,7},{6,4},{7,5},{8,10},{9,11},{10,... | collective-permute-start | bytes 147464 | tf_op jit(solution)/shard_map/ppermute | solution.py:193
  6.0 7.2 %collective-permute-start.2 = (bf16[32,768]{1,0:T(8,128)(2,1)S(1)}, bf16[32,768]{1,0:T(8,128)(2,1)S(1)}, u32[]{:S(2)}, u32[]{:S(2)}) collective-permute-start(bf16[32,768]{1,0:T(8,128)(2,1)S(1)} %pack.1.packed_ref), channel_id=1, source_target_pairs={{0,12},{4,0},{8,4},{12,8},{1,13},{5,1},{9,5},{13,9},{2,14},{6,2},{... | collective-permute-start | bytes 147464 | tf_op jit(solution)/shard_map/ppermute | solution.py:193
  8.3 5.0 %collective-permute-start.1 = (bf16[32,768]{1,0:T(8,128)(2,1)S(1)}, bf16[32,768]{1,0:T(8,128)(2,1)S(1)}, u32[]{:S(2)}, u32[]{:S(2)}) collective-permute-start(bf16[32,768]{1,0:T(8,128)(2,1)S(1)} %pack.1.packed_ref), channel_id=1, source_target_pairs={{0,8},{4,12},{8,0},{12,4},{1,9},{5,13},{9,1},{13,5},{2,10},{6,14},... | collective-permute-start | bytes 147464 | tf_op jit(solution)/shard_map/ppermute | solution.py:193
  13.3 0.7 %copy-start.1 = (s32[16,8,2]{0,2,1:T(2,128)S(1)}, s32[16,8,2]{0,2,1:T(2,128)}, u32[]{:S(2)}) copy-start(s32[16,8,2]{0,2,1:T(2,128)} %param.7) | copy-start | bytes 3076
  13.3 1.6 %collective-permute-start.5 = (bf16[5,32,768]{2,1,0:T(8,128)(2,1)S(1)}, bf16[5,32,768]{2,1,0:T(8,128)(2,1)S(1)}, u32[]{:S(2)}, u32[]{:S(2)}) collective-permute-start(bf16[5,32,768]{2,1,0:T(8,128)(2,1)S(1)} %bitcast_dynamic-update-slice_fusion.blocks_ref), channel_id=1, source_target_pairs={{0,1},{1,0},{2,3},{3,2},{4,5},{5,4},{6,7},{7,6},{8,9},{9,8},{10,11... | collective-permute-start | bytes 737288 | tf_op jit(solution)/shard_map/ppermute | solution.py:197
  13.4 6.3 %collective-permute-start.4 = (bf16[3,32,768]{2,1,0:T(8,128)(2,1)S(1)}, bf16[3,32,768]{2,1,0:T(8,128)(2,1)S(1)}, u32[]{:S(2)}, u32[]{:S(2)}) collective-permute-start(bf16[3,32,768]{2,1,0:T(8,128)(2,1)S(1)} %slice.3), channel_id=1, source_target_pairs={{0,2},{1,3},{2,0},{3,1},{4,6},{5,7},{6,4},{7,5},{8,10},{9,11},{10,... | collective-permute-start | bytes 442376 | tf_op jit(solution)/shard_map/ppermute | solution.py:193
  16.5 4.8 %copy-start = (bf16[16,768]{1,0:T(8,128)(2,1)S(1)}, bf16[16,768]{1,0:T(8,128)(2,1)}, u32[]{:S(2)}) copy-start(bf16[16,768]{1,0:T(8,128)(2,1)} %vectors_ref.3) | copy-start | bytes 73732
  16.5 4.8 %copy-start.2 = (f32[768]{0:T(1024)S(1)}, f32[768]{0:T(1024)}, u32[]{:S(2)}) copy-start(f32[768]{0:T(1024)} %degrees_ref.3) | copy-start | bytes 9220
  19.7 1.6 %collective-permute-start.6 = (bf16[3,32,768]{2,1,0:T(8,128)(2,1)S(1)}, bf16[3,32,768]{2,1,0:T(8,128)(2,1)S(1)}, u32[]{:S(2)}, u32[]{:S(2)}) collective-permute-start(bf16[3,32,768]{2,1,0:T(8,128)(2,1)S(1)} %collective-permute-done.4.blocks_ref), channel_id=1, source_target_pairs={{0,1},{1,0},{2,3},{3,2},{4,5},{5,4},{6,7},{7,6},{8,9},{9,8},{10,11... | collective-permute-start | bytes 442376 | tf_op jit(solution)/shard_map/ppermute | solution.py:197

commit v6 on v5

--- a/solution.py
+++ b/solution.py
@@ -73,7 +73,7 @@
     image_ref[...] = tile_image(left_ref, [packed_ref[...]])
 
 
-def add_blocks(places, sizes, table_ref, left_ref, blocks_ref, image_ref, list_ref):
+def add_blocks(swap, places, sizes, table_ref, left_ref, blocks_ref, image_ref, list_ref):
     n_row, n_col = sizes
     my_row, my_col = lax.axis_index("row"), lax.axis_index("col")
     me = my_row * n_col + my_col
@@ -87,10 +87,8 @@
         words.append(jnp.sum(bit).astype(jnp.int32))
 
     count = jnp.int32(0)
-    for step, (rows_back, chips_back, swap) in enumerate(places):
-        from_row = (my_row + n_row - rows_back) % n_row
-        from_col = ((my_col ^ swap) + n_col - 2 * chips_back) % n_col
-        block = from_row * n_col + from_col
+    for step, (row_bits, chip_bits) in enumerate(places):
+        block = (my_row ^ row_bits) * n_col + (my_col ^ (2 * chip_bits + swap))
         word = words[0]
         for w in range(1, len(words)):
             word = jnp.where(block // 16 == w, words[w], word)
@@ -109,17 +107,19 @@
         image_ref[...] += tile_image(left_ref, [blocks_ref[list_ref[count - 1]]])
 
 
-def part_kernel(places, sizes, table_ref, left_ref, blocks_ref, before_ref, image_ref, list_ref):
+def part_kernel(
+    swap, places, sizes, table_ref, left_ref, blocks_ref, before_ref, image_ref, list_ref
+):
     image_ref[...] = before_ref[...]
-    add_blocks(places, sizes, table_ref, left_ref, blocks_ref, image_ref, list_ref)
+    add_blocks(swap, places, sizes, table_ref, left_ref, blocks_ref, image_ref, list_ref)
 
 
 def last_kernel(
-    places, sizes, table_ref, left_ref, blocks_ref, before_ref, vectors_ref, degrees_ref,
+    swap, places, sizes, table_ref, left_ref, blocks_ref, before_ref, vectors_ref, degrees_ref,
     applied_ref, gram_ref, image_ref, list_ref,
 ):
     image_ref[...] = before_ref[...]
-    add_blocks(places, sizes, table_ref, left_ref, blocks_ref, image_ref, list_ref)
+    add_blocks(swap, places, sizes, table_ref, left_ref, blocks_ref, image_ref, list_ref)
     n = vectors_ref.shape[0]
     applied = image_ref[...].T * lax.rsqrt(degrees_ref[...])[None, :]
     applied_ref[...] = applied
@@ -188,9 +188,19 @@
     ritz_ref[...] = exact(half, vector_inverse, NT)
 
 
-def shifted(x, axis, step):
-    size = lax.axis_size(axis)
-    return lax.ppermute(x, axis, [(i, (i + step) % size) for i in range(size)])
+def sent(x, offset):
+    rows, chips = offset
+    axis, bits = ("row", rows) if rows else ("col", 2 * chips)
+    return lax.ppermute(x, axis, [(i, i ^ bits) for i in range(lax.axis_size(axis))])
+
+
+def exchange_plan(n_row, n_chip):
+    if (n_row, n_chip) == (4, 2):
+        direct = [(2, 0), (1, 0), (0, 1)]
+        return direct, [((0, 1), [(1, 0), (2, 0)]), ((3, 0), [(0, 1)]), ((1, 0), [(2, 0)])]
+    lines = [(r, 0) for r in range(1, n_row)]
+    chips = [(0, c) for c in range(1, n_chip)]
+    return lines + chips, [(chip, lines) for chip in chips]
 
 
 def swapped(x):
@@ -237,13 +247,15 @@
             pltpu.SemaphoreType.DMA((3,)),
         ],
     )
-    row_blocks = [shifted(packed, "row", s) for s in range(1, n_row)]
-    chip_blocks = [shifted(packed, "col", 2 * t) for t in range(1, n_col // 2)]
-    left, image = call(own_kernel, "own", [((rows, 3 * ncv + 16), jnp.bfloat16), image_type], packed, tiles=1)
-
-    def add(name, places, blocks, image):
+    direct, forwards = exchange_plan(n_row, n_col // 2)
+    held = {offset: sent(packed, offset) for offset in direct}
+    left, image = call(
+        own_kernel, "own", [((rows, 3 * ncv + 16), jnp.bfloat16), image_type], packed, tiles=1
+    )
+
+    def add(name, swap, places, blocks, image):
         (image,) = call(
-            functools.partial(part_kernel, places, sizes),
+            functools.partial(part_kernel, swap, places, sizes),
             name,
             [image_type],
             table,
@@ -256,20 +268,23 @@
         )
         return image
 
-    near = jnp.stack(row_blocks + chip_blocks + [packed])
-    near, image = lax.optimization_barrier((near, image))
-    across = [shifted(near[: n_row - 1], "col", 2 * t) for t in range(1, n_col // 2)]
-    across = across[0] if len(across) == 1 else jnp.concatenate(across)
-    near_places = [(s, 0, 0) for s in range(1, n_row)] + [(0, t, 0) for t in range(1, n_col // 2)]
-    across_places = [(s, t, 0) for t in range(1, n_col // 2) for s in range(1, n_row)]
-    image = add("add_near", near_places, near, image)
+    near_places = direct + [(0, 0)]
+    near = jnp.stack([held[offset] for offset in direct] + [packed])
+    near, image, held = lax.optimization_barrier((near, image, held))
+    across_places = []
+    across = []
+    for hop, offsets in forwards:
+        across.append(sent(jnp.stack([held[offset] for offset in offsets]), hop))
+        across_places += [(r ^ hop[0], c ^ hop[1]) for r, c in offsets]
     core = swapped(near)
-    image = add("add_core", [(s, t, 1) for s, t, _ in near_places + [(0, 0, 0)]], core, image)
+    image = add("add_near", 0, direct, near, image)
+    image = add("add_core", 1, near_places, core, image)
     across, image = lax.optimization_barrier((across, image))
+    across = jnp.concatenate(across)
     far = swapped(across)
-    image = add("add_across", across_places, across, image)
+    image = add("add_across", 0, across_places, across, image)
     applied, gram = call(
-        functools.partial(last_kernel, [(s, t, 1) for s, t, _ in across_places], sizes),
+        functools.partial(last_kernel, 1, across_places, sizes),
         "add_far",
         [((nvec, rows), jnp.float32), ((devices, nvec // 2, 8 * nvec), jnp.float32)],
         table,

time: 35.3 us -> 35.3 us (level)
  waiting for transfers between devices: 7.08 us -> 3.37 us
  starting transfers between devices: 8.21 us -> 10.7 us
  Pallas kernels: 7.86 us -> 8.64 us
  blocking collectives: 11 us -> 11.6 us
    ppermute x5 -> x6, waiting for transfers between devices: 6.43 us -> 2.95 us  [sent(): lax.ppermute(x, axis, [(i, i ^ bits) for i in range(lax.axis_size(axis))])]
    ppermute x5 -> x6, starting transfers between devices: 8.14 us -> 10.5 us  [sent(): lax.ppermute(x, axis, [(i, i ^ bits) for i in range(lax.axis_size(axis))])]
    pallas_call x7, Pallas kernels: 7.86 us -> 8.64 us  [call(): pl.pallas_call(kernel, out_shape=shapes, in_specs=[where] * len(args), ou...]
    all_to_all x1, blocking collectives: 11 us -> 11.6 us  [per_device(): grams = lax.all_to_all(gram, ('row', 'col'), 0, 0)]
  transfers between devices with their start and end apart: 7 -> 8, of which waited for: 3 -> 4; matrix products, arithmetic and copies ran while one was open for 0% -> 0% of each run, Pallas kernels for 12% -> 15%
where the time goes in v6:
time: 35.3 us; the launch traced here: 35.1 us
  blocking collectives  11.6 us (33%)
  starting transfers between devices  10.7 us (30%)
  Pallas kernels  8.64 us (24%)
  waiting for transfers between devices  3.37 us (10%)
  between operations  0.77 us (2%)
    all_to_all x1, blocking collectives, per_device(): grams = lax.all_to_all(gram, ('row', 'col'), 0, 0)  11.6 us
    ppermute x6, starting transfers between devices, sent(): lax.ppermute(x, axis, [(i, i ^ bits) for i in range(lax.axis_size(axis))])  10.5 us
    pallas_call x7, Pallas kernels, call(): pl.pallas_call(kernel, out_shape=shapes, in_specs=[where] * len(args), ou...  8.64 us
    ppermute x6, waiting for transfers between devices, sent(): lax.ppermute(x, axis, [(i, i ^ bits) for i in range(lax.axis_size(axis))])  2.95 us
  transfers between devices with their start and end apart: 8, of which 4 were waited for; matrix products, arithmetic and copies ran while one was open for 0% of the time, Pallas kernels for 15%

profile of v6, /device:TPU:0, one launch (start us, length us, event | category | flops | bytes accessed | tf_op | source)
XLA Modules:
  0.0 35.1 jit_solution(13425384385825369739)
XLA Ops:
  0.6 0.8 %pack.1.packed_ref = bf16[32,768]{1,0:T(8,128)(2,1)S(1)} custom-call(bf16[16,768]{1,0:T(8,128)(2,1)} %frames_ref.1, bf16[16,768]{1,0:T(8,128)(2,1)} %vectors_ref.3, f32[768]{0:T(1024)} %degrees_ref.3), custom_call_target="tpu_custom_call" | custom-call | bytes 52224 | tf_op jit(solution)/shard_map/pack/pallas_call | solution.py:225
  1.4 4.1 %collective-permute-start = (bf16[32,768]{1,0:T(8,128)(2,1)S(1)}, bf16[32,768]{1,0:T(8,128)(2,1)S(1)}, u32[]{:S(2)}, u32[]{:S(2)}) collective-permute-start(bf16[32,768]{1,0:T(8,128)(2,1)S(1)} %pack.1.packed_ref), channel_id=1, source_target_pairs={{0,8},{4,12},{8,0},{12,4},{1,9},{5,13},{9,1},{13,5},{2,10},{6,14},... | collective-permute-start | bytes 147464 | tf_op jit(solution)/shard_map/ppermute | solution.py:194
  5.5 1.6 %collective-permute-start.1 = (bf16[32,768]{1,0:T(8,128)(2,1)S(1)}, bf16[32,768]{1,0:T(8,128)(2,1)S(1)}, u32[]{:S(2)}, u32[]{:S(2)}) collective-permute-start(bf16[32,768]{1,0:T(8,128)(2,1)S(1)} %pack.1.packed_ref), channel_id=1, source_target_pairs={{0,4},{4,0},{8,12},{12,8},{1,5},{5,1},{9,13},{13,9},{2,6},{6,2},{1... | collective-permute-start | bytes 147464 | tf_op jit(solution)/shard_map/ppermute | solution.py:194
  7.1 1.5 %collective-permute-start.2 = (bf16[32,768]{1,0:T(8,128)(2,1)S(1)}, bf16[32,768]{1,0:T(8,128)(2,1)S(1)}, u32[]{:S(2)}, u32[]{:S(2)}) collective-permute-start(bf16[32,768]{1,0:T(8,128)(2,1)S(1)} %pack.1.packed_ref), channel_id=1, source_target_pairs={{0,2},{1,3},{2,0},{3,1},{4,6},{5,7},{6,4},{7,5},{8,10},{9,11},{10,... | collective-permute-start | bytes 147464 | tf_op jit(solution)/shard_map/ppermute | solution.py:194
  8.6 0.9 %own.1 = (bf16[768,64]{1,0:T(8,128)(2,1)S(1)}, f32[768,16]{1,0:T(8,128)S(1)}) custom-call(bf16[32,768]{1,0:T(8,128)(2,1)S(1)} %pack.1.packed_ref), custom_call_target="tpu_custom_call" | custom-call | flops 94371840 | bytes 49152 | tf_op jit(solution)/shard_map/own/pallas_call | solution.py:225
  9.6 0.0 collective-permute-done
  9.6 0.1 collective-permute-done.1
  9.6 1.6 %collective-permute-done.2 = bf16[32,768]{1,0:T(8,128)(2,1)S(1)} collective-permute-done((bf16[32,768]{1,0:T(8,128)(2,1)S(1)}, bf16[32,768]{1,0:T(8,128)(2,1)S(1)}, u32[]{:S(2)}, u32[]{:S(2)}) %collective-permute-start.2) | collective-permute-done | bytes 49184 | tf_op jit(solution)/shard_map/ppermute | solution.py:194
  11.2 0.1 collective-permute-start.6
  11.3 0.0 copy-start.1
  11.3 1.6 %collective-permute-start.3 = (bf16[2,32,768]{2,1,0:T(8,128)(2,1)S(1)}, bf16[2,32,768]{2,1,0:T(8,128)(2,1)S(1)}, u32[]{:S(2)}, u32[]{:S(2)}) collective-permute-start(bf16[2,32,768]{2,1,0:T(8,128)(2,1)S(1)} %pad_maximum_fusion.1), channel_id=1, source_target_pairs={{0,2},{1,3},{2,0},{3,1},{4,6},{5,7},{6,4},{7,5},{8,10},{9,11},{10,... | collective-permute-start | bytes 294920 | tf_op jit(solution)/shard_map/ppermute | solution.py:194
  12.9 0.4 %collective-permute-start.5 = (bf16[1,32,768]{2,1,0:T(8,128)(2,1)S(1)}, bf16[1,32,768]{2,1,0:T(8,128)(2,1)S(1)}, u32[]{:S(2)}, u32[]{:S(2)}) collective-permute-start(bf16[1,32,768]{2,1,0:T(8,128)(2,1)S(1)} %bitcast.15), channel_id=1, source_target_pairs={{0,4},{4,0},{8,12},{12,8},{1,5},{5,1},{9,13},{13,9},{2,6},{6,2},{1... | collective-permute-start | bytes 147464 | tf_op jit(solution)/shard_map/ppermute | solution.py:194
  13.4 1.3 %collective-permute-start.4 = (bf16[1,32,768]{2,1,0:T(8,128)(2,1)S(1)}, bf16[1,32,768]{2,1,0:T(8,128)(2,1)S(1)}, u32[]{:S(2)}, u32[]{:S(2)}) collective-permute-start(bf16[1,32,768]{2,1,0:T(8,128)(2,1)S(1)} %bitcast.19), channel_id=1, source_target_pairs={{0,12},{4,8},{8,4},{12,0},{1,13},{5,9},{9,5},{13,1},{2,14},{6,10},... | collective-permute-start | bytes 147464 | tf_op jit(solution)/shard_map/ppermute | solution.py:194
  14.7 0.0 copy-done.1
  14.7 1.6 %add_near.1.before_ref = f32[768,16]{1,0:T(8,128)S(1)} custom-call(s32[8,2,16]{2,1,0:T(2,128)S(1)} %bitcast.9, bf16[768,64]{1,0:T(8,128)(2,1)S(1)} %get-tuple-element.15.left_ref, bf16[4,32,768]{2,1,0:T(8,128)(2,1)S(1)} %pad_maximum_fusion.blocks_ref, f32[768,16]{1,0:T(8,128)S(1)} %get-tuple-element.21.before_ref), custom_call_target="tpu_custom_call", output_to_operand_aliasing={{}: (3, {})} | custom-call | flops 94371840 | bytes 345088 | tf_op jit(solution)/shard_map/add_near/pallas_call | solution.py:225
  16.3 0.0 collective-permute-done.6.blocks_ref
  16.3 1.6 %add_core.1.before_ref = f32[768,16]{1,0:T(8,128)S(1)} custom-call(s32[8,2,16]{2,1,0:T(2,128)S(1)} %bitcast.10, bf16[768,64]{1,0:T(8,128)(2,1)S(1)} %get-tuple-element.15.left_ref, bf16[4,32,768]{2,1,0:T(8,128)(2,1)S(1)} %collective-permute-done.6.blocks_ref, f32[768,16]{1,0:T(8,128)S(1)} %add_near.1.before_ref), custom_call_target="tpu_custom_call", output_to_operand_aliasing={{}: (3, {})} | custom-call | flops 188743680 | bytes 345088 | tf_op jit(solution)/shard_map/add_core/pallas_call | solution.py:225
  17.9 0.0 collective-permute-done.5
  17.9 1.3 %collective-permute-done.4 = bf16[1,32,768]{2,1,0:T(8,128)(2,1)S(1)} collective-permute-done((bf16[1,32,768]{2,1,0:T(8,128)(2,1)S(1)}, bf16[1,32,768]{2,1,0:T(8,128)(2,1)S(1)}, u32[]{:S(2)}, u32[]{:S(2)}) %collective-permute-start.4) | collective-permute-done | bytes 49184 | tf_op jit(solution)/shard_map/ppermute | solution.py:194
  19.2 0.0 collective-permute-done.3
  19.3 0.0 copy-start
  19.3 0.0 copy-start.2
  19.3 0.1 collective-permute-start.7
  19.4 1.0 %add_across.1.before_ref = f32[768,16]{1,0:T(8,128)S(1)} custom-call(s32[8,2,16]{2,1,0:T(2,128)S(1)} %bitcast.11, bf16[768,64]{1,0:T(8,128)(2,1)S(1)} %get-tuple-element.15.left_ref, bf16[4,32,768]{2,1,0:T(8,128)(2,1)S(1)} %constant_dynamic-update-slice_fusion.blocks_ref, f32[768,16]{1,0:T(8,128)S(1)} %add_core.1.before_ref), custom_call_target="tpu_custom_call", output_to_operand_aliasing={{}: (3, {})} | custom-call | flops 188743680 | bytes 345088 | tf_op jit(solution)/shard_map/add_across/pallas_call | solution.py:225
  20.4 0.4 %collective-permute-done.7.blocks_ref = bf16[4,32,768]{2,1,0:T(8,128)(2,1)S(1)} collective-permute-done((bf16[4,32,768]{2,1,0:T(8,128)(2,1)S(1)}, bf16[4,32,768]{2,1,0:T(8,128)(2,1)S(1)}, u32[]{:S(2)}, u32[]{:S(2)}) %collective-permute-start.7) | collective-permute-done | bytes 196640 | tf_op jit(solution)/shard_map/ppermute | solution.py:207
  20.8 0.0 copy-done
  20.8 0.0 copy-done.2
  20.8 1.4 %add_far.1 = (f32[16,768]{1,0:T(8,128)S(1)}, f32[16,8,128]{2,1,0:T(8,128)S(1)}) custom-call(s32[8,2,16]{2,1,0:T(2,128)S(1)} %bitcast.12, bf16[768,64]{1,0:T(8,128)(2,1)S(1)} %get-tuple-element.15.left_ref, bf16[4,32,768]{2,1,0:T(8,128)(2,1)S(1)} %collective-permute-done.7.blocks_ref, f32[768,16]{1,0:T(8,128)S(1)} %add_across.1.before_ref, ...), custom_call_target="tpu_custom_call" | custom-call | flops 188743680 | bytes 372736 | tf_op jit(solution)/shard_map/add_far/pallas_call | solution.py:225
  22.2 11.6 %all_to_all.5.grams_ref = f32[16,8,128]{2,1,0:T(8,128)S(1)} all-to-all(f32[16,8,128]{2,1,0:T(8,128)S(1)} %get-tuple-element.26), channel_id=1, replica_groups=mesh['grp'=2,'row'=4,'col'=4] {'row','col'}, dimensions={0} | all-to-all | bytes 131072 | tf_op jit(solution)/shard_map/all_to_all | solution.py:302
  33.8 1.3 %finish.1 = (f32[16,768]{1,0:T(8,128)}, f32[16,16]{1,0:T(8,128)}) custom-call(f32[16,8,128]{2,1,0:T(8,128)S(1)} %all_to_all.5.grams_ref, f32[16,768]{1,0:T(8,128)S(1)} %get-tuple-element.27.applied_ref), custom_call_target="tpu_custom_call" | custom-call | bytes 114688 | tf_op jit(solution)/shard_map/finish/pallas_call | solution.py:225
  (5 shorter events, 0.1 us)
Async XLA Ops:
  1.4 8.1 %collective-permute-start = (bf16[32,768]{1,0:T(8,128)(2,1)S(1)}, bf16[32,768]{1,0:T(8,128)(2,1)S(1)}, u32[]{:S(2)}, u32[]{:S(2)}) collective-permute-start(bf16[32,768]{1,0:T(8,128)(2,1)S(1)} %pack.1.packed_ref), channel_id=1, source_target_pairs={{0,8},{4,12},{8,0},{12,4},{1,9},{5,13},{9,1},{13,5},{2,10},{6,14},... | collective-permute-start | bytes 147464 | tf_op jit(solution)/shard_map/ppermute | solution.py:194
  5.5 4.1 %collective-permute-start.1 = (bf16[32,768]{1,0:T(8,128)(2,1)S(1)}, bf16[32,768]{1,0:T(8,128)(2,1)S(1)}, u32[]{:S(2)}, u32[]{:S(2)}) collective-permute-start(bf16[32,768]{1,0:T(8,128)(2,1)S(1)} %pack.1.packed_ref), channel_id=1, source_target_pairs={{0,4},{4,0},{8,12},{12,8},{1,5},{5,1},{9,13},{13,9},{2,6},{6,2},{1... | collective-permute-start | bytes 147464 | tf_op jit(solution)/shard_map/ppermute | solution.py:194
  7.1 4.1 %collective-permute-start.2 = (bf16[32,768]{1,0:T(8,128)(2,1)S(1)}, bf16[32,768]{1,0:T(8,128)(2,1)S(1)}, u32[]{:S(2)}, u32[]{:S(2)}) collective-permute-start(bf16[32,768]{1,0:T(8,128)(2,1)S(1)} %pack.1.packed_ref), channel_id=1, source_target_pairs={{0,2},{1,3},{2,0},{3,1},{4,6},{5,7},{6,4},{7,5},{8,10},{9,11},{10,... | collective-permute-start | bytes 147464 | tf_op jit(solution)/shard_map/ppermute | solution.py:194
  11.2 5.1 %collective-permute-start.6 = (bf16[4,32,768]{2,1,0:T(8,128)(2,1)S(1)}, bf16[4,32,768]{2,1,0:T(8,128)(2,1)S(1)}, u32[]{:S(2)}, u32[]{:S(2)}) collective-permute-start(bf16[4,32,768]{2,1,0:T(8,128)(2,1)S(1)} %pad_maximum_fusion.blocks_ref), channel_id=1, source_target_pairs={{0,1},{1,0},{2,3},{3,2},{4,5},{5,4},{6,7},{7,6},{8,9},{9,8},{10,11... | collective-permute-start | bytes 589832 | tf_op jit(solution)/shard_map/ppermute | solution.py:207
  11.3 3.4 %copy-start.1 = (s32[16,8,2]{0,2,1:T(2,128)S(1)}, s32[16,8,2]{0,2,1:T(2,128)}, u32[]{:S(2)}) copy-start(s32[16,8,2]{0,2,1:T(2,128)} %param.7) | copy-start | bytes 3076
  11.3 7.9 %collective-permute-start.3 = (bf16[2,32,768]{2,1,0:T(8,128)(2,1)S(1)}, bf16[2,32,768]{2,1,0:T(8,128)(2,1)S(1)}, u32[]{:S(2)}, u32[]{:S(2)}) collective-permute-start(bf16[2,32,768]{2,1,0:T(8,128)(2,1)S(1)} %pad_maximum_fusion.1), channel_id=1, source_target_pairs={{0,2},{1,3},{2,0},{3,1},{4,6},{5,7},{6,4},{7,5},{8,10},{9,11},{10,... | collective-permute-start | bytes 294920 | tf_op jit(solution)/shard_map/ppermute | solution.py:194
  12.9 5.0 %collective-permute-start.5 = (bf16[1,32,768]{2,1,0:T(8,128)(2,1)S(1)}, bf16[1,32,768]{2,1,0:T(8,128)(2,1)S(1)}, u32[]{:S(2)}, u32[]{:S(2)}) collective-permute-start(bf16[1,32,768]{2,1,0:T(8,128)(2,1)S(1)} %bitcast.15), channel_id=1, source_target_pairs={{0,4},{4,0},{8,12},{12,8},{1,5},{5,1},{9,13},{13,9},{2,6},{6,2},{1... | collective-permute-start | bytes 147464 | tf_op jit(solution)/shard_map/ppermute | solution.py:194
  13.4 5.9 %collective-permute-start.4 = (bf16[1,32,768]{2,1,0:T(8,128)(2,1)S(1)}, bf16[1,32,768]{2,1,0:T(8,128)(2,1)S(1)}, u32[]{:S(2)}, u32[]{:S(2)}) collective-permute-start(bf16[1,32,768]{2,1,0:T(8,128)(2,1)S(1)} %bitcast.19), channel_id=1, source_target_pairs={{0,12},{4,8},{8,4},{12,0},{1,13},{5,9},{9,5},{13,1},{2,14},{6,10},... | collective-permute-start | bytes 147464 | tf_op jit(solution)/shard_map/ppermute | solution.py:194
  19.3 1.5 %copy-start = (bf16[16,768]{1,0:T(8,128)(2,1)S(1)}, bf16[16,768]{1,0:T(8,128)(2,1)}, u32[]{:S(2)}) copy-start(bf16[16,768]{1,0:T(8,128)(2,1)} %vectors_ref.3) | copy-start | bytes 73732
  19.3 1.5 %copy-start.2 = (f32[768]{0:T(1024)S(1)}, f32[768]{0:T(1024)}, u32[]{:S(2)}) copy-start(f32[768]{0:T(1024)} %degrees_ref.3) | copy-start | bytes 9220
  19.3 1.5 %collective-permute-start.7 = (bf16[4,32,768]{2,1,0:T(8,128)(2,1)S(1)}, bf16[4,32,768]{2,1,0:T(8,128)(2,1)S(1)}, u32[]{:S(2)}, u32[]{:S(2)}) collective-permute-start(bf16[4,32,768]{2,1,0:T(8,128)(2,1)S(1)} %constant_dynamic-update-slice_fusion.blocks_ref), channel_id=1, source_target_pairs={{0,1},{1,0},{2,3},{3,2},{4,5},{5,4},{6,7},{7,6},{8,9},{9,8},{10,11... | collective-permute-start | bytes 589832 | tf_op jit(solution)/shard_map/ppermute | solution.py:207

commit v7 on v5

--- a/solution.py
+++ b/solution.py
@@ -87,10 +87,8 @@
         words.append(jnp.sum(bit).astype(jnp.int32))
 
     count = jnp.int32(0)
-    for step, (rows_back, chips_back, swap) in enumerate(places):
-        from_row = (my_row + n_row - rows_back) % n_row
-        from_col = ((my_col ^ swap) + n_col - 2 * chips_back) % n_col
-        block = from_row * n_col + from_col
+    for step, ((row_bits, chip_bits), swap) in enumerate(places):
+        block = (my_row ^ row_bits) * n_col + (my_col ^ (2 * chip_bits + swap))
         word = words[0]
         for w in range(1, len(words)):
             word = jnp.where(block // 16 == w, words[w], word)
@@ -188,9 +186,10 @@
     ritz_ref[...] = exact(half, vector_inverse, NT)
 
 
-def shifted(x, axis, step):
-    size = lax.axis_size(axis)
-    return lax.ppermute(x, axis, [(i, (i + step) % size) for i in range(size)])
+def sent(x, offset):
+    rows, chips = offset
+    axis, bits = ("row", rows) if rows else ("col", 2 * chips)
+    return lax.ppermute(x, axis, [(i, i ^ bits) for i in range(lax.axis_size(axis))])
 
 
 def swapped(x):
@@ -205,13 +204,8 @@
     sizes = (n_row, n_col)
     vmem = pl.BlockSpec(memory_space=pltpu.VMEM)
 
-    def call(kernel, name, outs, *args, limit=16, tiles=0, where=vmem, **keywords):
+    def call(kernel, name, outs, *args, limit=16, where=vmem, **keywords):
         shapes = [jax.ShapeDtypeStruct(*out) for out in outs]
-        keywords["cost_estimate"] = pl.CostEstimate(
-            flops=tiles * rows * rows * 2 * (4 * ncv + nvec),
-            transcendentals=tiles * rows * rows,
-            bytes_accessed=sum(a.size * a.dtype.itemsize for a in args),
-        )
         return pl.pallas_call(
             kernel,
             out_shape=shapes,
@@ -237,11 +231,13 @@
             pltpu.SemaphoreType.DMA((3,)),
         ],
     )
-    row_blocks = [shifted(packed, "row", s) for s in range(1, n_row)]
-    chip_blocks = [shifted(packed, "col", 2 * t) for t in range(1, n_col // 2)]
-    left, image = call(own_kernel, "own", [((rows, 3 * ncv + 16), jnp.bfloat16), image_type], packed, tiles=1)
-
-    def add(name, places, blocks, image):
+    def start_image(packed):
+        return call(
+            own_kernel, "own", [((rows, 3 * ncv + 16), jnp.bfloat16), image_type], packed
+        )
+
+    def add(name, offsets, swap, blocks, image):
+        places = [(offset, swap) for offset in offsets]
         (image,) = call(
             functools.partial(part_kernel, places, sizes),
             name,
@@ -250,26 +246,47 @@
             left,
             blocks,
             image,
-            tiles=len(places) // 2,
             input_output_aliases={3: 0},
             scratch_shapes=[pltpu.SMEM((len(places) + 1,), jnp.int32)],
         )
         return image
 
-    near = jnp.stack(row_blocks + chip_blocks + [packed])
-    near, image = lax.optimization_barrier((near, image))
-    across = [shifted(near[: n_row - 1], "col", 2 * t) for t in range(1, n_col // 2)]
-    across = across[0] if len(across) == 1 else jnp.concatenate(across)
-    near_places = [(s, 0, 0) for s in range(1, n_row)] + [(0, t, 0) for t in range(1, n_col // 2)]
-    across_places = [(s, t, 0) for t in range(1, n_col // 2) for s in range(1, n_row)]
-    image = add("add_near", near_places, near, image)
-    core = swapped(near)
-    image = add("add_core", [(s, t, 1) for s, t, _ in near_places + [(0, 0, 0)]], core, image)
-    across, image = lax.optimization_barrier((across, image))
-    far = swapped(across)
-    image = add("add_across", across_places, across, image)
+    n_chip = n_col // 2
+    own, row_1, row_2, row_3, chip = (0, 0), (1, 0), (2, 0), (3, 0), (0, 1)
+    if (n_row, n_chip) == (4, 2):
+        from_row_2, from_row_1, from_chip = sent(packed, row_2), sent(packed, row_1), sent(packed, chip)
+        left, image = start_image(packed)
+        (from_row_1, from_chip), image = lax.optimization_barrier(((from_row_1, from_chip), image))
+        chip_row_1 = sent(from_row_1, chip)
+        image = add("add_near", [row_1, chip], 0, jnp.stack([from_row_1, from_chip]), image)
+        from_row_2, image = lax.optimization_barrier((from_row_2, image))
+        chip_row_2 = sent(from_row_2, chip)
+        from_row_3 = sent(from_row_2, row_1)
+        core = swapped(jnp.stack([packed, from_row_1, from_chip, from_row_2, chip_row_1]))
+        image = add("add_next", [row_2, (1, 1)], 0, jnp.stack([from_row_2, chip_row_1]), image)
+        chip_row_2, image = lax.optimization_barrier((chip_row_2, image))
+        chip_row_3 = sent(chip_row_2, row_1)
+        image = add("add_core", [own, row_1, chip, row_2, (1, 1)], 1, core, image)
+        last = [from_row_3, chip_row_2, chip_row_3]
+        last, image = lax.optimization_barrier((last, image))
+        last, last_offsets = jnp.stack(last), [row_3, (2, 1), (3, 1)]
+    else:
+        rows_on = [(r, 0) for r in range(1, n_row)]
+        chips_on = [(0, c) for c in range(1, n_chip)]
+        near = jnp.stack([sent(packed, offset) for offset in rows_on + chips_on] + [packed])
+        left, image = start_image(packed)
+        near, image = lax.optimization_barrier((near, image))
+        last = [sent(near[: n_row - 1], offset) for offset in chips_on]
+        core = swapped(near)
+        image = add("add_near", rows_on + chips_on, 0, near, image)
+        image = add("add_core", rows_on + chips_on + [own], 1, core, image)
+        last, image = lax.optimization_barrier((last, image))
+        last = jnp.concatenate(last)
+        last_offsets = [(r, c) for _, c in chips_on for r, _ in rows_on]
+    far = swapped(last)
+    image = add("add_last", last_offsets, 0, last, image)
     applied, gram = call(
-        functools.partial(last_kernel, [(s, t, 1) for s, t, _ in across_places], sizes),
+        functools.partial(last_kernel, [(offset, 1) for offset in last_offsets], sizes),
         "add_far",
         [((nvec, rows), jnp.float32), ((devices, nvec // 2, 8 * nvec), jnp.float32)],
         table,
@@ -278,10 +295,9 @@
         image,
         vectors,
         degrees,
-        tiles=len(across_places) // 2,
         scratch_shapes=[
             pltpu.VMEM(*image_type),
-            pltpu.SMEM((len(across_places) + 1,), jnp.int32),
+            pltpu.SMEM((len(last_offsets) + 1,), jnp.int32),
         ],
     )
     grams = lax.all_to_all(gram, ("row", "col"), 0, 0)

time: 35.3 us -> 38.6 us (1.093)
  Pallas kernels: 7.86 us -> 12.7 us
  waiting for transfers between devices: 7.08 us -> 3.91 us
  starting transfers between devices: 8.21 us -> 9.34 us
  local copies, waits for them, and re-layouts: 0.11 us -> 0.72 us
    pallas_call x7 -> x8, Pallas kernels: 7.86 us -> 12.7 us  [call(): pl.pallas_call(kernel, out_shape=shapes, in_specs=[where] * len(args), ou...]
    ppermute x5 -> x7, waiting for transfers between devices: 6.43 us -> 3.91 us  [sent(): lax.ppermute(x, axis, [(i, i ^ bits) for i in range(lax.axis_size(axis))])]
    ppermute x5 -> x7, starting transfers between devices: 8.14 us -> 9.27 us  [sent(): lax.ppermute(x, axis, [(i, i ^ bits) for i in range(lax.axis_size(axis))])]
    ppermute x2, waiting for transfers between devices: 0.66 us -> 0.01 us  [swapped(): lax.ppermute(x, 'col', [(i, i ^ 1) for i in range(lax.axis_size('col'))])]
    unnamed x10, local copies, waits for them, and re-layouts: 0.1 us -> 0.72 us
  transfers between devices with their start and end apart: 7 -> 9, of which waited for: 3 -> 2; matrix products, arithmetic and copies ran while one was open for 0% -> 0% of each run, Pallas kernels for 12% -> 23%
where the time goes in v7:
time: 38.6 us
  Pallas kernels  12.7 us (33%)
  blocking collectives  11 us (28%)
  starting transfers between devices  9.34 us (24%)
  waiting for transfers between devices  3.91 us (10%)
  between operations  0.81 us (2%)
  local copies, waits for them, and re-layouts  0.72 us (2%)
    pallas_call x8, Pallas kernels, call(): pl.pallas_call(kernel, out_shape=shapes, in_specs=[where] * len(args), ou...  12.7 us
    all_to_all x1, blocking collectives, per_device(): grams = lax.all_to_all(gram, ('row', 'col'), 0, 0)  11 us
    ppermute x7, starting transfers between devices, sent(): lax.ppermute(x, axis, [(i, i ^ bits) for i in range(lax.axis_size(axis))])  9.27 us
    ppermute x7, waiting for transfers between devices, sent(): lax.ppermute(x, axis, [(i, i ^ bits) for i in range(lax.axis_size(axis))])  3.91 us
  transfers between devices with their start and end apart: 9, of which 2 were waited for; matrix products, arithmetic and copies ran while one was open for 0% of the time, Pallas kernels for 23%

profile of v7, /device:TPU:0, one launch (start us, length us, event | category | flops | bytes accessed | tf_op | source)
XLA Modules:
  0.0 38.6 jit_solution(16616487394976171295)
XLA Ops:
  0.6 0.8 %pack.1.packed_ref = bf16[32,768]{1,0:T(8,128)(2,1)S(1)} custom-call(bf16[16,768]{1,0:T(8,128)(2,1)} %frames_ref.1, bf16[16,768]{1,0:T(8,128)(2,1)} %vectors_ref.3, f32[768]{0:T(1024)} %degrees_ref.3), custom_call_target="tpu_custom_call" | custom-call | tf_op jit(solution)/shard_map/pack/pallas_call | solution.py:209
  1.4 3.1 %collective-permute-start.1 = (bf16[32,768]{1,0:T(8,128)(2,1)S(1)}, bf16[32,768]{1,0:T(8,128)(2,1)S(1)}, u32[]{:S(2)}, u32[]{:S(2)}) collective-permute-start(bf16[32,768]{1,0:T(8,128)(2,1)S(1)} %pack.1.packed_ref), channel_id=1, source_target_pairs={{0,4},{4,0},{8,12},{12,8},{1,5},{5,1},{9,13},{13,9},{2,6},{6,2},{1... | collective-permute-start | bytes 147464 | tf_op jit(solution)/shard_map/ppermute | solution.py:192
  4.5 1.5 %collective-permute-start.2 = (bf16[32,768]{1,0:T(8,128)(2,1)S(1)}, bf16[32,768]{1,0:T(8,128)(2,1)S(1)}, u32[]{:S(2)}, u32[]{:S(2)}) collective-permute-start(bf16[32,768]{1,0:T(8,128)(2,1)S(1)} %pack.1.packed_ref), channel_id=1, source_target_pairs={{0,2},{1,3},{2,0},{3,1},{4,6},{5,7},{6,4},{7,5},{8,10},{9,11},{10,... | collective-permute-start | bytes 147464 | tf_op jit(solution)/shard_map/ppermute | solution.py:192
  6.0 2.6 %collective-permute-start = (bf16[32,768]{1,0:T(8,128)(2,1)S(1)}, bf16[32,768]{1,0:T(8,128)(2,1)S(1)}, u32[]{:S(2)}, u32[]{:S(2)}) collective-permute-start(bf16[32,768]{1,0:T(8,128)(2,1)S(1)} %pack.1.packed_ref), channel_id=1, source_target_pairs={{0,8},{4,12},{8,0},{12,4},{1,9},{5,13},{9,1},{13,5},{2,10},{6,14},... | collective-permute-start | bytes 147464 | tf_op jit(solution)/shard_map/ppermute | solution.py:192
  8.6 0.9 %own.1 = (bf16[768,64]{1,0:T(8,128)(2,1)S(1)}, f32[768,16]{1,0:T(8,128)S(1)}) custom-call(bf16[32,768]{1,0:T(8,128)(2,1)S(1)} %pack.1.packed_ref), custom_call_target="tpu_custom_call" | custom-call | tf_op jit(solution)/shard_map/own/pallas_call | solution.py:209
  9.6 0.0 collective-permute-done.1
  9.6 0.0 collective-permute-done.2
  9.6 0.6 %collective-permute-start.5 = (bf16[32,768]{1,0:T(8,128)(2,1)S(1)}, bf16[32,768]{1,0:T(8,128)(2,1)S(1)}, u32[]{:S(2)}, u32[]{:S(2)}) collective-permute-start(bf16[32,768]{1,0:T(8,128)(2,1)S(1)} %collective-permute-done.1), channel_id=1, source_target_pairs={{0,2},{1,3},{2,0},{3,1},{4,6},{5,7},{6,4},{7,5},{8,10},{9,11},{10,... | collective-permute-start | bytes 147464 | tf_op jit(solution)/shard_map/ppermute | solution.py:192
  10.2 0.7 %copy-done = s32[16,8,2]{0,2,1:T(2,128)S(1)} copy-done((s32[16,8,2]{0,2,1:T(2,128)S(1)}, s32[16,8,2]{0,2,1:T(2,128)}, u32[]{:S(2)}) %copy-start) | copy-done | bytes 1048
  10.9 1.0 %add_near.1.before_ref = f32[768,16]{1,0:T(8,128)S(1)} custom-call(s32[8,2,16]{2,1,0:T(2,128)S(1)} %bitcast.14, bf16[768,64]{1,0:T(8,128)(2,1)S(1)} %get-tuple-element.17.left_ref, bf16[2,32,768]{2,1,0:T(8,128)(2,1)S(1)} %pad_maximum_fusion.1.blocks_ref, f32[768,16]{1,0:T(8,128)S(1)} %get-tuple-element.21.before_ref), custom_call_target="tpu_custom_call", output_to_operand_aliasing={{}: (3, {})} | custom-call | tf_op jit(solution)/shard_map/add_near/pallas_call | solution.py:209
  11.9 0.0 collective-permute-done
  11.9 1.8 %collective-permute-done.5 = bf16[32,768]{1,0:T(8,128)(2,1)S(1)} collective-permute-done((bf16[32,768]{1,0:T(8,128)(2,1)S(1)}, bf16[32,768]{1,0:T(8,128)(2,1)S(1)}, u32[]{:S(2)}, u32[]{:S(2)}) %collective-permute-start.5) | collective-permute-done | bytes 49184 | tf_op jit(solution)/shard_map/ppermute | solution.py:192
  13.7 0.0 collective-permute-start.7
  13.7 0.6 %collective-permute-start.4 = (bf16[32,768]{1,0:T(8,128)(2,1)S(1)}, bf16[32,768]{1,0:T(8,128)(2,1)S(1)}, u32[]{:S(2)}, u32[]{:S(2)}) collective-permute-start(bf16[32,768]{1,0:T(8,128)(2,1)S(1)} %collective-permute-done), channel_id=1, source_target_pairs={{0,2},{1,3},{2,0},{3,1},{4,6},{5,7},{6,4},{7,5},{8,10},{9,11},{10,... | collective-permute-start | bytes 147464 | tf_op jit(solution)/shard_map/ppermute | solution.py:192
  14.3 0.4 %collective-permute-start.3 = (bf16[32,768]{1,0:T(8,128)(2,1)S(1)}, bf16[32,768]{1,0:T(8,128)(2,1)S(1)}, u32[]{:S(2)}, u32[]{:S(2)}) collective-permute-start(bf16[32,768]{1,0:T(8,128)(2,1)S(1)} %collective-permute-done), channel_id=1, source_target_pairs={{0,4},{4,0},{8,12},{12,8},{1,5},{5,1},{9,13},{13,9},{2,6},{6,2},{1... | collective-permute-start | bytes 147464 | tf_op jit(solution)/shard_map/ppermute | solution.py:192
  14.8 1.0 %add_next.1.before_ref = f32[768,16]{1,0:T(8,128)S(1)} custom-call(s32[8,2,16]{2,1,0:T(2,128)S(1)} %bitcast.15, bf16[768,64]{1,0:T(8,128)(2,1)S(1)} %get-tuple-element.17.left_ref, bf16[2,32,768]{2,1,0:T(8,128)(2,1)S(1)} %pad_maximum_fusion.2.blocks_ref, f32[768,16]{1,0:T(8,128)S(1)} %add_near.1.before_ref), custom_call_target="tpu_custom_call", output_to_operand_aliasing={{}: (3, {})} | custom-call | tf_op jit(solution)/shard_map/add_next/pallas_call | solution.py:209
  15.8 2.1 %collective-permute-done.4 = bf16[32,768]{1,0:T(8,128)(2,1)S(1)} collective-permute-done((bf16[32,768]{1,0:T(8,128)(2,1)S(1)}, bf16[32,768]{1,0:T(8,128)(2,1)S(1)}, u32[]{:S(2)}, u32[]{:S(2)}) %collective-permute-start.4) | collective-permute-done | bytes 49184 | tf_op jit(solution)/shard_map/ppermute | solution.py:192
  17.9 0.4 %collective-permute-start.6 = (bf16[32,768]{1,0:T(8,128)(2,1)S(1)}, bf16[32,768]{1,0:T(8,128)(2,1)S(1)}, u32[]{:S(2)}, u32[]{:S(2)}) collective-permute-start(bf16[32,768]{1,0:T(8,128)(2,1)S(1)} %collective-permute-done.4), channel_id=1, source_target_pairs={{0,4},{4,0},{8,12},{12,8},{1,5},{5,1},{9,13},{13,9},{2,6},{6,2},{1... | collective-permute-start | bytes 147464 | tf_op jit(solution)/shard_map/ppermute | solution.py:192
  18.4 0.0 collective-permute-done.7.blocks_ref
  18.4 3.8 %add_core.1.before_ref = f32[768,16]{1,0:T(8,128)S(1)} custom-call(s32[8,2,16]{2,1,0:T(2,128)S(1)} %bitcast.16, bf16[768,64]{1,0:T(8,128)(2,1)S(1)} %get-tuple-element.17.left_ref, bf16[5,32,768]{2,1,0:T(8,128)(2,1)S(1)} %collective-permute-done.7.blocks_ref, f32[768,16]{1,0:T(8,128)S(1)} %add_next.1.before_ref), custom_call_target="tpu_custom_call", output_to_operand_aliasing={{}: (3, {})} | custom-call | tf_op jit(solution)/shard_map/add_core/pallas_call | solution.py:209
  22.1 0.0 collective-permute-done.3
  22.1 0.0 collective-permute-done.6
  22.2 0.0 copy-start.1
  22.2 0.0 copy-start.2
  22.2 0.1 collective-permute-start.8
  22.3 2.4 %add_last.1.before_ref = f32[768,16]{1,0:T(8,128)S(1)} custom-call(s32[8,2,16]{2,1,0:T(2,128)S(1)} %bitcast.17, bf16[768,64]{1,0:T(8,128)(2,1)S(1)} %get-tuple-element.17.left_ref, bf16[3,32,768]{2,1,0:T(8,128)(2,1)S(1)} %pad_maximum_fusion.blocks_ref, f32[768,16]{1,0:T(8,128)S(1)} %add_core.1.before_ref), custom_call_target="tpu_custom_call", output_to_operand_aliasing={{}: (3, {})} | custom-call | tf_op jit(solution)/shard_map/add_last/pallas_call | solution.py:209
  24.7 0.0 collective-permute-done.8.blocks_ref
  24.7 0.0 copy-done.1
  24.7 0.0 copy-done.2
  24.7 1.6 %add_far.1 = (f32[16,768]{1,0:T(8,128)S(1)}, f32[16,8,128]{2,1,0:T(8,128)S(1)}) custom-call(s32[8,2,16]{2,1,0:T(2,128)S(1)} %bitcast.18, bf16[768,64]{1,0:T(8,128)(2,1)S(1)} %get-tuple-element.17.left_ref, bf16[3,32,768]{2,1,0:T(8,128)(2,1)S(1)} %collective-permute-done.8.blocks_ref, f32[768,16]{1,0:T(8,128)S(1)} %add_last.1.before_ref, ...), custom_call_target="tpu_custom_call" | custom-call | tf_op jit(solution)/shard_map/add_far/pallas_call | solution.py:209
  26.3 11.0 %all_to_all.5.grams_ref = f32[16,8,128]{2,1,0:T(8,128)S(1)} all-to-all(f32[16,8,128]{2,1,0:T(8,128)S(1)} %get-tuple-element.30), channel_id=1, replica_groups=mesh['grp'=2,'row'=4,'col'=4] {'row','col'}, dimensions={0} | all-to-all | bytes 131072 | tf_op jit(solution)/shard_map/all_to_all | solution.py:303
  37.3 1.3 %finish.1 = (f32[16,768]{1,0:T(8,128)}, f32[16,16]{1,0:T(8,128)}) custom-call(f32[16,8,128]{2,1,0:T(8,128)S(1)} %all_to_all.5.grams_ref, f32[16,768]{1,0:T(8,128)S(1)} %get-tuple-element.31.applied_ref), custom_call_target="tpu_custom_call" | custom-call | tf_op jit(solution)/shard_map/finish/pallas_call | solution.py:209
  (9 shorter events, 0.1 us)
Async XLA Ops:
  1.4 8.1 %collective-permute-start.1 = (bf16[32,768]{1,0:T(8,128)(2,1)S(1)}, bf16[32,768]{1,0:T(8,128)(2,1)S(1)}, u32[]{:S(2)}, u32[]{:S(2)}) collective-permute-start(bf16[32,768]{1,0:T(8,128)(2,1)S(1)} %pack.1.packed_ref), channel_id=1, source_target_pairs={{0,4},{4,0},{8,12},{12,8},{1,5},{5,1},{9,13},{13,9},{2,6},{6,2},{1... | collective-permute-start | bytes 147464 | tf_op jit(solution)/shard_map/ppermute | solution.py:192
  4.5 5.0 %collective-permute-start.2 = (bf16[32,768]{1,0:T(8,128)(2,1)S(1)}, bf16[32,768]{1,0:T(8,128)(2,1)S(1)}, u32[]{:S(2)}, u32[]{:S(2)}) collective-permute-start(bf16[32,768]{1,0:T(8,128)(2,1)S(1)} %pack.1.packed_ref), channel_id=1, source_target_pairs={{0,2},{1,3},{2,0},{3,1},{4,6},{5,7},{6,4},{7,5},{8,10},{9,11},{10,... | collective-permute-start | bytes 147464 | tf_op jit(solution)/shard_map/ppermute | solution.py:192
  6.0 5.9 %collective-permute-start = (bf16[32,768]{1,0:T(8,128)(2,1)S(1)}, bf16[32,768]{1,0:T(8,128)(2,1)S(1)}, u32[]{:S(2)}, u32[]{:S(2)}) collective-permute-start(bf16[32,768]{1,0:T(8,128)(2,1)S(1)} %pack.1.packed_ref), channel_id=1, source_target_pairs={{0,8},{4,12},{8,0},{12,4},{1,9},{5,13},{9,1},{13,5},{2,10},{6,14},... | collective-permute-start | bytes 147464 | tf_op jit(solution)/shard_map/ppermute | solution.py:192
  9.6 4.2 %collective-permute-start.5 = (bf16[32,768]{1,0:T(8,128)(2,1)S(1)}, bf16[32,768]{1,0:T(8,128)(2,1)S(1)}, u32[]{:S(2)}, u32[]{:S(2)}) collective-permute-start(bf16[32,768]{1,0:T(8,128)(2,1)S(1)} %collective-permute-done.1), channel_id=1, source_target_pairs={{0,2},{1,3},{2,0},{3,1},{4,6},{5,7},{6,4},{7,5},{8,10},{9,11},{10,... | collective-permute-start | bytes 147464 | tf_op jit(solution)/shard_map/ppermute | solution.py:192
  10.2 0.7 %copy-start = (s32[16,8,2]{0,2,1:T(2,128)S(1)}, s32[16,8,2]{0,2,1:T(2,128)}, u32[]{:S(2)}) copy-start(s32[16,8,2]{0,2,1:T(2,128)} %param.7) | copy-start | bytes 3076
  13.7 4.6 %collective-permute-start.7 = (bf16[5,32,768]{2,1,0:T(8,128)(2,1)S(1)}, bf16[5,32,768]{2,1,0:T(8,128)(2,1)S(1)}, u32[]{:S(2)}, u32[]{:S(2)}) collective-permute-start(bf16[5,32,768]{2,1,0:T(8,128)(2,1)S(1)} %constant_dynamic-update-slice_fusion), channel_id=1, source_target_pairs={{0,1},{1,0},{2,3},{3,2},{4,5},{5,4},{6,7},{7,6},{8,9},{9,8},{10,11... | collective-permute-start | bytes 737288 | tf_op jit(solution)/shard_map/ppermute | solution.py:196
  13.7 4.2 %collective-permute-start.4 = (bf16[32,768]{1,0:T(8,128)(2,1)S(1)}, bf16[32,768]{1,0:T(8,128)(2,1)S(1)}, u32[]{:S(2)}, u32[]{:S(2)}) collective-permute-start(bf16[32,768]{1,0:T(8,128)(2,1)S(1)} %collective-permute-done), channel_id=1, source_target_pairs={{0,2},{1,3},{2,0},{3,1},{4,6},{5,7},{6,4},{7,5},{8,10},{9,11},{10,... | collective-permute-start | bytes 147464 | tf_op jit(solution)/shard_map/ppermute | solution.py:192
  14.3 7.8 %collective-permute-start.3 = (bf16[32,768]{1,0:T(8,128)(2,1)S(1)}, bf16[32,768]{1,0:T(8,128)(2,1)S(1)}, u32[]{:S(2)}, u32[]{:S(2)}) collective-permute-start(bf16[32,768]{1,0:T(8,128)(2,1)S(1)} %collective-permute-done), channel_id=1, source_target_pairs={{0,4},{4,0},{8,12},{12,8},{1,5},{5,1},{9,13},{13,9},{2,6},{6,2},{1... | collective-permute-start | bytes 147464 | tf_op jit(solution)/shard_map/ppermute | solution.py:192
  17.9 4.2 %collective-permute-start.6 = (bf16[32,768]{1,0:T(8,128)(2,1)S(1)}, bf16[32,768]{1,0:T(8,128)(2,1)S(1)}, u32[]{:S(2)}, u32[]{:S(2)}) collective-permute-start(bf16[32,768]{1,0:T(8,128)(2,1)S(1)} %collective-permute-done.4), channel_id=1, source_target_pairs={{0,4},{4,0},{8,12},{12,8},{1,5},{5,1},{9,13},{13,9},{2,6},{6,2},{1... | collective-permute-start | bytes 147464 | tf_op jit(solution)/shard_map/ppermute | solution.py:192
  22.2 2.5 %copy-start.1 = (bf16[16,768]{1,0:T(8,128)(2,1)S(1)}, bf16[16,768]{1,0:T(8,128)(2,1)}, u32[]{:S(2)}) copy-start(bf16[16,768]{1,0:T(8,128)(2,1)} %vectors_ref.3) | copy-start | bytes 73732
  22.2 2.5 %copy-start.2 = (f32[768]{0:T(1024)S(1)}, f32[768]{0:T(1024)}, u32[]{:S(2)}) copy-start(f32[768]{0:T(1024)} %degrees_ref.3) | copy-start | bytes 9220
  22.2 2.5 %collective-permute-start.8 = (bf16[3,32,768]{2,1,0:T(8,128)(2,1)S(1)}, bf16[3,32,768]{2,1,0:T(8,128)(2,1)S(1)}, u32[]{:S(2)}, u32[]{:S(2)}) collective-permute-start(bf16[3,32,768]{2,1,0:T(8,128)(2,1)S(1)} %pad_maximum_fusion.blocks_ref), channel_id=1, source_target_pairs={{0,1},{1,0},{2,3},{3,2},{4,5},{5,4},{6,7},{7,6},{8,9},{9,8},{10,11... | collective-permute-start | bytes 442376 | tf_op jit(solution)/shard_map/ppermute | solution.py:196

commit v8 on v7

--- a/solution.py
+++ b/solution.py
@@ -254,22 +254,26 @@
     n_chip = n_col // 2
     own, row_1, row_2, row_3, chip = (0, 0), (1, 0), (2, 0), (3, 0), (0, 1)
     if (n_row, n_chip) == (4, 2):
-        from_row_2, from_row_1, from_chip = sent(packed, row_2), sent(packed, row_1), sent(packed, chip)
+        near = [sent(packed, chip), sent(packed, row_1), sent(packed, row_2)]
+        core_own = swapped(packed)
         left, image = start_image(packed)
-        (from_row_1, from_chip), image = lax.optimization_barrier(((from_row_1, from_chip), image))
-        chip_row_1 = sent(from_row_1, chip)
-        image = add("add_near", [row_1, chip], 0, jnp.stack([from_row_1, from_chip]), image)
-        from_row_2, image = lax.optimization_barrier((from_row_2, image))
-        chip_row_2 = sent(from_row_2, chip)
-        from_row_3 = sent(from_row_2, row_1)
-        core = swapped(jnp.stack([packed, from_row_1, from_chip, from_row_2, chip_row_1]))
-        image = add("add_next", [row_2, (1, 1)], 0, jnp.stack([from_row_2, chip_row_1]), image)
-        chip_row_2, image = lax.optimization_barrier((chip_row_2, image))
-        chip_row_3 = sent(chip_row_2, row_1)
-        image = add("add_core", [own, row_1, chip, row_2, (1, 1)], 1, core, image)
-        last = [from_row_3, chip_row_2, chip_row_3]
+        core_own, image = lax.optimization_barrier((core_own, image))
+        image = add("add_own", [own], 1, core_own[None], image)
+        near, image = lax.optimization_barrier((near, image))
+        across = sent(jnp.stack(near[1:]), chip)
+        from_row_3 = sent(near[2], row_1)
+        near = jnp.stack(near)
+        core = swapped(near)
+        image = add("add_near", [chip, row_1, row_2], 0, near, image)
+        image = add("add_core", [chip, row_1, row_2], 1, core, image)
+        from_row_3, image = lax.optimization_barrier((from_row_3, image))
+        last = sent(from_row_3, chip)
+        across = jnp.concatenate([from_row_3[None], across])
+        core = swapped(across)
+        image = add("add_across", [row_3, (1, 1), (2, 1)], 0, across, image)
+        image = add("add_far", [row_3, (1, 1), (2, 1)], 1, core, image)
         last, image = lax.optimization_barrier((last, image))
-        last, last_offsets = jnp.stack(last), [row_3, (2, 1), (3, 1)]
+        last, last_offsets = last[None], [(3, 1)]
     else:
         rows_on = [(r, 0) for r in range(1, n_row)]
         chips_on = [(0, c) for c in range(1, n_chip)]
@@ -283,21 +287,21 @@
         last, image = lax.optimization_barrier((last, image))
         last = jnp.concatenate(last)
         last_offsets = [(r, c) for _, c in chips_on for r, _ in rows_on]
-    far = swapped(last)
-    image = add("add_last", last_offsets, 0, last, image)
+    places = [(offset, 0) for offset in last_offsets] + [(offset, 1) for offset in last_offsets]
+    last = jnp.concatenate([last, swapped(last)])
     applied, gram = call(
-        functools.partial(last_kernel, [(offset, 1) for offset in last_offsets], sizes),
-        "add_far",
+        functools.partial(last_kernel, places, sizes),
+        "add_last",
         [((nvec, rows), jnp.float32), ((devices, nvec // 2, 8 * nvec), jnp.float32)],
         table,
         left,
-        far,
+        last,
         image,
         vectors,
         degrees,
         scratch_shapes=[
             pltpu.VMEM(*image_type),
-            pltpu.SMEM((len(last_offsets) + 1,), jnp.int32),
+            pltpu.SMEM((len(places) + 1,), jnp.int32),
         ],
     )
     grams = lax.all_to_all(gram, ("row", "col"), 0, 0)

time: 38.6 us -> 36.2 us (0.938)
  Pallas kernels: 12.7 us -> 10.8 us
  blocking collectives: 11 us -> 9.49 us
  waiting for transfers between devices: 3.91 us -> 5.27 us
  local copies, waits for them, and re-layouts: 0.72 us -> 0.01 us
    pallas_call x8 -> x9, Pallas kernels: 12.7 us -> 10.8 us  [call(): pl.pallas_call(kernel, out_shape=shapes, in_specs=[where] * len(args), ou...]
    all_to_all x1, blocking collectives: 11 us -> 9.49 us  [per_device(): grams = lax.all_to_all(gram, ('row', 'col'), 0, 0)]
    ppermute x2 -> x4, waiting for transfers between devices: 0.01 us -> 1.5 us  [swapped(): lax.ppermute(x, 'col', [(i, i ^ 1) for i in range(lax.axis_size('col'))])]
    unnamed x10 -> x6, local copies, waits for them, and re-layouts: 0.72 us -> 0.01 us
    ppermute x2 -> x4, starting transfers between devices: 0.07 us -> 0.66 us  [swapped(): lax.ppermute(x, 'col', [(i, i ^ 1) for i in range(lax.axis_size('col'))])]
    ppermute x7 -> x6, starting transfers between devices: 9.27 us -> 8.81 us  [sent(): lax.ppermute(x, axis, [(i, i ^ bits) for i in range(lax.axis_size(axis))])]
    ppermute x7 -> x6, waiting for transfers between devices: 3.91 us -> 3.77 us  [sent(): lax.ppermute(x, axis, [(i, i ^ bits) for i in range(lax.axis_size(axis))])]
  transfers between devices with their start and end apart: 9 -> 10, of which waited for: 2 -> 4; matrix products, arithmetic and copies ran while one was open for 0% -> 0% of each run, Pallas kernels for 23% -> 20%
where the time goes in v8:
time: 36.2 us; the launch traced here: 35.9 us
  Pallas kernels  10.8 us (30%)
  blocking collectives  9.49 us (26%)
  starting transfers between devices  9.47 us (26%)
  waiting for transfers between devices  5.27 us (15%)
  between operations  0.81 us (2%)
    pallas_call x9, Pallas kernels, call(): pl.pallas_call(kernel, out_shape=shapes, in_specs=[where] * len(args), ou...  10.8 us
    all_to_all x1, blocking collectives, per_device(): grams = lax.all_to_all(gram, ('row', 'col'), 0, 0)  9.49 us
    ppermute x6, starting transfers between devices, sent(): lax.ppermute(x, axis, [(i, i ^ bits) for i in range(lax.axis_size(axis))])  8.81 us
    ppermute x6, waiting for transfers between devices, sent(): lax.ppermute(x, axis, [(i, i ^ bits) for i in range(lax.axis_size(axis))])  3.77 us
    ppermute x4, waiting for transfers between devices, swapped(): lax.ppermute(x, 'col', [(i, i ^ 1) for i in range(lax.axis_size('col'))])  1.5 us
  transfers between devices with their start and end apart: 10, of which 4 were waited for; matrix products, arithmetic and copies ran while one was open for 0% of the time, Pallas kernels for 20%

profile of v8, /device:TPU:0, one launch (start us, length us, event | category | flops | bytes accessed | tf_op | source)
XLA Modules:
  0.0 35.9 jit_solution(5505231644085371436)
XLA Ops:
  0.6 0.8 %pack.1.packed_ref = bf16[32,768]{1,0:T(8,128)(2,1)S(1)} custom-call(bf16[16,768]{1,0:T(8,128)(2,1)} %frames_ref.1, bf16[16,768]{1,0:T(8,128)(2,1)} %vectors_ref.3, f32[768]{0:T(1024)} %degrees_ref.3), custom_call_target="tpu_custom_call" | custom-call | tf_op jit(solution)/shard_map/pack/pallas_call | solution.py:209
  1.4 0.5 %collective-permute-start.3 = (bf16[32,768]{1,0:T(8,128)(2,1)S(1)}, bf16[32,768]{1,0:T(8,128)(2,1)S(1)}, u32[]{:S(2)}, u32[]{:S(2)}) collective-permute-start(bf16[32,768]{1,0:T(8,128)(2,1)S(1)} %pack.1.packed_ref), channel_id=1, source_target_pairs={{0,1},{1,0},{2,3},{3,2},{4,5},{5,4},{6,7},{7,6},{8,9},{9,8},{10,11... | collective-permute-start | bytes 147464 | tf_op jit(solution)/shard_map/ppermute | solution.py:196
  2.0 3.7 %collective-permute-start.2 = (bf16[32,768]{1,0:T(8,128)(2,1)S(1)}, bf16[32,768]{1,0:T(8,128)(2,1)S(1)}, u32[]{:S(2)}, u32[]{:S(2)}) collective-permute-start(bf16[32,768]{1,0:T(8,128)(2,1)S(1)} %pack.1.packed_ref), channel_id=1, source_target_pairs={{0,8},{4,12},{8,0},{12,4},{1,9},{5,13},{9,1},{13,5},{2,10},{6,14},... | collective-permute-start | bytes 147464 | tf_op jit(solution)/shard_map/ppermute | solution.py:192
  5.6 1.6 %collective-permute-start.1 = (bf16[32,768]{1,0:T(8,128)(2,1)S(1)}, bf16[32,768]{1,0:T(8,128)(2,1)S(1)}, u32[]{:S(2)}, u32[]{:S(2)}) collective-permute-start(bf16[32,768]{1,0:T(8,128)(2,1)S(1)} %pack.1.packed_ref), channel_id=1, source_target_pairs={{0,4},{4,0},{8,12},{12,8},{1,5},{5,1},{9,13},{13,9},{2,6},{6,2},{1... | collective-permute-start | bytes 147464 | tf_op jit(solution)/shard_map/ppermute | solution.py:192
  7.2 1.5 %collective-permute-start = (bf16[32,768]{1,0:T(8,128)(2,1)S(1)}, bf16[32,768]{1,0:T(8,128)(2,1)S(1)}, u32[]{:S(2)}, u32[]{:S(2)}) collective-permute-start(bf16[32,768]{1,0:T(8,128)(2,1)S(1)} %pack.1.packed_ref), channel_id=1, source_target_pairs={{0,2},{1,3},{2,0},{3,1},{4,6},{5,7},{6,4},{7,5},{8,10},{9,11},{10,... | collective-permute-start | bytes 147464 | tf_op jit(solution)/shard_map/ppermute | solution.py:192
  8.7 0.9 %own.1 = (bf16[768,64]{1,0:T(8,128)(2,1)S(1)}, f32[768,16]{1,0:T(8,128)S(1)}) custom-call(bf16[32,768]{1,0:T(8,128)(2,1)S(1)} %pack.1.packed_ref), custom_call_target="tpu_custom_call" | custom-call | tf_op jit(solution)/shard_map/own/pallas_call | solution.py:209
  9.6 0.0 collective-permute-done.3
  9.6 0.0 copy-done
  9.7 0.2 add_own.1.before_ref
  9.9 0.0 collective-permute-done.2
  9.9 0.0 collective-permute-done.1
  9.9 1.4 %collective-permute-done = bf16[32,768]{1,0:T(8,128)(2,1)S(1)} collective-permute-done((bf16[32,768]{1,0:T(8,128)(2,1)S(1)}, bf16[32,768]{1,0:T(8,128)(2,1)S(1)}, u32[]{:S(2)}, u32[]{:S(2)}) %collective-permute-start) | collective-permute-done | bytes 49184 | tf_op jit(solution)/shard_map/ppermute | solution.py:192
  11.3 0.1 collective-permute-start.5
  11.4 1.6 %collective-permute-start.7 = (bf16[2,32,768]{2,1,0:T(8,128)(2,1)S(1)}, bf16[2,32,768]{2,1,0:T(8,128)(2,1)S(1)}, u32[]{:S(2)}, u32[]{:S(2)}) collective-permute-start(bf16[2,32,768]{2,1,0:T(8,128)(2,1)S(1)} %pad_maximum_fusion.2), channel_id=1, source_target_pairs={{0,2},{1,3},{2,0},{3,1},{4,6},{5,7},{6,4},{7,5},{8,10},{9,11},{10,... | collective-permute-start | bytes 294920 | tf_op jit(solution)/shard_map/ppermute | solution.py:192
  13.0 0.4 %collective-permute-start.4 = (bf16[32,768]{1,0:T(8,128)(2,1)S(1)}, bf16[32,768]{1,0:T(8,128)(2,1)S(1)}, u32[]{:S(2)}, u32[]{:S(2)}) collective-permute-start(bf16[32,768]{1,0:T(8,128)(2,1)S(1)} %collective-permute-done.2), channel_id=1, source_target_pairs={{0,4},{4,0},{8,12},{12,8},{1,5},{5,1},{9,13},{13,9},{2,6},{6,2},{1... | collective-permute-start | bytes 147464 | tf_op jit(solution)/shard_map/ppermute | solution.py:192
  13.4 2.4 %add_near.1.before_ref = f32[768,16]{1,0:T(8,128)S(1)} custom-call(s32[8,2,16]{2,1,0:T(2,128)S(1)} %bitcast.8, bf16[768,64]{1,0:T(8,128)(2,1)S(1)} %get-tuple-element.16.left_ref, bf16[3,32,768]{2,1,0:T(8,128)(2,1)S(1)} %pad_maximum_fusion.blocks_ref, f32[768,16]{1,0:T(8,128)S(1)} %add_own.1.before_ref), custom_call_target="tpu_custom_call", output_to_operand_aliasing={{}: (3, {})} | custom-call | tf_op jit(solution)/shard_map/add_near/pallas_call | solution.py:209
  15.8 0.0 collective-permute-done.5.blocks_ref
  15.8 2.4 %add_core.1.before_ref = f32[768,16]{1,0:T(8,128)S(1)} custom-call(s32[8,2,16]{2,1,0:T(2,128)S(1)} %bitcast.9, bf16[768,64]{1,0:T(8,128)(2,1)S(1)} %get-tuple-element.16.left_ref, bf16[3,32,768]{2,1,0:T(8,128)(2,1)S(1)} %collective-permute-done.5.blocks_ref, f32[768,16]{1,0:T(8,128)S(1)} %add_near.1.before_ref), custom_call_target="tpu_custom_call", output_to_operand_aliasing={{}: (3, {})} | custom-call | tf_op jit(solution)/shard_map/add_core/pallas_call | solution.py:209
  18.2 0.0 collective-permute-done.4
  18.2 0.0 collective-permute-done.7
  18.2 0.1 collective-permute-start.8
  18.3 0.1 collective-permute-start.6
  18.4 1.0 %add_across.1.before_ref = f32[768,16]{1,0:T(8,128)S(1)} custom-call(s32[8,2,16]{2,1,0:T(2,128)S(1)} %bitcast.10, bf16[768,64]{1,0:T(8,128)(2,1)S(1)} %get-tuple-element.16.left_ref, bf16[3,32,768]{2,1,0:T(8,128)(2,1)S(1)} %pad_maximum_fusion.1.blocks_ref, f32[768,16]{1,0:T(8,128)S(1)} %add_core.1.before_ref), custom_call_target="tpu_custom_call", output_to_operand_aliasing={{}: (3, {})} | custom-call | tf_op jit(solution)/shard_map/add_across/pallas_call | solution.py:209
  19.4 0.3 collective-permute-done.8.blocks_ref
  19.7 0.4 %add_far.1.before_ref = f32[768,16]{1,0:T(8,128)S(1)} custom-call(s32[8,2,16]{2,1,0:T(2,128)S(1)} %bitcast.11, bf16[768,64]{1,0:T(8,128)(2,1)S(1)} %get-tuple-element.16.left_ref, bf16[3,32,768]{2,1,0:T(8,128)(2,1)S(1)} %collective-permute-done.8.blocks_ref, f32[768,16]{1,0:T(8,128)S(1)} %add_across.1.before_ref), custom_call_target="tpu_custom_call", output_to_operand_aliasing={{}: (3, {})} | custom-call | tf_op jit(solution)/shard_map/add_far/pallas_call | solution.py:209
  20.1 2.4 %collective-permute-done.6 = bf16[32,768]{1,0:T(8,128)(2,1)S(1)} collective-permute-done((bf16[32,768]{1,0:T(8,128)(2,1)S(1)}, bf16[32,768]{1,0:T(8,128)(2,1)S(1)}, u32[]{:S(2)}, u32[]{:S(2)}) %collective-permute-start.6) | collective-permute-done | bytes 49184 | tf_op jit(solution)/shard_map/ppermute | solution.py:192
  22.5 0.0 collective-permute-start.9
  22.5 1.2 %collective-permute-done.9 = bf16[1,32,768]{2,1,0:T(8,128)(2,1)S(1)} collective-permute-done((bf16[1,32,768]{2,1,0:T(8,128)(2,1)S(1)}, bf16[1,32,768]{2,1,0:T(8,128)(2,1)S(1)}, u32[]{:S(2)}, u32[]{:S(2)}) %collective-permute-start.9) | collective-permute-done | bytes 49184 | tf_op jit(solution)/shard_map/ppermute | solution.py:196
  23.7 0.0 copy-done.1
  23.7 1.4 %add_last.1 = (f32[16,768]{1,0:T(8,128)S(1)}, f32[16,8,128]{2,1,0:T(8,128)S(1)}) custom-call(s32[8,2,16]{2,1,0:T(2,128)S(1)} %bitcast.12, bf16[768,64]{1,0:T(8,128)(2,1)S(1)} %get-tuple-element.16.left_ref, bf16[2,32,768]{2,1,0:T(8,128)(2,1)S(1)} %pad_maximum_fusion.3.blocks_ref, f32[768,16]{1,0:T(8,128)S(1)} %add_far.1.before_ref, ...), custom_call_target="tpu_custom_call" | custom-call | tf_op jit(solution)/shard_map/add_last/pallas_call | solution.py:209
  25.2 9.5 %all_to_all.5.grams_ref = f32[16,8,128]{2,1,0:T(8,128)S(1)} all-to-all(f32[16,8,128]{2,1,0:T(8,128)S(1)} %get-tuple-element.28), channel_id=1, replica_groups=mesh['grp'=2,'row'=4,'col'=4] {'row','col'}, dimensions={0} | all-to-all | bytes 131072 | tf_op jit(solution)/shard_map/all_to_all | solution.py:307
  34.6 1.3 %finish.1 = (f32[16,768]{1,0:T(8,128)}, f32[16,16]{1,0:T(8,128)}) custom-call(f32[16,8,128]{2,1,0:T(8,128)S(1)} %all_to_all.5.grams_ref, f32[16,768]{1,0:T(8,128)S(1)} %get-tuple-element.29.applied_ref), custom_call_target="tpu_custom_call" | custom-call | tf_op jit(solution)/shard_map/finish/pallas_call | solution.py:209
  (8 shorter events, 0.1 us)
Async XLA Ops:
  1.4 8.2 %collective-permute-start.3 = (bf16[32,768]{1,0:T(8,128)(2,1)S(1)}, bf16[32,768]{1,0:T(8,128)(2,1)S(1)}, u32[]{:S(2)}, u32[]{:S(2)}) collective-permute-start(bf16[32,768]{1,0:T(8,128)(2,1)S(1)} %pack.1.packed_ref), channel_id=1, source_target_pairs={{0,1},{1,0},{2,3},{3,2},{4,5},{5,4},{6,7},{7,6},{8,9},{9,8},{10,11... | collective-permute-start | bytes 147464 | tf_op jit(solution)/shard_map/ppermute | solution.py:196
  2.0 7.9 %collective-permute-start.2 = (bf16[32,768]{1,0:T(8,128)(2,1)S(1)}, bf16[32,768]{1,0:T(8,128)(2,1)S(1)}, u32[]{:S(2)}, u32[]{:S(2)}) collective-permute-start(bf16[32,768]{1,0:T(8,128)(2,1)S(1)} %pack.1.packed_ref), channel_id=1, source_target_pairs={{0,8},{4,12},{8,0},{12,4},{1,9},{5,13},{9,1},{13,5},{2,10},{6,14},... | collective-permute-start | bytes 147464 | tf_op jit(solution)/shard_map/ppermute | solution.py:192
  5.6 4.3 %collective-permute-start.1 = (bf16[32,768]{1,0:T(8,128)(2,1)S(1)}, bf16[32,768]{1,0:T(8,128)(2,1)S(1)}, u32[]{:S(2)}, u32[]{:S(2)}) collective-permute-start(bf16[32,768]{1,0:T(8,128)(2,1)S(1)} %pack.1.packed_ref), channel_id=1, source_target_pairs={{0,4},{4,0},{8,12},{12,8},{1,5},{5,1},{9,13},{13,9},{2,6},{6,2},{1... | collective-permute-start | bytes 147464 | tf_op jit(solution)/shard_map/ppermute | solution.py:192
  7.2 4.1 %collective-permute-start = (bf16[32,768]{1,0:T(8,128)(2,1)S(1)}, bf16[32,768]{1,0:T(8,128)(2,1)S(1)}, u32[]{:S(2)}, u32[]{:S(2)}) collective-permute-start(bf16[32,768]{1,0:T(8,128)(2,1)S(1)} %pack.1.packed_ref), channel_id=1, source_target_pairs={{0,2},{1,3},{2,0},{3,1},{4,6},{5,7},{6,4},{7,5},{8,10},{9,11},{10,... | collective-permute-start | bytes 147464 | tf_op jit(solution)/shard_map/ppermute | solution.py:192
  8.7 1.0 %copy-start = (s32[16,8,2]{0,2,1:T(2,128)S(1)}, s32[16,8,2]{0,2,1:T(2,128)}, u32[]{:S(2)}) copy-start(s32[16,8,2]{0,2,1:T(2,128)} %param.7) | copy-start | bytes 3076
  11.3 4.5 %collective-permute-start.5 = (bf16[3,32,768]{2,1,0:T(8,128)(2,1)S(1)}, bf16[3,32,768]{2,1,0:T(8,128)(2,1)S(1)}, u32[]{:S(2)}, u32[]{:S(2)}) collective-permute-start(bf16[3,32,768]{2,1,0:T(8,128)(2,1)S(1)} %pad_maximum_fusion.blocks_ref), channel_id=1, source_target_pairs={{0,1},{1,0},{2,3},{3,2},{4,5},{5,4},{6,7},{7,6},{8,9},{9,8},{10,11... | collective-permute-start | bytes 442376 | tf_op jit(solution)/shard_map/ppermute | solution.py:196
  11.4 6.8 %collective-permute-start.7 = (bf16[2,32,768]{2,1,0:T(8,128)(2,1)S(1)}, bf16[2,32,768]{2,1,0:T(8,128)(2,1)S(1)}, u32[]{:S(2)}, u32[]{:S(2)}) collective-permute-start(bf16[2,32,768]{2,1,0:T(8,128)(2,1)S(1)} %pad_maximum_fusion.2), channel_id=1, source_target_pairs={{0,2},{1,3},{2,0},{3,1},{4,6},{5,7},{6,4},{7,5},{8,10},{9,11},{10,... | collective-permute-start | bytes 294920 | tf_op jit(solution)/shard_map/ppermute | solution.py:192
  13.0 5.2 %collective-permute-start.4 = (bf16[32,768]{1,0:T(8,128)(2,1)S(1)}, bf16[32,768]{1,0:T(8,128)(2,1)S(1)}, u32[]{:S(2)}, u32[]{:S(2)}) collective-permute-start(bf16[32,768]{1,0:T(8,128)(2,1)S(1)} %collective-permute-done.2), channel_id=1, source_target_pairs={{0,4},{4,0},{8,12},{12,8},{1,5},{5,1},{9,13},{13,9},{2,6},{6,2},{1... | collective-permute-start | bytes 147464 | tf_op jit(solution)/shard_map/ppermute | solution.py:192
  18.2 1.4 %collective-permute-start.8 = (bf16[3,32,768]{2,1,0:T(8,128)(2,1)S(1)}, bf16[3,32,768]{2,1,0:T(8,128)(2,1)S(1)}, u32[]{:S(2)}, u32[]{:S(2)}) collective-permute-start(bf16[3,32,768]{2,1,0:T(8,128)(2,1)S(1)} %pad_maximum_fusion.1.blocks_ref), channel_id=1, source_target_pairs={{0,1},{1,0},{2,3},{3,2},{4,5},{5,4},{6,7},{7,6},{8,9},{9,8},{10,11... | collective-permute-start | bytes 442376 | tf_op jit(solution)/shard_map/ppermute | solution.py:196
  18.3 4.2 %collective-permute-start.6 = (bf16[32,768]{1,0:T(8,128)(2,1)S(1)}, bf16[32,768]{1,0:T(8,128)(2,1)S(1)}, u32[]{:S(2)}, u32[]{:S(2)}) collective-permute-start(bf16[32,768]{1,0:T(8,128)(2,1)S(1)} %collective-permute-done.4), channel_id=1, source_target_pairs={{0,2},{1,3},{2,0},{3,1},{4,6},{5,7},{6,4},{7,5},{8,10},{9,11},{10,... | collective-permute-start | bytes 147464 | tf_op jit(solution)/shard_map/ppermute | solution.py:192
  22.5 1.3 %copy-start.1 = (bf16[16,768]{1,0:T(8,128)(2,1)S(1)}, bf16[16,768]{1,0:T(8,128)(2,1)}, u32[]{:S(2)}) copy-start(bf16[16,768]{1,0:T(8,128)(2,1)} %vectors_ref.3) | copy-start | bytes 73732
  22.5 1.3 %copy-start.2 = (f32[768]{0:T(1024)S(1)}, f32[768]{0:T(1024)}, u32[]{:S(2)}) copy-start(f32[768]{0:T(1024)} %degrees_ref.3) | copy-start | bytes 9220
  22.5 1.2 %collective-permute-start.9 = (bf16[1,32,768]{2,1,0:T(8,128)(2,1)S(1)}, bf16[1,32,768]{2,1,0:T(8,128)(2,1)S(1)}, u32[]{:S(2)}, u32[]{:S(2)}) collective-permute-start(bf16[1,32,768]{2,1,0:T(8,128)(2,1)S(1)} %bitcast.20), channel_id=1, source_target_pairs={{0,1},{1,0},{2,3},{3,2},{4,5},{5,4},{6,7},{7,6},{8,9},{9,8},{10,11... | collective-permute-start | bytes 147464 | tf_op jit(solution)/shard_map/ppermute | solution.py:196

commit v9 on v8

--- a/solution.py
+++ b/solution.py
@@ -68,15 +68,9 @@
     return lax.dot_general(kern, v, NT, preferred_element_type=jnp.float32)
 
 
-def own_kernel(packed_ref, left_ref, image_ref):
-    left_ref[...] = own_side(packed_ref[: packed_ref.shape[0] // 2, :])
-    image_ref[...] = tile_image(left_ref, [packed_ref[...]])
-
-
-def add_blocks(places, sizes, table_ref, left_ref, blocks_ref, image_ref, list_ref):
+def linked_words(sizes, table_ref):
     n_row, n_col = sizes
-    my_row, my_col = lax.axis_index("row"), lax.axis_index("col")
-    me = my_row * n_col + my_col
+    me = lax.axis_index("row") * n_col + lax.axis_index("col")
     first, second = table_ref[:, 0, :], table_ref[:, 1, :]
     other = jnp.where(first == me, second, jnp.where(second == me, first, -1))
     words = []
@@ -85,39 +79,67 @@
         for b in range(16):
             bit = jnp.where(other == start + b, float(1 << b), bit)
         words.append(jnp.sum(bit).astype(jnp.int32))
-
+    return words
+
+
+def is_linked(words, block):
+    word = words[0]
+    for w in range(1, len(words)):
+        word = jnp.where(block // 16 == w, words[w], word)
+    return (word >> (block % 16)) & 1
+
+
+def own_kernel(sizes, table_ref, chip_ref, left_ref, image_ref):
+    left_ref[...] = own_side(chip_ref[0, : chip_ref.shape[1] // 2, :])
+    other = (lax.axis_index("row") * sizes[1] + lax.axis_index("col")) ^ 1
+    linked = is_linked(linked_words(sizes, table_ref), other)
+
+    @pl.when(linked == 1)
+    def _():
+        image_ref[...] = tile_image(left_ref, [chip_ref[0], chip_ref[1]])
+
+    @pl.when(linked == 0)
+    def _():
+        image_ref[...] = tile_image(left_ref, [chip_ref[0]])
+
+
+def add_blocks(places, sizes, table_ref, left_ref, odd_ref, even_ref, image_ref, list_ref):
+    my_row, my_col = lax.axis_index("row"), lax.axis_index("col")
+    odd = my_col % 2 == 1
+    words = linked_words(sizes, table_ref)
     count = jnp.int32(0)
-    for step, ((row_bits, chip_bits), swap) in enumerate(places):
-        block = (my_row ^ row_bits) * n_col + (my_col ^ (2 * chip_bits + swap))
-        word = words[0]
-        for w in range(1, len(words)):
-            word = jnp.where(block // 16 == w, words[w], word)
+    for step, ((row_bits, chip_bits), even) in enumerate(places):
+        owner_col = ((my_col ^ (2 * chip_bits)) | 1) ^ even
         list_ref[count] = step
-        count += (word >> (block % 16)) & 1
+        count += is_linked(words, (my_row ^ row_bits) * sizes[1] + owner_col)
+
+    def block(at):
+        return jnp.where(odd, odd_ref[list_ref[at]], even_ref[list_ref[at]])
 
     def visit(pair, _):
-        blocks = [blocks_ref[list_ref[2 * pair]], blocks_ref[list_ref[2 * pair + 1]]]
-        image_ref[...] += tile_image(left_ref, blocks)
+        image_ref[...] += tile_image(left_ref, [block(2 * pair), block(2 * pair + 1)])
         return 0
 
     lax.fori_loop(0, count // 2, visit, 0)
 
     @pl.when(count % 2 == 1)
     def _():
-        image_ref[...] += tile_image(left_ref, [blocks_ref[list_ref[count - 1]]])
-
-
-def part_kernel(places, sizes, table_ref, left_ref, blocks_ref, before_ref, image_ref, list_ref):
+        image_ref[...] += tile_image(left_ref, [block(count - 1)])
+
+
+def part_kernel(
+    places, sizes, table_ref, left_ref, odd_ref, even_ref, before_ref, image_ref, list_ref
+):
     image_ref[...] = before_ref[...]
-    add_blocks(places, sizes, table_ref, left_ref, blocks_ref, image_ref, list_ref)
+    add_blocks(places, sizes, table_ref, left_ref, odd_ref, even_ref, image_ref, list_ref)
 
 
 def last_kernel(
-    places, sizes, table_ref, left_ref, blocks_ref, before_ref, vectors_ref, degrees_ref,
+    places, sizes, table_ref, left_ref, odd_ref, even_ref, before_ref, vectors_ref, degrees_ref,
     applied_ref, gram_ref, image_ref, list_ref,
 ):
     image_ref[...] = before_ref[...]
-    add_blocks(places, sizes, table_ref, left_ref, blocks_ref, image_ref, list_ref)
+    add_blocks(places, sizes, table_ref, left_ref, odd_ref, even_ref, image_ref, list_ref)
     n = vectors_ref.shape[0]
     applied = image_ref[...].T * lax.rsqrt(degrees_ref[...])[None, :]
     applied_ref[...] = applied
@@ -188,12 +210,21 @@
 
 def sent(x, offset):
     rows, chips = offset
-    axis, bits = ("row", rows) if rows else ("col", 2 * chips)
-    return lax.ppermute(x, axis, [(i, i ^ bits) for i in range(lax.axis_size(axis))])
+    n_row, n_col = lax.axis_size("row"), lax.axis_size("col")
+    pairs = [
+        (r * n_col + c, (r ^ rows) * n_col + (c ^ (2 * chips)))
+        for r in range(n_row)
+        for c in range(1, n_col, 2)
+    ]
+    return lax.ppermute(x, ("row", "col"), pairs)
 
 
 def swapped(x):
     return lax.ppermute(x, "col", [(i, i ^ 1) for i in range(lax.axis_size("col"))])
+
+
+def passed_down(x):
+    return lax.ppermute(x, "col", [(i, i ^ 1) for i in range(1, lax.axis_size("col"), 2)])
 
 
 def per_device(frames, vectors, degrees, tile_table):
@@ -231,13 +262,8 @@
             pltpu.SemaphoreType.DMA((3,)),
         ],
     )
-    def start_image(packed):
-        return call(
-            own_kernel, "own", [((rows, 3 * ncv + 16), jnp.bfloat16), image_type], packed
-        )
-
-    def add(name, offsets, swap, blocks, image):
-        places = [(offset, swap) for offset in offsets]
+    def add(name, offsets, blocks, image):
+        places = [(offset, even) for offset in offsets for even in (0, 1)]
         (image,) = call(
             functools.partial(part_kernel, places, sizes),
             name,
@@ -245,50 +271,48 @@
             table,
             left,
             blocks,
+            passed_down(blocks),
             image,
-            input_output_aliases={3: 0},
+            input_output_aliases={4: 0},
             scratch_shapes=[pltpu.SMEM((len(places) + 1,), jnp.int32)],
         )
         return image
 
     n_chip = n_col // 2
-    own, row_1, row_2, row_3, chip = (0, 0), (1, 0), (2, 0), (3, 0), (0, 1)
+    pair = jnp.stack([packed, swapped(packed)])
+    row_hops = [(r, 0) for r in range(1, n_row)]
+    chip_hops = [(0, c) for c in range(1, n_chip)]
     if (n_row, n_chip) == (4, 2):
-        near = [sent(packed, chip), sent(packed, row_1), sent(packed, row_2)]
-        core_own = swapped(packed)
-        left, image = start_image(packed)
-        core_own, image = lax.optimization_barrier((core_own, image))
-        image = add("add_own", [own], 1, core_own[None], image)
-        near, image = lax.optimization_barrier((near, image))
-        across = sent(jnp.stack(near[1:]), chip)
-        from_row_3 = sent(near[2], row_1)
-        near = jnp.stack(near)
-        core = swapped(near)
-        image = add("add_near", [chip, row_1, row_2], 0, near, image)
-        image = add("add_core", [chip, row_1, row_2], 1, core, image)
+        near_offsets = [(2, 0), (1, 0), (0, 1)]
+    else:
+        near_offsets = chip_hops + row_hops
+    near = [sent(pair, offset) for offset in near_offsets]
+    left, image = call(
+        functools.partial(own_kernel, sizes),
+        "own",
+        [((rows, 3 * ncv + 16), jnp.bfloat16), image_type],
+        table,
+        pair,
+    )
+    near, image = lax.optimization_barrier((near, image))
+    if (n_row, n_chip) == (4, 2):
+        from_chip = sent(jnp.concatenate(near[:2]), (0, 1))
+        from_row_3 = sent(near[0], (1, 0))
+        image = add("add_near", near_offsets, jnp.concatenate(near), image)
         from_row_3, image = lax.optimization_barrier((from_row_3, image))
-        last = sent(from_row_3, chip)
-        across = jnp.concatenate([from_row_3[None], across])
-        core = swapped(across)
-        image = add("add_across", [row_3, (1, 1), (2, 1)], 0, across, image)
-        image = add("add_far", [row_3, (1, 1), (2, 1)], 1, core, image)
+        last = sent(from_row_3, (0, 1))
+        image = add(
+            "add_next", [(3, 0), (2, 1), (1, 1)], jnp.concatenate([from_row_3, from_chip]), image
+        )
         last, image = lax.optimization_barrier((last, image))
-        last, last_offsets = last[None], [(3, 1)]
+        last_offsets = [(3, 1)]
     else:
-        rows_on = [(r, 0) for r in range(1, n_row)]
-        chips_on = [(0, c) for c in range(1, n_chip)]
-        near = jnp.stack([sent(packed, offset) for offset in rows_on + chips_on] + [packed])
-        left, image = start_image(packed)
-        near, image = lax.optimization_barrier((near, image))
-        last = [sent(near[: n_row - 1], offset) for offset in chips_on]
-        core = swapped(near)
-        image = add("add_near", rows_on + chips_on, 0, near, image)
-        image = add("add_core", rows_on + chips_on + [own], 1, core, image)
+        lines = jnp.concatenate(near[len(chip_hops) :])
+        last = jnp.concatenate([sent(lines, hop) for hop in chip_hops])
+        image = add("add_near", near_offsets, jnp.concatenate(near), image)
         last, image = lax.optimization_barrier((last, image))
-        last = jnp.concatenate(last)
-        last_offsets = [(r, c) for _, c in chips_on for r, _ in rows_on]
-    places = [(offset, 0) for offset in last_offsets] + [(offset, 1) for offset in last_offsets]
-    last = jnp.concatenate([last, swapped(last)])
+        last_offsets = [(r, c) for _, c in chip_hops for r, _ in row_hops]
+    places = [(offset, even) for offset in last_offsets for even in (0, 1)]
     applied, gram = call(
         functools.partial(last_kernel, places, sizes),
         "add_last",
@@ -296,6 +320,7 @@
         table,
         left,
         last,
+        passed_down(last),
         image,
         vectors,
         degrees,

time: 36.2 us -> 50.5 us (1.40)
  waiting for transfers between devices: 5.27 us -> 22.2 us
  Pallas kernels: 10.8 us -> 6.99 us
  blocking collectives: 9.49 us -> 11.3 us
  starting transfers between devices: 9.47 us -> 8.4 us
    ppermute x6 -> x9, waiting for transfers between devices: 3.77 us -> 21.3 us  [the longest x3 21.3 us: passed_down(): lax.ppermute(x, 'col', [(i, i ^ 1) for i in range(1, lax.axis_size('col')...]
    pallas_call x9 -> x6, Pallas kernels: 10.8 us -> 6.99 us  [call(): pl.pallas_call(kernel, out_shape=shapes, in_specs=[where] * len(args), ou...]
    all_to_all x1, blocking collectives: 9.49 us -> 11.3 us  [per_device(): grams = lax.all_to_all(gram, ('row', 'col'), 0, 0)]
    ppermute x6 -> x9, starting transfers between devices: 8.81 us -> 7.88 us  [the longest x6 4.01 us: sent(): return lax.ppermute(x, ('row', 'col'), pairs)]
    ppermute x4 -> x1, waiting for transfers between devices: 1.5 us -> 0.88 us  [swapped(): lax.ppermute(x, 'col', [(i, i ^ 1) for i in range(lax.axis_size('col'))])]
  transfers between devices with their start and end apart: 10 -> 10, of which waited for: 4 -> 4; matrix products, arithmetic and copies ran while one was open for 0% -> 0% of each run, Pallas kernels for 20% -> 9%
where the time goes in v9:
time: 50.5 us; the launch traced here: 49.9 us
  waiting for transfers between devices  22.2 us (44%)
  blocking collectives  11.3 us (22%)
  starting transfers between devices  8.4 us (17%)
  Pallas kernels  6.99 us (14%)
  between operations  0.86 us (2%)
    ppermute x3, waiting for transfers between devices, passed_down(): lax.ppermute(x, 'col', [(i, i ^ 1) for i in range(1, lax.axis_size('col')...  21.3 us
    all_to_all x1, blocking collectives, per_device(): grams = lax.all_to_all(gram, ('row', 'col'), 0, 0)  11.3 us
    pallas_call x6, Pallas kernels, call(): pl.pallas_call(kernel, out_shape=shapes, in_specs=[where] * len(args), ou...  6.99 us
    ppermute x6, starting transfers between devices, sent(): return lax.ppermute(x, ('row', 'col'), pairs)  4.01 us
    ppermute x3, starting transfers between devices, passed_down(): lax.ppermute(x, 'col', [(i, i ^ 1) for i in range(1, lax.axis_size('col')...  3.88 us
  transfers between devices with their start and end apart: 10, of which 4 were waited for; matrix products, arithmetic and copies ran while one was open for 0% of the time, Pallas kernels for 9%

profile of v9, /device:TPU:0, one launch (start us, length us, event | category | flops | bytes accessed | tf_op | source)
XLA Modules:
  0.0 49.9 jit_solution(9165479334337382449)
XLA Ops:
  0.6 0.8 %pack.1 = bf16[32,768]{1,0:T(8,128)(2,1)S(1)} custom-call(bf16[16,768]{1,0:T(8,128)(2,1)} %frames_ref.1, bf16[16,768]{1,0:T(8,128)(2,1)} %vectors_ref.3, f32[768]{0:T(1024)} %degrees_ref.3), custom_call_target="tpu_custom_call" | custom-call | tf_op jit(solution)/shard_map/pack/pallas_call | solution.py:240
  1.4 0.5 %collective-permute-start = (bf16[32,768]{1,0:T(8,128)(2,1)S(1)}, bf16[32,768]{1,0:T(8,128)(2,1)S(1)}, u32[]{:S(2)}, u32[]{:S(2)}) collective-permute-start(bf16[32,768]{1,0:T(8,128)(2,1)S(1)} %pack.1), channel_id=1, source_target_pairs={{0,1},{1,0},{2,3},{3,2},{4,5},{5,4},{6,7},{7,6},{8,9},{9,8},{10,11... | collective-permute-start | bytes 147464 | tf_op jit(solution)/shard_map/ppermute | solution.py:223
  2.0 0.9 %collective-permute-done = bf16[32,768]{1,0:T(8,128)(2,1)S(1)} collective-permute-done((bf16[32,768]{1,0:T(8,128)(2,1)S(1)}, bf16[32,768]{1,0:T(8,128)(2,1)S(1)}, u32[]{:S(2)}, u32[]{:S(2)}) %collective-permute-start) | collective-permute-done | bytes 49184 | tf_op jit(solution)/shard_map/ppermute | solution.py:223
  2.9 0.7 %collective-permute-start.1 = (bf16[2,32,768]{2,1,0:T(8,128)(2,1)S(1)}, bf16[2,32,768]{2,1,0:T(8,128)(2,1)S(1)}, u32[]{:S(2)}, u32[]{:S(2)}) collective-permute-start(bf16[2,32,768]{2,1,0:T(8,128)(2,1)S(1)} %pad_maximum_fusion.1.chip_ref), channel_id=1, source_target_pairs={{1,9},{3,11},{5,13},{7,15},{9,1},{11,3},{13,5},{15,7},{17,25},{19,... | collective-permute-start | bytes 294920 | tf_op jit(solution)/shard_map/ppermute | solution.py:219
  3.5 0.7 %collective-permute-start.2 = (bf16[2,32,768]{2,1,0:T(8,128)(2,1)S(1)}, bf16[2,32,768]{2,1,0:T(8,128)(2,1)S(1)}, u32[]{:S(2)}, u32[]{:S(2)}) collective-permute-start(bf16[2,32,768]{2,1,0:T(8,128)(2,1)S(1)} %pad_maximum_fusion.1.chip_ref), channel_id=1, source_target_pairs={{1,5},{3,7},{5,1},{7,3},{9,13},{11,15},{13,9},{15,11},{17,21},{19,... | collective-permute-start | bytes 294920 | tf_op jit(solution)/shard_map/ppermute | solution.py:219
  4.2 0.7 %collective-permute-start.3 = (bf16[2,32,768]{2,1,0:T(8,128)(2,1)S(1)}, bf16[2,32,768]{2,1,0:T(8,128)(2,1)S(1)}, u32[]{:S(2)}, u32[]{:S(2)}) collective-permute-start(bf16[2,32,768]{2,1,0:T(8,128)(2,1)S(1)} %pad_maximum_fusion.1.chip_ref), channel_id=1, source_target_pairs={{1,3},{3,1},{5,7},{7,5},{9,11},{11,9},{13,15},{15,13},{17,19},{19,... | collective-permute-start | bytes 294920 | tf_op jit(solution)/shard_map/ppermute | solution.py:219
  4.9 0.0 copy-done
  4.9 1.0 %own.1 = (bf16[768,64]{1,0:T(8,128)(2,1)S(1)}, f32[768,16]{1,0:T(8,128)S(1)}) custom-call(s32[8,2,16]{2,1,0:T(2,128)S(1)} %bitcast.4, bf16[2,32,768]{2,1,0:T(8,128)(2,1)S(1)} %pad_maximum_fusion.1.chip_ref), custom_call_target="tpu_custom_call" | custom-call | tf_op jit(solution)/shard_map/own/pallas_call | solution.py:240
  5.9 0.0 collective-permute-done.1
  6.0 0.0 collective-permute-done.2
  6.0 0.0 collective-permute-done.3
  6.0 1.3 %collective-permute-start.5 = (bf16[6,32,768]{2,1,0:T(8,128)(2,1)S(1)}, bf16[6,32,768]{2,1,0:T(8,128)(2,1)S(1)}, u32[]{:S(2)}, u32[]{:S(2)}) collective-permute-start(bf16[6,32,768]{2,1,0:T(8,128)(2,1)S(1)} %constant_dynamic-update-slice_fusion.odd_ref), channel_id=1, source_target_pairs={{1,0},{3,2},{5,4},{7,6},{9,8},{11,10},{13,12},{15,14},{17,16},{19,... | collective-permute-start | bytes 884744 | tf_op jit(solution)/shard_map/ppermute | solution.py:227
  7.3 0.7 %collective-permute-start.4 = (bf16[2,32,768]{2,1,0:T(8,128)(2,1)S(1)}, bf16[2,32,768]{2,1,0:T(8,128)(2,1)S(1)}, u32[]{:S(2)}, u32[]{:S(2)}) collective-permute-start(bf16[2,32,768]{2,1,0:T(8,128)(2,1)S(1)} %collective-permute-done.1), channel_id=1, source_target_pairs={{1,5},{3,7},{5,1},{7,3},{9,13},{11,15},{13,9},{15,11},{17,21},{19,... | collective-permute-start | bytes 294920 | tf_op jit(solution)/shard_map/ppermute | solution.py:219
  8.0 0.7 %collective-permute-start.7 = (bf16[4,32,768]{2,1,0:T(8,128)(2,1)S(1)}, bf16[4,32,768]{2,1,0:T(8,128)(2,1)S(1)}, u32[]{:S(2)}, u32[]{:S(2)}) collective-permute-start(bf16[4,32,768]{2,1,0:T(8,128)(2,1)S(1)} %pad_maximum_fusion), channel_id=1, source_target_pairs={{1,3},{3,1},{5,7},{7,5},{9,11},{11,9},{13,15},{15,13},{17,19},{19,... | collective-permute-start | bytes 589832 | tf_op jit(solution)/shard_map/ppermute | solution.py:219
  8.7 10.8 %collective-permute-done.5.even_ref = bf16[6,32,768]{2,1,0:T(8,128)(2,1)S(1)} collective-permute-done((bf16[6,32,768]{2,1,0:T(8,128)(2,1)S(1)}, bf16[6,32,768]{2,1,0:T(8,128)(2,1)S(1)}, u32[]{:S(2)}, u32[]{:S(2)}) %collective-permute-start.5) | collective-permute-done | bytes 294944 | tf_op jit(solution)/shard_map/ppermute | solution.py:227
  19.6 1.6 %add_near.1.before_ref = f32[768,16]{1,0:T(8,128)S(1)} custom-call(s32[8,2,16]{2,1,0:T(2,128)S(1)} %bitcast.5, bf16[768,64]{1,0:T(8,128)(2,1)S(1)} %get-tuple-element.14.left_ref, bf16[6,32,768]{2,1,0:T(8,128)(2,1)S(1)} %constant_dynamic-update-slice_fusion.odd_ref, ...), custom_call_target="tpu_custom_call", output_to_operand_aliasing={{}: (4, {})} | custom-call | tf_op jit(solution)/shard_map/add_near/pallas_call | solution.py:240
  21.2 0.0 collective-permute-done.4
  21.2 0.0 collective-permute-done.7
  21.2 0.0 copy-start.1
  21.2 0.0 copy-start.2
  21.2 1.3 %collective-permute-start.8 = (bf16[6,32,768]{2,1,0:T(8,128)(2,1)S(1)}, bf16[6,32,768]{2,1,0:T(8,128)(2,1)S(1)}, u32[]{:S(2)}, u32[]{:S(2)}) collective-permute-start(bf16[6,32,768]{2,1,0:T(8,128)(2,1)S(1)} %constant_dynamic-update-slice_fusion.3.odd_ref), channel_id=1, source_target_pairs={{1,0},{3,2},{5,4},{7,6},{9,8},{11,10},{13,12},{15,14},{17,16},{19,... | collective-permute-start | bytes 884744 | tf_op jit(solution)/shard_map/ppermute | solution.py:227
  22.5 0.7 %collective-permute-start.6 = (bf16[2,32,768]{2,1,0:T(8,128)(2,1)S(1)}, bf16[2,32,768]{2,1,0:T(8,128)(2,1)S(1)}, u32[]{:S(2)}, u32[]{:S(2)}) collective-permute-start(bf16[2,32,768]{2,1,0:T(8,128)(2,1)S(1)} %collective-permute-done.4), channel_id=1, source_target_pairs={{1,3},{3,1},{5,7},{7,5},{9,11},{11,9},{13,15},{15,13},{17,19},{19,... | collective-permute-start | bytes 294920 | tf_op jit(solution)/shard_map/ppermute | solution.py:219
  23.2 6.8 %collective-permute-done.8.even_ref = bf16[6,32,768]{2,1,0:T(8,128)(2,1)S(1)} collective-permute-done((bf16[6,32,768]{2,1,0:T(8,128)(2,1)S(1)}, bf16[6,32,768]{2,1,0:T(8,128)(2,1)S(1)}, u32[]{:S(2)}, u32[]{:S(2)}) %collective-permute-start.8) | collective-permute-done | bytes 294944 | tf_op jit(solution)/shard_map/ppermute | solution.py:227
  30.0 1.6 %add_next.1.before_ref = f32[768,16]{1,0:T(8,128)S(1)} custom-call(s32[8,2,16]{2,1,0:T(2,128)S(1)} %bitcast.6, bf16[768,64]{1,0:T(8,128)(2,1)S(1)} %get-tuple-element.14.left_ref, bf16[6,32,768]{2,1,0:T(8,128)(2,1)S(1)} %constant_dynamic-update-slice_fusion.3.odd_ref, ...), custom_call_target="tpu_custom_call", output_to_operand_aliasing={{}: (4, {})} | custom-call | tf_op jit(solution)/shard_map/add_next/pallas_call | solution.py:240
  31.6 0.0 collective-permute-done.6.odd_ref
  31.6 1.3 %collective-permute-start.9 = (bf16[2,32,768]{2,1,0:T(8,128)(2,1)S(1)}, bf16[2,32,768]{2,1,0:T(8,128)(2,1)S(1)}, u32[]{:S(2)}, u32[]{:S(2)}) collective-permute-start(bf16[2,32,768]{2,1,0:T(8,128)(2,1)S(1)} %collective-permute-done.6.odd_ref), channel_id=1, source_target_pairs={{1,0},{3,2},{5,4},{7,6},{9,8},{11,10},{13,12},{15,14},{17,16},{19,... | collective-permute-start | bytes 294920 | tf_op jit(solution)/shard_map/ppermute | solution.py:227
  32.9 3.7 %collective-permute-done.9.even_ref = bf16[2,32,768]{2,1,0:T(8,128)(2,1)S(1)} collective-permute-done((bf16[2,32,768]{2,1,0:T(8,128)(2,1)S(1)}, bf16[2,32,768]{2,1,0:T(8,128)(2,1)S(1)}, u32[]{:S(2)}, u32[]{:S(2)}) %collective-permute-start.9) | collective-permute-done | bytes 98336 | tf_op jit(solution)/shard_map/ppermute | solution.py:227
  36.6 0.0 copy-done.1
  36.6 0.0 copy-done.2
  36.6 0.7 %add_last.1 = (f32[16,768]{1,0:T(8,128)S(1)}, f32[16,8,128]{2,1,0:T(8,128)S(1)}) custom-call(s32[8,2,16]{2,1,0:T(2,128)S(1)} %bitcast.7, bf16[768,64]{1,0:T(8,128)(2,1)S(1)} %get-tuple-element.14.left_ref, bf16[2,32,768]{2,1,0:T(8,128)(2,1)S(1)} %collective-permute-done.6.odd_ref, bf16[2,32,768]{2,1,0:T(8,128)(2,1)S(1)} %collective-permute-done.9.even_ref, ...), custom_call_target="tpu_custom_call" | custom-call | tf_op jit(solution)/shard_map/add_last/pallas_call | solution.py:240
  37.3 11.3 %all_to_all.5.grams_ref = f32[16,8,128]{2,1,0:T(8,128)S(1)} all-to-all(f32[16,8,128]{2,1,0:T(8,128)S(1)} %get-tuple-element.24), channel_id=1, replica_groups=mesh['grp'=2,'row'=4,'col'=4] {'row','col'}, dimensions={0} | all-to-all | bytes 131072 | tf_op jit(solution)/shard_map/all_to_all | solution.py:332
  48.6 1.3 %finish.1 = (f32[16,768]{1,0:T(8,128)}, f32[16,16]{1,0:T(8,128)}) custom-call(f32[16,8,128]{2,1,0:T(8,128)S(1)} %all_to_all.5.grams_ref, f32[16,768]{1,0:T(8,128)S(1)} %get-tuple-element.25.applied_ref), custom_call_target="tpu_custom_call" | custom-call | tf_op jit(solution)/shard_map/finish/pallas_call | solution.py:240
  (8 shorter events, 0.1 us)
Async XLA Ops:
  1.4 1.4 %collective-permute-start = (bf16[32,768]{1,0:T(8,128)(2,1)S(1)}, bf16[32,768]{1,0:T(8,128)(2,1)S(1)}, u32[]{:S(2)}, u32[]{:S(2)}) collective-permute-start(bf16[32,768]{1,0:T(8,128)(2,1)S(1)} %pack.1), channel_id=1, source_target_pairs={{0,1},{1,0},{2,3},{3,2},{4,5},{5,4},{6,7},{7,6},{8,9},{9,8},{10,11... | collective-permute-start | bytes 147464 | tf_op jit(solution)/shard_map/ppermute | solution.py:223
  2.8 2.0 %copy-start = (s32[16,8,2]{0,2,1:T(2,128)S(1)}, s32[16,8,2]{0,2,1:T(2,128)}, u32[]{:S(2)}) copy-start(s32[16,8,2]{0,2,1:T(2,128)} %param.7) | copy-start | bytes 3076
  2.9 3.1 %collective-permute-start.1 = (bf16[2,32,768]{2,1,0:T(8,128)(2,1)S(1)}, bf16[2,32,768]{2,1,0:T(8,128)(2,1)S(1)}, u32[]{:S(2)}, u32[]{:S(2)}) collective-permute-start(bf16[2,32,768]{2,1,0:T(8,128)(2,1)S(1)} %pad_maximum_fusion.1.chip_ref), channel_id=1, source_target_pairs={{1,9},{3,11},{5,13},{7,15},{9,1},{11,3},{13,5},{15,7},{17,25},{19,... | collective-permute-start | bytes 294920 | tf_op jit(solution)/shard_map/ppermute | solution.py:219
  3.5 2.4 %collective-permute-start.2 = (bf16[2,32,768]{2,1,0:T(8,128)(2,1)S(1)}, bf16[2,32,768]{2,1,0:T(8,128)(2,1)S(1)}, u32[]{:S(2)}, u32[]{:S(2)}) collective-permute-start(bf16[2,32,768]{2,1,0:T(8,128)(2,1)S(1)} %pad_maximum_fusion.1.chip_ref), channel_id=1, source_target_pairs={{1,5},{3,7},{5,1},{7,3},{9,13},{11,15},{13,9},{15,11},{17,21},{19,... | collective-permute-start | bytes 294920 | tf_op jit(solution)/shard_map/ppermute | solution.py:219
  4.2 1.8 %collective-permute-start.3 = (bf16[2,32,768]{2,1,0:T(8,128)(2,1)S(1)}, bf16[2,32,768]{2,1,0:T(8,128)(2,1)S(1)}, u32[]{:S(2)}, u32[]{:S(2)}) collective-permute-start(bf16[2,32,768]{2,1,0:T(8,128)(2,1)S(1)} %pad_maximum_fusion.1.chip_ref), channel_id=1, source_target_pairs={{1,3},{3,1},{5,7},{7,5},{9,11},{11,9},{13,15},{15,13},{17,19},{19,... | collective-permute-start | bytes 294920 | tf_op jit(solution)/shard_map/ppermute | solution.py:219
  6.0 13.5 %collective-permute-start.5 = (bf16[6,32,768]{2,1,0:T(8,128)(2,1)S(1)}, bf16[6,32,768]{2,1,0:T(8,128)(2,1)S(1)}, u32[]{:S(2)}, u32[]{:S(2)}) collective-permute-start(bf16[6,32,768]{2,1,0:T(8,128)(2,1)S(1)} %constant_dynamic-update-slice_fusion.odd_ref), channel_id=1, source_target_pairs={{1,0},{3,2},{5,4},{7,6},{9,8},{11,10},{13,12},{15,14},{17,16},{19,... | collective-permute-start | bytes 884744 | tf_op jit(solution)/shard_map/ppermute | solution.py:227
  7.3 13.8 %collective-permute-start.4 = (bf16[2,32,768]{2,1,0:T(8,128)(2,1)S(1)}, bf16[2,32,768]{2,1,0:T(8,128)(2,1)S(1)}, u32[]{:S(2)}, u32[]{:S(2)}) collective-permute-start(bf16[2,32,768]{2,1,0:T(8,128)(2,1)S(1)} %collective-permute-done.1), channel_id=1, source_target_pairs={{1,5},{3,7},{5,1},{7,3},{9,13},{11,15},{13,9},{15,11},{17,21},{19,... | collective-permute-start | bytes 294920 | tf_op jit(solution)/shard_map/ppermute | solution.py:219
  8.0 13.2 %collective-permute-start.7 = (bf16[4,32,768]{2,1,0:T(8,128)(2,1)S(1)}, bf16[4,32,768]{2,1,0:T(8,128)(2,1)S(1)}, u32[]{:S(2)}, u32[]{:S(2)}) collective-permute-start(bf16[4,32,768]{2,1,0:T(8,128)(2,1)S(1)} %pad_maximum_fusion), channel_id=1, source_target_pairs={{1,3},{3,1},{5,7},{7,5},{9,11},{11,9},{13,15},{15,13},{17,19},{19,... | collective-permute-start | bytes 589832 | tf_op jit(solution)/shard_map/ppermute | solution.py:219
  21.2 15.4 %copy-start.1 = (bf16[16,768]{1,0:T(8,128)(2,1)S(1)}, bf16[16,768]{1,0:T(8,128)(2,1)}, u32[]{:S(2)}) copy-start(bf16[16,768]{1,0:T(8,128)(2,1)} %vectors_ref.3) | copy-start | bytes 73732
  21.2 15.4 %copy-start.2 = (f32[768]{0:T(1024)S(1)}, f32[768]{0:T(1024)}, u32[]{:S(2)}) copy-start(f32[768]{0:T(1024)} %degrees_ref.3) | copy-start | bytes 9220
  21.2 8.7 %collective-permute-start.8 = (bf16[6,32,768]{2,1,0:T(8,128)(2,1)S(1)}, bf16[6,32,768]{2,1,0:T(8,128)(2,1)S(1)}, u32[]{:S(2)}, u32[]{:S(2)}) collective-permute-start(bf16[6,32,768]{2,1,0:T(8,128)(2,1)S(1)} %constant_dynamic-update-slice_fusion.3.odd_ref), channel_id=1, source_target_pairs={{1,0},{3,2},{5,4},{7,6},{9,8},{11,10},{13,12},{15,14},{17,16},{19,... | collective-permute-start | bytes 884744 | tf_op jit(solution)/shard_map/ppermute | solution.py:227
  22.5 9.1 %collective-permute-start.6 = (bf16[2,32,768]{2,1,0:T(8,128)(2,1)S(1)}, bf16[2,32,768]{2,1,0:T(8,128)(2,1)S(1)}, u32[]{:S(2)}, u32[]{:S(2)}) collective-permute-start(bf16[2,32,768]{2,1,0:T(8,128)(2,1)S(1)} %collective-permute-done.4), channel_id=1, source_target_pairs={{1,3},{3,1},{5,7},{7,5},{9,11},{11,9},{13,15},{15,13},{17,19},{19,... | collective-permute-start | bytes 294920 | tf_op jit(solution)/shard_map/ppermute | solution.py:219
  31.6 5.0 %collective-permute-start.9 = (bf16[2,32,768]{2,1,0:T(8,128)(2,1)S(1)}, bf16[2,32,768]{2,1,0:T(8,128)(2,1)S(1)}, u32[]{:S(2)}, u32[]{:S(2)}) collective-permute-start(bf16[2,32,768]{2,1,0:T(8,128)(2,1)S(1)} %collective-permute-done.6.odd_ref), channel_id=1, source_target_pairs={{1,0},{3,2},{5,4},{7,6},{9,8},{11,10},{13,12},{15,14},{17,16},{19,... | collective-permute-start | bytes 294920 | tf_op jit(solution)/shard_map/ppermute | solution.py:227

commit v10 on v5

--- a/solution.py
+++ b/solution.py
@@ -87,10 +87,8 @@
         words.append(jnp.sum(bit).astype(jnp.int32))
 
     count = jnp.int32(0)
-    for step, (rows_back, chips_back, swap) in enumerate(places):
-        from_row = (my_row + n_row - rows_back) % n_row
-        from_col = ((my_col ^ swap) + n_col - 2 * chips_back) % n_col
-        block = from_row * n_col + from_col
+    for step, (row_bits, col_bits) in enumerate(places):
+        block = (my_row ^ row_bits) * n_col + (my_col ^ col_bits)
         word = words[0]
         for w in range(1, len(words)):
             word = jnp.where(block // 16 == w, words[w], word)
@@ -188,13 +186,27 @@
     ritz_ref[...] = exact(half, vector_inverse, NT)
 
 
-def shifted(x, axis, step):
-    size = lax.axis_size(axis)
-    return lax.ppermute(x, axis, [(i, (i + step) % size) for i in range(size)])
-
-
-def swapped(x):
-    return lax.ppermute(x, "col", [(i, i ^ 1) for i in range(lax.axis_size("col"))])
+def sent(x, hop):
+    n_row, n_col = lax.axis_size("row"), lax.axis_size("col")
+    pairs = [
+        (r * n_col + c, (r ^ hop[0]) * n_col + (c ^ hop[1]))
+        for r in range(n_row)
+        for c in range(n_col)
+    ]
+    return lax.ppermute(x, ("row", "col"), pairs)
+
+
+def beyond(offsets, hop):
+    return [(r ^ hop[0], c ^ hop[1]) for r, c in offsets]
+
+
+def exchange_plan(n_row, n_col):
+    if (n_row, n_col) == (4, 4):
+        direct = [(2, 1), (1, 1), (0, 3)]
+        return direct, [((0, 3), [(1, 1), (2, 1)]), ((3, 1), [(0, 3)]), ((1, 1), [(2, 1)])]
+    lines = [(r, 1) for r in range(1, n_row)]
+    chips = [(0, c) for c in range(3, n_col, 2)]
+    return lines + chips, [(chip, lines) for chip in chips]
 
 
 def per_device(frames, vectors, degrees, tile_table):
@@ -205,13 +217,8 @@
     sizes = (n_row, n_col)
     vmem = pl.BlockSpec(memory_space=pltpu.VMEM)
 
-    def call(kernel, name, outs, *args, limit=16, tiles=0, where=vmem, **keywords):
+    def call(kernel, name, outs, *args, limit=16, where=vmem, **keywords):
         shapes = [jax.ShapeDtypeStruct(*out) for out in outs]
-        keywords["cost_estimate"] = pl.CostEstimate(
-            flops=tiles * rows * rows * 2 * (4 * ncv + nvec),
-            transcendentals=tiles * rows * rows,
-            bytes_accessed=sum(a.size * a.dtype.itemsize for a in args),
-        )
         return pl.pallas_call(
             kernel,
             out_shape=shapes,
@@ -237,9 +244,12 @@
             pltpu.SemaphoreType.DMA((3,)),
         ],
     )
-    row_blocks = [shifted(packed, "row", s) for s in range(1, n_row)]
-    chip_blocks = [shifted(packed, "col", 2 * t) for t in range(1, n_col // 2)]
-    left, image = call(own_kernel, "own", [((rows, 3 * ncv + 16), jnp.bfloat16), image_type], packed, tiles=1)
+    core = (0, 1)
+    direct, forwards = exchange_plan(n_row, n_col)
+    held = {offset: sent(packed, offset) for offset in direct}
+    left, image = call(
+        own_kernel, "own", [((rows, 3 * ncv + 16), jnp.bfloat16), image_type], packed
+    )
 
     def add(name, places, blocks, image):
         (image,) = call(
@@ -250,26 +260,28 @@
             left,
             blocks,
             image,
-            tiles=len(places) // 2,
             input_output_aliases={3: 0},
             scratch_shapes=[pltpu.SMEM((len(places) + 1,), jnp.int32)],
         )
         return image
 
-    near = jnp.stack(row_blocks + chip_blocks + [packed])
-    near, image = lax.optimization_barrier((near, image))
-    across = [shifted(near[: n_row - 1], "col", 2 * t) for t in range(1, n_col // 2)]
-    across = across[0] if len(across) == 1 else jnp.concatenate(across)
-    near_places = [(s, 0, 0) for s in range(1, n_row)] + [(0, t, 0) for t in range(1, n_col // 2)]
-    across_places = [(s, t, 0) for t in range(1, n_col // 2) for s in range(1, n_row)]
-    image = add("add_near", near_places, near, image)
-    core = swapped(near)
-    image = add("add_core", [(s, t, 1) for s, t, _ in near_places + [(0, 0, 0)]], core, image)
+    near = jnp.stack([held[offset] for offset in direct] + [packed])
+    near, image, held = lax.optimization_barrier((near, image, held))
+    across_places = []
+    across = []
+    for hop, offsets in forwards:
+        across.append(sent(jnp.stack([held[offset] for offset in offsets]), hop))
+        across_places += beyond(offsets, hop)
+    other_near = sent(near, core)
+    image = add("add_near", direct, near, image)
+    image = add("add_core", beyond(direct + [(0, 0)], core), other_near, image)
     across, image = lax.optimization_barrier((across, image))
-    far = swapped(across)
+    across = jnp.concatenate(across)
+    far = sent(across, core)
     image = add("add_across", across_places, across, image)
+    far_places = beyond(across_places, core)
     applied, gram = call(
-        functools.partial(last_kernel, [(s, t, 1) for s, t, _ in across_places], sizes),
+        functools.partial(last_kernel, far_places, sizes),
         "add_far",
         [((nvec, rows), jnp.float32), ((devices, nvec // 2, 8 * nvec), jnp.float32)],
         table,
@@ -278,10 +290,9 @@
         image,
         vectors,
         degrees,
-        tiles=len(across_places) // 2,
         scratch_shapes=[
             pltpu.VMEM(*image_type),
-            pltpu.SMEM((len(across_places) + 1,), jnp.int32),
+            pltpu.SMEM((len(far_places) + 1,), jnp.int32),
         ],
     )
     grams = lax.all_to_all(gram, ("row", "col"), 0, 0)

time: 35.3 us -> 35.2 us (level)
  waiting for transfers between devices: 7.08 us -> 3.09 us
  Pallas kernels: 7.86 us -> 10.6 us
  starting transfers between devices: 8.21 us -> 9.81 us
    ppermute x7 -> x8, waiting for transfers between devices: 7.08 us -> 3.09 us  [sent(): return lax.ppermute(x, ('row', 'col'), pairs)]
    pallas_call x7, Pallas kernels: 7.86 us -> 10.6 us  [call(): pl.pallas_call(kernel, out_shape=shapes, in_specs=[where] * len(args), ou...]
    ppermute x7 -> x8, starting transfers between devices: 8.21 us -> 9.81 us  [sent(): return lax.ppermute(x, ('row', 'col'), pairs)]
  transfers between devices with their start and end apart: 7 -> 8, of which waited for: 3 -> 2; matrix products, arithmetic and copies ran while one was open for 0% -> 0% of each run, Pallas kernels for 12% -> 16%
where the time goes in v10:
time: 35.2 us; the launch traced here: 35.3 us
  blocking collectives  10.9 us (31%)
  Pallas kernels  10.6 us (30%)
  starting transfers between devices  9.81 us (28%)
  waiting for transfers between devices  3.09 us (9%)
  between operations  0.77 us (2%)
    all_to_all x1, blocking collectives, per_device(): grams = lax.all_to_all(gram, ('row', 'col'), 0, 0)  10.9 us
    pallas_call x7, Pallas kernels, call(): pl.pallas_call(kernel, out_shape=shapes, in_specs=[where] * len(args), ou...  10.6 us
    ppermute x8, starting transfers between devices, sent(): return lax.ppermute(x, ('row', 'col'), pairs)  9.81 us
    ppermute x8, waiting for transfers between devices, sent(): return lax.ppermute(x, ('row', 'col'), pairs)  3.09 us
  transfers between devices with their start and end apart: 8, of which 2 were waited for; matrix products, arithmetic and copies ran while one was open for 0% of the time, Pallas kernels for 16%

profile of v10, /device:TPU:0, one launch (start us, length us, event | category | flops | bytes accessed | tf_op | source)
XLA Modules:
  0.0 35.3 jit_solution(6981778886760477956)
XLA Ops:
  0.6 0.8 %pack.1.packed_ref = bf16[32,768]{1,0:T(8,128)(2,1)S(1)} custom-call(bf16[16,768]{1,0:T(8,128)(2,1)} %frames_ref.1, bf16[16,768]{1,0:T(8,128)(2,1)} %vectors_ref.3, f32[768]{0:T(1024)} %degrees_ref.3), custom_call_target="tpu_custom_call" | custom-call | tf_op jit(solution)/shard_map/pack/pallas_call | solution.py:222
  1.4 3.5 %collective-permute-start = (bf16[32,768]{1,0:T(8,128)(2,1)S(1)}, bf16[32,768]{1,0:T(8,128)(2,1)S(1)}, u32[]{:S(2)}, u32[]{:S(2)}) collective-permute-start(bf16[32,768]{1,0:T(8,128)(2,1)S(1)} %pack.1.packed_ref), channel_id=1, source_target_pairs={{0,9},{1,8},{2,11},{3,10},{4,13},{5,12},{6,15},{7,14},{8,1},{9,0},... | collective-permute-start | bytes 147464 | tf_op jit(solution)/shard_map/ppermute | solution.py:196
  5.0 1.9 %collective-permute-start.1 = (bf16[32,768]{1,0:T(8,128)(2,1)S(1)}, bf16[32,768]{1,0:T(8,128)(2,1)S(1)}, u32[]{:S(2)}, u32[]{:S(2)}) collective-permute-start(bf16[32,768]{1,0:T(8,128)(2,1)S(1)} %pack.1.packed_ref), channel_id=1, source_target_pairs={{0,5},{1,4},{2,7},{3,6},{4,1},{5,0},{6,3},{7,2},{8,13},{9,12},{10,... | collective-permute-start | bytes 147464 | tf_op jit(solution)/shard_map/ppermute | solution.py:196
  6.8 0.9 %collective-permute-start.2 = (bf16[32,768]{1,0:T(8,128)(2,1)S(1)}, bf16[32,768]{1,0:T(8,128)(2,1)S(1)}, u32[]{:S(2)}, u32[]{:S(2)}) collective-permute-start(bf16[32,768]{1,0:T(8,128)(2,1)S(1)} %pack.1.packed_ref), channel_id=1, source_target_pairs={{0,3},{1,2},{2,1},{3,0},{4,7},{5,6},{6,5},{7,4},{8,11},{9,10},{10,... | collective-permute-start | bytes 147464 | tf_op jit(solution)/shard_map/ppermute | solution.py:196
  7.8 0.9 %own.1 = (bf16[768,64]{1,0:T(8,128)(2,1)S(1)}, f32[768,16]{1,0:T(8,128)S(1)}) custom-call(bf16[32,768]{1,0:T(8,128)(2,1)S(1)} %pack.1.packed_ref), custom_call_target="tpu_custom_call" | custom-call | tf_op jit(solution)/shard_map/own/pallas_call | solution.py:222
  8.7 0.0 collective-permute-done
  8.7 0.0 collective-permute-done.1
  8.7 2.1 %collective-permute-done.2 = bf16[32,768]{1,0:T(8,128)(2,1)S(1)} collective-permute-done((bf16[32,768]{1,0:T(8,128)(2,1)S(1)}, bf16[32,768]{1,0:T(8,128)(2,1)S(1)}, u32[]{:S(2)}, u32[]{:S(2)}) %collective-permute-start.2) | collective-permute-done | bytes 49184 | tf_op jit(solution)/shard_map/ppermute | solution.py:196
  10.9 0.2 collective-permute-start.6
  11.0 0.0 copy-start
  11.1 1.6 %collective-permute-start.3 = (bf16[2,32,768]{2,1,0:T(8,128)(2,1)S(1)}, bf16[2,32,768]{2,1,0:T(8,128)(2,1)S(1)}, u32[]{:S(2)}, u32[]{:S(2)}) collective-permute-start(bf16[2,32,768]{2,1,0:T(8,128)(2,1)S(1)} %pad_maximum_fusion.1), channel_id=1, source_target_pairs={{0,3},{1,2},{2,1},{3,0},{4,7},{5,6},{6,5},{7,4},{8,11},{9,10},{10,... | collective-permute-start | bytes 294920 | tf_op jit(solution)/shard_map/ppermute | solution.py:196
  12.6 0.1 collective-permute-start.5
  12.7 1.2 %collective-permute-start.4 = (bf16[1,32,768]{2,1,0:T(8,128)(2,1)S(1)}, bf16[1,32,768]{2,1,0:T(8,128)(2,1)S(1)}, u32[]{:S(2)}, u32[]{:S(2)}) collective-permute-start(bf16[1,32,768]{2,1,0:T(8,128)(2,1)S(1)} %bitcast.19), channel_id=1, source_target_pairs={{0,13},{1,12},{2,15},{3,14},{4,9},{5,8},{6,11},{7,10},{8,5},{9,4},... | collective-permute-start | bytes 147464 | tf_op jit(solution)/shard_map/ppermute | solution.py:196
  13.9 0.0 copy-done
  13.9 1.6 %add_near.1.before_ref = f32[768,16]{1,0:T(8,128)S(1)} custom-call(s32[8,2,16]{2,1,0:T(2,128)S(1)} %bitcast.9, bf16[768,64]{1,0:T(8,128)(2,1)S(1)} %get-tuple-element.15.left_ref, bf16[4,32,768]{2,1,0:T(8,128)(2,1)S(1)} %pad_maximum_fusion.blocks_ref, f32[768,16]{1,0:T(8,128)S(1)} %get-tuple-element.21.before_ref), custom_call_target="tpu_custom_call", output_to_operand_aliasing={{}: (3, {})} | custom-call | tf_op jit(solution)/shard_map/add_near/pallas_call | solution.py:222
  15.5 0.0 collective-permute-done.6.blocks_ref
  15.6 1.6 %add_core.1.before_ref = f32[768,16]{1,0:T(8,128)S(1)} custom-call(s32[8,2,16]{2,1,0:T(2,128)S(1)} %bitcast.10, bf16[768,64]{1,0:T(8,128)(2,1)S(1)} %get-tuple-element.15.left_ref, bf16[4,32,768]{2,1,0:T(8,128)(2,1)S(1)} %collective-permute-done.6.blocks_ref, f32[768,16]{1,0:T(8,128)S(1)} %add_near.1.before_ref), custom_call_target="tpu_custom_call", output_to_operand_aliasing={{}: (3, {})} | custom-call | tf_op jit(solution)/shard_map/add_core/pallas_call | solution.py:222
  17.2 0.0 collective-permute-done.5
  17.2 1.0 %collective-permute-done.4 = bf16[1,32,768]{2,1,0:T(8,128)(2,1)S(1)} collective-permute-done((bf16[1,32,768]{2,1,0:T(8,128)(2,1)S(1)}, bf16[1,32,768]{2,1,0:T(8,128)(2,1)S(1)}, u32[]{:S(2)}, u32[]{:S(2)}) %collective-permute-start.4) | collective-permute-done | bytes 49184 | tf_op jit(solution)/shard_map/ppermute | solution.py:196
  18.2 0.0 collective-permute-done.3
  18.2 0.0 copy-start.1
  18.2 0.0 copy-start.2
  18.2 0.4 %collective-permute-start.7 = (bf16[4,32,768]{2,1,0:T(8,128)(2,1)S(1)}, bf16[4,32,768]{2,1,0:T(8,128)(2,1)S(1)}, u32[]{:S(2)}, u32[]{:S(2)}) collective-permute-start(bf16[4,32,768]{2,1,0:T(8,128)(2,1)S(1)} %constant_dynamic-update-slice_fusion.blocks_ref), channel_id=1, source_target_pairs={{0,1},{1,0},{2,3},{3,2},{4,5},{5,4},{6,7},{7,6},{8,9},{9,8},{10,11... | collective-permute-start | bytes 589832 | tf_op jit(solution)/shard_map/ppermute | solution.py:196
  18.7 1.6 %add_across.1.before_ref = f32[768,16]{1,0:T(8,128)S(1)} custom-call(s32[8,2,16]{2,1,0:T(2,128)S(1)} %bitcast.11, bf16[768,64]{1,0:T(8,128)(2,1)S(1)} %get-tuple-element.15.left_ref, bf16[4,32,768]{2,1,0:T(8,128)(2,1)S(1)} %constant_dynamic-update-slice_fusion.blocks_ref, f32[768,16]{1,0:T(8,128)S(1)} %add_core.1.before_ref), custom_call_target="tpu_custom_call", output_to_operand_aliasing={{}: (3, {})} | custom-call | tf_op jit(solution)/shard_map/add_across/pallas_call | solution.py:222
  20.3 0.0 collective-permute-done.7.blocks_ref
  20.3 0.0 copy-done.1
  20.3 0.0 copy-done.2
  20.3 2.8 %add_far.1 = (f32[16,768]{1,0:T(8,128)S(1)}, f32[16,8,128]{2,1,0:T(8,128)S(1)}) custom-call(s32[8,2,16]{2,1,0:T(2,128)S(1)} %bitcast.12, bf16[768,64]{1,0:T(8,128)(2,1)S(1)} %get-tuple-element.15.left_ref, bf16[4,32,768]{2,1,0:T(8,128)(2,1)S(1)} %collective-permute-done.7.blocks_ref, f32[768,16]{1,0:T(8,128)S(1)} %add_across.1.before_ref, ...), custom_call_target="tpu_custom_call" | custom-call | tf_op jit(solution)/shard_map/add_far/pallas_call | solution.py:222
  23.1 10.9 %all_to_all.5.grams_ref = f32[16,8,128]{2,1,0:T(8,128)S(1)} all-to-all(f32[16,8,128]{2,1,0:T(8,128)S(1)} %get-tuple-element.26), channel_id=1, replica_groups=mesh['grp'=2,'row'=4,'col'=4] {'row','col'}, dimensions={0} | all-to-all | bytes 131072 | tf_op jit(solution)/shard_map/all_to_all | solution.py:298
  34.0 1.3 %finish.1 = (f32[16,768]{1,0:T(8,128)}, f32[16,16]{1,0:T(8,128)}) custom-call(f32[16,8,128]{2,1,0:T(8,128)S(1)} %all_to_all.5.grams_ref, f32[16,768]{1,0:T(8,128)S(1)} %get-tuple-element.27.applied_ref), custom_call_target="tpu_custom_call" | custom-call | tf_op jit(solution)/shard_map/finish/pallas_call | solution.py:222
  (5 shorter events, 0.1 us)
Async XLA Ops:
  1.4 7.3 %collective-permute-start = (bf16[32,768]{1,0:T(8,128)(2,1)S(1)}, bf16[32,768]{1,0:T(8,128)(2,1)S(1)}, u32[]{:S(2)}, u32[]{:S(2)}) collective-permute-start(bf16[32,768]{1,0:T(8,128)(2,1)S(1)} %pack.1.packed_ref), channel_id=1, source_target_pairs={{0,9},{1,8},{2,11},{3,10},{4,13},{5,12},{6,15},{7,14},{8,1},{9,0},... | collective-permute-start | bytes 147464 | tf_op jit(solution)/shard_map/ppermute | solution.py:196
  5.0 3.7 %collective-permute-start.1 = (bf16[32,768]{1,0:T(8,128)(2,1)S(1)}, bf16[32,768]{1,0:T(8,128)(2,1)S(1)}, u32[]{:S(2)}, u32[]{:S(2)}) collective-permute-start(bf16[32,768]{1,0:T(8,128)(2,1)S(1)} %pack.1.packed_ref), channel_id=1, source_target_pairs={{0,5},{1,4},{2,7},{3,6},{4,1},{5,0},{6,3},{7,2},{8,13},{9,12},{10,... | collective-permute-start | bytes 147464 | tf_op jit(solution)/shard_map/ppermute | solution.py:196
  6.8 4.0 %collective-permute-start.2 = (bf16[32,768]{1,0:T(8,128)(2,1)S(1)}, bf16[32,768]{1,0:T(8,128)(2,1)S(1)}, u32[]{:S(2)}, u32[]{:S(2)}) collective-permute-start(bf16[32,768]{1,0:T(8,128)(2,1)S(1)} %pack.1.packed_ref), channel_id=1, source_target_pairs={{0,3},{1,2},{2,1},{3,0},{4,7},{5,6},{6,5},{7,4},{8,11},{9,10},{10,... | collective-permute-start | bytes 147464 | tf_op jit(solution)/shard_map/ppermute | solution.py:196
  10.9 4.7 %collective-permute-start.6 = (bf16[4,32,768]{2,1,0:T(8,128)(2,1)S(1)}, bf16[4,32,768]{2,1,0:T(8,128)(2,1)S(1)}, u32[]{:S(2)}, u32[]{:S(2)}) collective-permute-start(bf16[4,32,768]{2,1,0:T(8,128)(2,1)S(1)} %pad_maximum_fusion.blocks_ref), channel_id=1, source_target_pairs={{0,1},{1,0},{2,3},{3,2},{4,5},{5,4},{6,7},{7,6},{8,9},{9,8},{10,11... | collective-permute-start | bytes 589832 | tf_op jit(solution)/shard_map/ppermute | solution.py:196
  11.0 2.9 %copy-start = (s32[16,8,2]{0,2,1:T(2,128)S(1)}, s32[16,8,2]{0,2,1:T(2,128)}, u32[]{:S(2)}) copy-start(s32[16,8,2]{0,2,1:T(2,128)} %param.7) | copy-start | bytes 3076
  11.1 7.1 %collective-permute-start.3 = (bf16[2,32,768]{2,1,0:T(8,128)(2,1)S(1)}, bf16[2,32,768]{2,1,0:T(8,128)(2,1)S(1)}, u32[]{:S(2)}, u32[]{:S(2)}) collective-permute-start(bf16[2,32,768]{2,1,0:T(8,128)(2,1)S(1)} %pad_maximum_fusion.1), channel_id=1, source_target_pairs={{0,3},{1,2},{2,1},{3,0},{4,7},{5,6},{6,5},{7,4},{8,11},{9,10},{10,... | collective-permute-start | bytes 294920 | tf_op jit(solution)/shard_map/ppermute | solution.py:196
  12.6 4.5 %collective-permute-start.5 = (bf16[1,32,768]{2,1,0:T(8,128)(2,1)S(1)}, bf16[1,32,768]{2,1,0:T(8,128)(2,1)S(1)}, u32[]{:S(2)}, u32[]{:S(2)}) collective-permute-start(bf16[1,32,768]{2,1,0:T(8,128)(2,1)S(1)} %bitcast.15), channel_id=1, source_target_pairs={{0,5},{1,4},{2,7},{3,6},{4,1},{5,0},{6,3},{7,2},{8,13},{9,12},{10,... | collective-permute-start | bytes 147464 | tf_op jit(solution)/shard_map/ppermute | solution.py:196
  12.7 5.4 %collective-permute-start.4 = (bf16[1,32,768]{2,1,0:T(8,128)(2,1)S(1)}, bf16[1,32,768]{2,1,0:T(8,128)(2,1)S(1)}, u32[]{:S(2)}, u32[]{:S(2)}) collective-permute-start(bf16[1,32,768]{2,1,0:T(8,128)(2,1)S(1)} %bitcast.19), channel_id=1, source_target_pairs={{0,13},{1,12},{2,15},{3,14},{4,9},{5,8},{6,11},{7,10},{8,5},{9,4},... | collective-permute-start | bytes 147464 | tf_op jit(solution)/shard_map/ppermute | solution.py:196
  18.2 2.1 %copy-start.1 = (bf16[16,768]{1,0:T(8,128)(2,1)S(1)}, bf16[16,768]{1,0:T(8,128)(2,1)}, u32[]{:S(2)}) copy-start(bf16[16,768]{1,0:T(8,128)(2,1)} %vectors_ref.3) | copy-start | bytes 73732
  18.2 2.1 %copy-start.2 = (f32[768]{0:T(1024)S(1)}, f32[768]{0:T(1024)}, u32[]{:S(2)}) copy-start(f32[768]{0:T(1024)} %degrees_ref.3) | copy-start | bytes 9220
  18.2 2.0 %collective-permute-start.7 = (bf16[4,32,768]{2,1,0:T(8,128)(2,1)S(1)}, bf16[4,32,768]{2,1,0:T(8,128)(2,1)S(1)}, u32[]{:S(2)}, u32[]{:S(2)}) collective-permute-start(bf16[4,32,768]{2,1,0:T(8,128)(2,1)S(1)} %constant_dynamic-update-slice_fusion.blocks_ref), channel_id=1, source_target_pairs={{0,1},{1,0},{2,3},{3,2},{4,5},{5,4},{6,7},{7,6},{8,9},{9,8},{10,11... | collective-permute-start | bytes 589832 | tf_op jit(solution)/shard_map/ppermute | solution.py:196

commit v11 on v10

--- a/solution.py
+++ b/solution.py
@@ -203,7 +203,7 @@
 def exchange_plan(n_row, n_col):
     if (n_row, n_col) == (4, 4):
         direct = [(2, 1), (1, 1), (0, 3)]
-        return direct, [((0, 3), [(1, 1), (2, 1)]), ((3, 1), [(0, 3)]), ((1, 1), [(2, 1)])]
+        return direct, [((0, 3), [(2, 1)]), ((1, 1), [(2, 1), (0, 3)]), ((1, 3), [(2, 1)])]
     lines = [(r, 1) for r in range(1, n_row)]
     chips = [(0, c) for c in range(3, n_col, 2)]
     return lines + chips, [(chip, lines) for chip in chips]
@@ -273,8 +273,8 @@
         across.append(sent(jnp.stack([held[offset] for offset in offsets]), hop))
         across_places += beyond(offsets, hop)
     other_near = sent(near, core)
-    image = add("add_near", direct, near, image)
-    image = add("add_core", beyond(direct + [(0, 0)], core), other_near, image)
+    near = jnp.concatenate([near[:-1], other_near])
+    image = add("add_near", direct + beyond(direct + [(0, 0)], core), near, image)
     across, image = lax.optimization_barrier((across, image))
     across = jnp.concatenate(across)
     far = sent(across, core)

time: 35.2 us -> 35.6 us (1.011); the launches traced: 35.3 us -> 35.2 us
  Pallas kernels: 10.6 us -> 9.15 us
  local copies, waits for them, and re-layouts: 0.04 us -> 0.7 us
    pallas_call x7 -> x6, Pallas kernels: 10.6 us -> 9.15 us  [call(): pl.pallas_call(kernel, out_shape=shapes, in_specs=[where] * len(args), ou...]
    unnamed x8, local copies, waits for them, and re-layouts: 0.03 us -> 0.69 us
  transfers between devices with their start and end apart: 8 -> 8, of which waited for: 2 -> 3; matrix products, arithmetic and copies ran while one was open for 0% -> 0% of each run, Pallas kernels for 16% -> 12%
where the time goes in v11:
time: 35.6 us; the launch traced here: 35.2 us
  blocking collectives  11.2 us (31%)
  starting transfers between devices  10.1 us (28%)
  Pallas kernels  9.15 us (26%)
  waiting for transfers between devices  3.3 us (9%)
  between operations  0.74 us (2%)
  local copies, waits for them, and re-layouts  0.7 us (2%)
    all_to_all x1, blocking collectives, per_device(): grams = lax.all_to_all(gram, ('row', 'col'), 0, 0)  11.2 us
    ppermute x8, starting transfers between devices, sent(): return lax.ppermute(x, ('row', 'col'), pairs)  10.1 us
    pallas_call x6, Pallas kernels, call(): pl.pallas_call(kernel, out_shape=shapes, in_specs=[where] * len(args), ou...  9.15 us
    ppermute x8, waiting for transfers between devices, sent(): return lax.ppermute(x, ('row', 'col'), pairs)  3.3 us
  transfers between devices with their start and end apart: 8, of which 3 were waited for; matrix products, arithmetic and copies ran while one was open for 0% of the time, Pallas kernels for 12%

profile of v11, /device:TPU:0, one launch (start us, length us, event | category | flops | bytes accessed | tf_op | source)
XLA Modules:
  0.0 35.2 jit_solution(17192434657360232958)
XLA Ops:
  0.6 0.8 %pack.1.packed_ref = bf16[32,768]{1,0:T(8,128)(2,1)S(1)} custom-call(bf16[16,768]{1,0:T(8,128)(2,1)} %frames_ref.1, bf16[16,768]{1,0:T(8,128)(2,1)} %vectors_ref.3, f32[768]{0:T(1024)} %degrees_ref.3), custom_call_target="tpu_custom_call" | custom-call | tf_op jit(solution)/shard_map/pack/pallas_call | solution.py:222
  1.4 3.5 %collective-permute-start = (bf16[32,768]{1,0:T(8,128)(2,1)S(1)}, bf16[32,768]{1,0:T(8,128)(2,1)S(1)}, u32[]{:S(2)}, u32[]{:S(2)}) collective-permute-start(bf16[32,768]{1,0:T(8,128)(2,1)S(1)} %pack.1.packed_ref), channel_id=1, source_target_pairs={{0,9},{1,8},{2,11},{3,10},{4,13},{5,12},{6,15},{7,14},{8,1},{9,0},... | collective-permute-start | bytes 147464 | tf_op jit(solution)/shard_map/ppermute | solution.py:196
  5.0 1.9 %collective-permute-start.1 = (bf16[32,768]{1,0:T(8,128)(2,1)S(1)}, bf16[32,768]{1,0:T(8,128)(2,1)S(1)}, u32[]{:S(2)}, u32[]{:S(2)}) collective-permute-start(bf16[32,768]{1,0:T(8,128)(2,1)S(1)} %pack.1.packed_ref), channel_id=1, source_target_pairs={{0,5},{1,4},{2,7},{3,6},{4,1},{5,0},{6,3},{7,2},{8,13},{9,12},{10,... | collective-permute-start | bytes 147464 | tf_op jit(solution)/shard_map/ppermute | solution.py:196
  6.8 0.9 %collective-permute-start.2 = (bf16[32,768]{1,0:T(8,128)(2,1)S(1)}, bf16[32,768]{1,0:T(8,128)(2,1)S(1)}, u32[]{:S(2)}, u32[]{:S(2)}) collective-permute-start(bf16[32,768]{1,0:T(8,128)(2,1)S(1)} %pack.1.packed_ref), channel_id=1, source_target_pairs={{0,3},{1,2},{2,1},{3,0},{4,7},{5,6},{6,5},{7,4},{8,11},{9,10},{10,... | collective-permute-start | bytes 147464 | tf_op jit(solution)/shard_map/ppermute | solution.py:196
  7.8 0.9 %own.1 = (bf16[768,64]{1,0:T(8,128)(2,1)S(1)}, f32[768,16]{1,0:T(8,128)S(1)}) custom-call(bf16[32,768]{1,0:T(8,128)(2,1)S(1)} %pack.1.packed_ref), custom_call_target="tpu_custom_call" | custom-call | tf_op jit(solution)/shard_map/own/pallas_call | solution.py:222
  8.7 0.0 collective-permute-done
  8.7 0.0 collective-permute-done.1
  8.7 2.1 %collective-permute-done.2 = bf16[32,768]{1,0:T(8,128)(2,1)S(1)} collective-permute-done((bf16[32,768]{1,0:T(8,128)(2,1)S(1)}, bf16[32,768]{1,0:T(8,128)(2,1)S(1)}, u32[]{:S(2)}, u32[]{:S(2)}) %collective-permute-start.2) | collective-permute-done | bytes 49184 | tf_op jit(solution)/shard_map/ppermute | solution.py:196
  10.9 0.2 collective-permute-start.6
  11.1 1.6 %collective-permute-start.3 = (bf16[1,32,768]{2,1,0:T(8,128)(2,1)S(1)}, bf16[1,32,768]{2,1,0:T(8,128)(2,1)S(1)}, u32[]{:S(2)}, u32[]{:S(2)}) collective-permute-start(bf16[1,32,768]{2,1,0:T(8,128)(2,1)S(1)} %bitcast.12), channel_id=1, source_target_pairs={{0,3},{1,2},{2,1},{3,0},{4,7},{5,6},{6,5},{7,4},{8,11},{9,10},{10,... | collective-permute-start | bytes 147464 | tf_op jit(solution)/shard_map/ppermute | solution.py:196
  12.6 0.1 collective-permute-start.5
  12.7 1.7 %collective-permute-start.4 = (bf16[2,32,768]{2,1,0:T(8,128)(2,1)S(1)}, bf16[2,32,768]{2,1,0:T(8,128)(2,1)S(1)}, u32[]{:S(2)}, u32[]{:S(2)}) collective-permute-start(bf16[2,32,768]{2,1,0:T(8,128)(2,1)S(1)} %pad_maximum_fusion.2), channel_id=1, source_target_pairs={{0,5},{1,4},{2,7},{3,6},{4,1},{5,0},{6,3},{7,2},{8,13},{9,12},{10,... | collective-permute-start | bytes 294920 | tf_op jit(solution)/shard_map/ppermute | solution.py:196
  14.4 0.0 collective-permute-done.6
  14.4 0.0 copy-start.1
  14.5 0.7 %copy-done.1 = s32[16,8,2]{0,2,1:T(2,128)S(1)} copy-done((s32[16,8,2]{0,2,1:T(2,128)S(1)}, s32[16,8,2]{0,2,1:T(2,128)}, u32[]{:S(2)}) %copy-start.1) | copy-done | bytes 1048
  15.1 2.4 %add_near.1.before_ref = f32[768,16]{1,0:T(8,128)S(1)} custom-call(s32[8,2,16]{2,1,0:T(2,128)S(1)} %bitcast.8, bf16[768,64]{1,0:T(8,128)(2,1)S(1)} %get-tuple-element.14.left_ref, bf16[7,32,768]{2,1,0:T(8,128)(2,1)S(1)} %pad_maximum_fusion.blocks_ref, f32[768,16]{1,0:T(8,128)S(1)} %get-tuple-element.19.before_ref), custom_call_target="tpu_custom_call", output_to_operand_aliasing={{}: (3, {})} | custom-call | tf_op jit(solution)/shard_map/add_near/pallas_call | solution.py:222
  17.5 0.0 collective-permute-done.3
  17.5 0.0 collective-permute-done.5
  17.5 0.9 %collective-permute-done.4 = bf16[2,32,768]{2,1,0:T(8,128)(2,1)S(1)} collective-permute-done((bf16[2,32,768]{2,1,0:T(8,128)(2,1)S(1)}, bf16[2,32,768]{2,1,0:T(8,128)(2,1)S(1)}, u32[]{:S(2)}, u32[]{:S(2)}) %collective-permute-start.4) | collective-permute-done | bytes 98336 | tf_op jit(solution)/shard_map/ppermute | solution.py:196
  18.4 0.0 copy-start
  18.4 0.0 copy-start.2
  18.5 0.2 collective-permute-start.7
  18.7 1.0 %add_across.1.before_ref = f32[768,16]{1,0:T(8,128)S(1)} custom-call(s32[8,2,16]{2,1,0:T(2,128)S(1)} %bitcast.9, bf16[768,64]{1,0:T(8,128)(2,1)S(1)} %get-tuple-element.14.left_ref, bf16[4,32,768]{2,1,0:T(8,128)(2,1)S(1)} %constant_dynamic-update-slice_fusion.blocks_ref, f32[768,16]{1,0:T(8,128)S(1)} %add_near.1.before_ref), custom_call_target="tpu_custom_call", output_to_operand_aliasing={{}: (3, {})} | custom-call | tf_op jit(solution)/shard_map/add_across/pallas_call | solution.py:222
  19.7 0.3 collective-permute-done.7.blocks_ref
  20.0 0.0 copy-done
  20.0 0.0 copy-done.2
  20.0 2.8 %add_far.1 = (f32[16,768]{1,0:T(8,128)S(1)}, f32[16,8,128]{2,1,0:T(8,128)S(1)}) custom-call(s32[8,2,16]{2,1,0:T(2,128)S(1)} %bitcast.10, bf16[768,64]{1,0:T(8,128)(2,1)S(1)} %get-tuple-element.14.left_ref, bf16[4,32,768]{2,1,0:T(8,128)(2,1)S(1)} %collective-permute-done.7.blocks_ref, f32[768,16]{1,0:T(8,128)S(1)} %add_across.1.before_ref, ...), custom_call_target="tpu_custom_call" | custom-call | tf_op jit(solution)/shard_map/add_far/pallas_call | solution.py:222
  22.8 11.2 %all_to_all.5.grams_ref = f32[16,8,128]{2,1,0:T(8,128)S(1)} all-to-all(f32[16,8,128]{2,1,0:T(8,128)S(1)} %get-tuple-element.24), channel_id=1, replica_groups=mesh['grp'=2,'row'=4,'col'=4] {'row','col'}, dimensions={0} | all-to-all | bytes 131072 | tf_op jit(solution)/shard_map/all_to_all | solution.py:298
  33.9 1.3 %finish.1 = (f32[16,768]{1,0:T(8,128)}, f32[16,16]{1,0:T(8,128)}) custom-call(f32[16,8,128]{2,1,0:T(8,128)S(1)} %all_to_all.5.grams_ref, f32[16,768]{1,0:T(8,128)S(1)} %get-tuple-element.25.applied_ref), custom_call_target="tpu_custom_call" | custom-call | tf_op jit(solution)/shard_map/finish/pallas_call | solution.py:222
  (7 shorter events, 0.1 us)
Async XLA Ops:
  1.4 7.3 %collective-permute-start = (bf16[32,768]{1,0:T(8,128)(2,1)S(1)}, bf16[32,768]{1,0:T(8,128)(2,1)S(1)}, u32[]{:S(2)}, u32[]{:S(2)}) collective-permute-start(bf16[32,768]{1,0:T(8,128)(2,1)S(1)} %pack.1.packed_ref), channel_id=1, source_target_pairs={{0,9},{1,8},{2,11},{3,10},{4,13},{5,12},{6,15},{7,14},{8,1},{9,0},... | collective-permute-start | bytes 147464 | tf_op jit(solution)/shard_map/ppermute | solution.py:196
  5.0 3.7 %collective-permute-start.1 = (bf16[32,768]{1,0:T(8,128)(2,1)S(1)}, bf16[32,768]{1,0:T(8,128)(2,1)S(1)}, u32[]{:S(2)}, u32[]{:S(2)}) collective-permute-start(bf16[32,768]{1,0:T(8,128)(2,1)S(1)} %pack.1.packed_ref), channel_id=1, source_target_pairs={{0,5},{1,4},{2,7},{3,6},{4,1},{5,0},{6,3},{7,2},{8,13},{9,12},{10,... | collective-permute-start | bytes 147464 | tf_op jit(solution)/shard_map/ppermute | solution.py:196
  6.8 4.0 %collective-permute-start.2 = (bf16[32,768]{1,0:T(8,128)(2,1)S(1)}, bf16[32,768]{1,0:T(8,128)(2,1)S(1)}, u32[]{:S(2)}, u32[]{:S(2)}) collective-permute-start(bf16[32,768]{1,0:T(8,128)(2,1)S(1)} %pack.1.packed_ref), channel_id=1, source_target_pairs={{0,3},{1,2},{2,1},{3,0},{4,7},{5,6},{6,5},{7,4},{8,11},{9,10},{10,... | collective-permute-start | bytes 147464 | tf_op jit(solution)/shard_map/ppermute | solution.py:196
  10.9 3.6 %collective-permute-start.6 = (bf16[4,32,768]{2,1,0:T(8,128)(2,1)S(1)}, bf16[4,32,768]{2,1,0:T(8,128)(2,1)S(1)}, u32[]{:S(2)}, u32[]{:S(2)}) collective-permute-start(bf16[4,32,768]{2,1,0:T(8,128)(2,1)S(1)} %pad_maximum_fusion.1), channel_id=1, source_target_pairs={{0,1},{1,0},{2,3},{3,2},{4,5},{5,4},{6,7},{7,6},{8,9},{9,8},{10,11... | collective-permute-start | bytes 589832 | tf_op jit(solution)/shard_map/ppermute | solution.py:196
  11.1 6.4 %collective-permute-start.3 = (bf16[1,32,768]{2,1,0:T(8,128)(2,1)S(1)}, bf16[1,32,768]{2,1,0:T(8,128)(2,1)S(1)}, u32[]{:S(2)}, u32[]{:S(2)}) collective-permute-start(bf16[1,32,768]{2,1,0:T(8,128)(2,1)S(1)} %bitcast.12), channel_id=1, source_target_pairs={{0,3},{1,2},{2,1},{3,0},{4,7},{5,6},{6,5},{7,4},{8,11},{9,10},{10,... | collective-permute-start | bytes 147464 | tf_op jit(solution)/shard_map/ppermute | solution.py:196
  12.6 4.9 %collective-permute-start.5 = (bf16[1,32,768]{2,1,0:T(8,128)(2,1)S(1)}, bf16[1,32,768]{2,1,0:T(8,128)(2,1)S(1)}, u32[]{:S(2)}, u32[]{:S(2)}) collective-permute-start(bf16[1,32,768]{2,1,0:T(8,128)(2,1)S(1)} %bitcast.13), channel_id=1, source_target_pairs={{0,7},{1,6},{2,5},{3,4},{4,3},{5,2},{6,1},{7,0},{8,15},{9,14},{10,... | collective-permute-start | bytes 147464 | tf_op jit(solution)/shard_map/ppermute | solution.py:196
  12.7 5.7 %collective-permute-start.4 = (bf16[2,32,768]{2,1,0:T(8,128)(2,1)S(1)}, bf16[2,32,768]{2,1,0:T(8,128)(2,1)S(1)}, u32[]{:S(2)}, u32[]{:S(2)}) collective-permute-start(bf16[2,32,768]{2,1,0:T(8,128)(2,1)S(1)} %pad_maximum_fusion.2), channel_id=1, source_target_pairs={{0,5},{1,4},{2,7},{3,6},{4,1},{5,0},{6,3},{7,2},{8,13},{9,12},{10,... | collective-permute-start | bytes 294920 | tf_op jit(solution)/shard_map/ppermute | solution.py:196
  14.4 0.7 %copy-start.1 = (s32[16,8,2]{0,2,1:T(2,128)S(1)}, s32[16,8,2]{0,2,1:T(2,128)}, u32[]{:S(2)}) copy-start(s32[16,8,2]{0,2,1:T(2,128)} %param.7) | copy-start | bytes 3076
  18.4 1.5 %copy-start = (bf16[16,768]{1,0:T(8,128)(2,1)S(1)}, bf16[16,768]{1,0:T(8,128)(2,1)}, u32[]{:S(2)}) copy-start(bf16[16,768]{1,0:T(8,128)(2,1)} %vectors_ref.3) | copy-start | bytes 73732
  18.4 1.5 %copy-start.2 = (f32[768]{0:T(1024)S(1)}, f32[768]{0:T(1024)}, u32[]{:S(2)}) copy-start(f32[768]{0:T(1024)} %degrees_ref.3) | copy-start | bytes 9220
  18.5 1.5 %collective-permute-start.7 = (bf16[4,32,768]{2,1,0:T(8,128)(2,1)S(1)}, bf16[4,32,768]{2,1,0:T(8,128)(2,1)S(1)}, u32[]{:S(2)}, u32[]{:S(2)}) collective-permute-start(bf16[4,32,768]{2,1,0:T(8,128)(2,1)S(1)} %constant_dynamic-update-slice_fusion.blocks_ref), channel_id=1, source_target_pairs={{0,1},{1,0},{2,3},{3,2},{4,5},{5,4},{6,7},{7,6},{8,9},{9,8},{10,11... | collective-permute-start | bytes 589832 | tf_op jit(solution)/shard_map/ppermute | solution.py:196

commit v12 on v10

--- a/solution.py
+++ b/solution.py
@@ -22,20 +22,26 @@
     return high, mid, low
 
 
-def pack_kernel(frames_ref, vectors_ref, degrees_ref, out_ref, raw_ref, degree_ref, sems):
+def pack_kernel(
+    frames_ref, vectors_in, degrees_ref, table_in,
+    packed_ref, vectors_ref, root_ref, table_ref, degree_ref, sems,
+):
     ncv = frames_ref.shape[0]
     copies = [
-        pltpu.make_async_copy(vectors_ref, raw_ref, sems.at[0]),
+        pltpu.make_async_copy(vectors_in, vectors_ref, sems.at[0]),
         pltpu.make_async_copy(degrees_ref, degree_ref, sems.at[1]),
-        pltpu.make_async_copy(frames_ref, out_ref.at[pl.ds(0, ncv)], sems.at[2]),
+        pltpu.make_async_copy(frames_ref, packed_ref.at[pl.ds(0, ncv)], sems.at[2]),
+        pltpu.make_async_copy(table_in, table_ref, sems.at[3]),
     ]
     for copy in copies:
         copy.start()
     copies[0].wait()
     copies[1].wait()
     root = lax.rsqrt(degree_ref[...])[None, :]
-    out_ref[ncv:, :] = (raw_ref[...].astype(jnp.float32) * root).astype(jnp.bfloat16)
+    root_ref[...] = root
+    packed_ref[ncv:, :] = (vectors_ref[...].astype(jnp.float32) * root).astype(jnp.bfloat16)
     copies[2].wait()
+    copies[3].wait()
 
 
 def edge_rows(square, ones_first):
@@ -56,24 +62,28 @@
     return jnp.concatenate([high, mid, low, edge], axis=0).T.astype(jnp.bfloat16)
 
 
-def tile_image(left_ref, blocks):
+def tile_image(left_ref, kern_ref, blocks):
     both = blocks[0] if len(blocks) == 1 else jnp.concatenate(blocks, axis=1)
     ncv = both.shape[0] // 2
     x, v = both[:ncv, :], both[ncv:, :]
     wide = x.astype(jnp.float32)
     edge = edge_rows(jnp.sum(wide * wide, axis=0, keepdims=True), False).astype(jnp.bfloat16)
     right = jnp.concatenate([x, x, x, edge], axis=0)
-    power = jnp.dot(left_ref[...], right, preferred_element_type=jnp.float32)
-    kern = jnp.exp2(power).astype(jnp.bfloat16)
-    return lax.dot_general(kern, v, NT, preferred_element_type=jnp.float32)
-
-
-def own_kernel(packed_ref, left_ref, image_ref):
+    chunk, total = 256, right.shape[1]
+    for start in range(0, total, chunk):
+        power = jnp.dot(
+            left_ref[...], right[:, start : start + chunk], preferred_element_type=jnp.float32
+        )
+        kern_ref[:, start : start + chunk] = jnp.exp2(power).astype(jnp.bfloat16)
+    return lax.dot_general(kern_ref[:, :total], v, NT, preferred_element_type=jnp.float32)
+
+
+def own_kernel(packed_ref, left_ref, image_ref, kern_ref):
     left_ref[...] = own_side(packed_ref[: packed_ref.shape[0] // 2, :])
-    image_ref[...] = tile_image(left_ref, [packed_ref[...]])
-
-
-def add_blocks(places, sizes, table_ref, left_ref, blocks_ref, image_ref, list_ref):
+    image_ref[...] = tile_image(left_ref, kern_ref, [packed_ref[...]])
+
+
+def add_blocks(places, sizes, table_ref, left_ref, blocks_ref, image_ref, list_ref, kern_ref):
     n_row, n_col = sizes
     my_row, my_col = lax.axis_index("row"), lax.axis_index("col")
     me = my_row * n_col + my_col
@@ -97,29 +107,31 @@
 
     def visit(pair, _):
         blocks = [blocks_ref[list_ref[2 * pair]], blocks_ref[list_ref[2 * pair + 1]]]
-        image_ref[...] += tile_image(left_ref, blocks)
+        image_ref[...] += tile_image(left_ref, kern_ref, blocks)
         return 0
 
     lax.fori_loop(0, count // 2, visit, 0)
 
     @pl.when(count % 2 == 1)
     def _():
-        image_ref[...] += tile_image(left_ref, [blocks_ref[list_ref[count - 1]]])
-
-
-def part_kernel(places, sizes, table_ref, left_ref, blocks_ref, before_ref, image_ref, list_ref):
-    image_ref[...] = before_ref[...]
-    add_blocks(places, sizes, table_ref, left_ref, blocks_ref, image_ref, list_ref)
-
-
-def last_kernel(
-    places, sizes, table_ref, left_ref, blocks_ref, before_ref, vectors_ref, degrees_ref,
-    applied_ref, gram_ref, image_ref, list_ref,
+        image_ref[...] += tile_image(left_ref, kern_ref, [blocks_ref[list_ref[count - 1]]])
+
+
+def part_kernel(
+    places, sizes, table_ref, left_ref, blocks_ref, before_ref, image_ref, list_ref, kern_ref
 ):
     image_ref[...] = before_ref[...]
-    add_blocks(places, sizes, table_ref, left_ref, blocks_ref, image_ref, list_ref)
+    add_blocks(places, sizes, table_ref, left_ref, blocks_ref, image_ref, list_ref, kern_ref)
+
+
+def last_kernel(
+    places, sizes, table_ref, left_ref, blocks_ref, before_ref, vectors_ref, root_ref,
+    applied_ref, gram_ref, image_ref, list_ref, kern_ref,
+):
+    image_ref[...] = before_ref[...]
+    add_blocks(places, sizes, table_ref, left_ref, blocks_ref, image_ref, list_ref, kern_ref)
     n = vectors_ref.shape[0]
-    applied = image_ref[...].T * lax.rsqrt(degrees_ref[...])[None, :]
+    applied = image_ref[...].T * root_ref[...]
     applied_ref[...] = applied
     both = jnp.concatenate([applied, vectors_ref[...].astype(jnp.float32)], axis=0)
     gram = lax.dot_general(
@@ -202,11 +214,11 @@
 
 def exchange_plan(n_row, n_col):
     if (n_row, n_col) == (4, 4):
-        direct = [(2, 1), (1, 1), (0, 3)]
+        direct = [(0, 3), (2, 1), (1, 1)]
         return direct, [((0, 3), [(1, 1), (2, 1)]), ((3, 1), [(0, 3)]), ((1, 1), [(2, 1)])]
     lines = [(r, 1) for r in range(1, n_row)]
     chips = [(0, c) for c in range(3, n_col, 2)]
-    return lines + chips, [(chip, lines) for chip in chips]
+    return chips + lines, [(chip, lines) for chip in chips]
 
 
 def per_device(frames, vectors, degrees, tile_table):
@@ -229,26 +241,38 @@
             **keywords,
         )(*args)
 
+    image_type = ((rows, nvec), jnp.float32)
+    kern_scratch = pltpu.VMEM((rows, 2 * rows), jnp.bfloat16)
+
     table = tile_table.transpose(1, 2, 0)
-    image_type = ((rows, nvec), jnp.float32)
-
-    (packed,) = call(
+    packed, vectors, root, table = call(
         pack_kernel,
         "pack",
-        [((ncv + nvec, rows), jnp.bfloat16)],
-        *(pltpu.with_memory_space_constraint(x, pltpu.HBM) for x in (frames, vectors, degrees)),
+        [
+            ((ncv + nvec, rows), jnp.bfloat16),
+            (vectors.shape, vectors.dtype),
+            ((1, rows), jnp.float32),
+            (table.shape, table.dtype),
+        ],
+        *(
+            pltpu.with_memory_space_constraint(x, pltpu.HBM)
+            for x in (frames, vectors, degrees, table)
+        ),
         where=pl.BlockSpec(memory_space=pltpu.HBM),
         scratch_shapes=[
-            pltpu.VMEM(vectors.shape, vectors.dtype),
             pltpu.VMEM(degrees.shape, degrees.dtype),
-            pltpu.SemaphoreType.DMA((3,)),
+            pltpu.SemaphoreType.DMA((4,)),
         ],
     )
     core = (0, 1)
     direct, forwards = exchange_plan(n_row, n_col)
     held = {offset: sent(packed, offset) for offset in direct}
     left, image = call(
-        own_kernel, "own", [((rows, 3 * ncv + 16), jnp.bfloat16), image_type], packed
+        own_kernel,
+        "own",
+        [((rows, 3 * ncv + 16), jnp.bfloat16), image_type],
+        packed,
+        scratch_shapes=[kern_scratch],
     )
 
     def add(name, places, blocks, image):
@@ -261,20 +285,23 @@
             blocks,
             image,
             input_output_aliases={3: 0},
-            scratch_shapes=[pltpu.SMEM((len(places) + 1,), jnp.int32)],
+            scratch_shapes=[pltpu.SMEM((len(places) + 1,), jnp.int32), kern_scratch],
         )
         return image
 
-    near = jnp.stack([held[offset] for offset in direct] + [packed])
-    near, image, held = lax.optimization_barrier((near, image, held))
+    early, others = direct[0], direct[1:]
+    held[early], image = lax.optimization_barrier((held[early], image))
+    image = add("add_first", [early], held[early][None], image)
+    rest, image = lax.optimization_barrier(([held[offset] for offset in others], image))
+    held.update(zip(others, rest))
     across_places = []
     across = []
     for hop, offsets in forwards:
         across.append(sent(jnp.stack([held[offset] for offset in offsets]), hop))
         across_places += beyond(offsets, hop)
-    other_near = sent(near, core)
-    image = add("add_near", direct, near, image)
-    image = add("add_core", beyond(direct + [(0, 0)], core), other_near, image)
+    other_near = sent(jnp.stack([packed] + [held[offset] for offset in direct]), core)
+    near = jnp.concatenate([jnp.stack([held[offset] for offset in others]), other_near])
+    image = add("add_near", others + beyond([(0, 0)] + direct, core), near, image)
     across, image = lax.optimization_barrier((across, image))
     across = jnp.concatenate(across)
     far = sent(across, core)
@@ -289,10 +316,11 @@
         far,
         image,
         vectors,
-        degrees,
+        root,
         scratch_shapes=[
             pltpu.VMEM(*image_type),
             pltpu.SMEM((len(far_places) + 1,), jnp.int32),
+            kern_scratch,
         ],
     )
     grams = lax.all_to_all(gram, ("row", "col"), 0, 0)

time: 35.2 us -> 35.3 us (level)
  Pallas kernels: 10.6 us -> 9.28 us
  waiting for transfers between devices: 3.09 us -> 4.31 us
  blocking collectives: 10.9 us -> 11.6 us
    pallas_call x7, Pallas kernels: 10.6 us -> 9.28 us  [call(): pl.pallas_call(kernel, out_shape=shapes, in_specs=[where] * len(args), ou...]
    ppermute x8, waiting for transfers between devices: 3.09 us -> 4.31 us  [sent(): return lax.ppermute(x, ('row', 'col'), pairs)]
    all_to_all x1, blocking collectives: 10.9 us -> 11.6 us  [per_device(): grams = lax.all_to_all(gram, ('row', 'col'), 0, 0)]
  transfers between devices with their start and end apart: 8 -> 8, of which waited for: 2 -> 2; matrix products, arithmetic and copies ran while one was open for 0% -> 0% of each run, Pallas kernels for 16% -> 15%
where the time goes in v12:
time: 35.3 us; the launch traced here: 35.6 us
  blocking collectives  11.6 us (33%)
  starting transfers between devices  9.65 us (27%)
  Pallas kernels  9.28 us (26%)
  waiting for transfers between devices  4.31 us (12%)
  between operations  0.74 us (2%)
    all_to_all x1, blocking collectives, per_device(): grams = lax.all_to_all(gram, ('row', 'col'), 0, 0)  11.6 us
    ppermute x8, starting transfers between devices, sent(): return lax.ppermute(x, ('row', 'col'), pairs)  9.65 us
    pallas_call x7, Pallas kernels, call(): pl.pallas_call(kernel, out_shape=shapes, in_specs=[where] * len(args), ou...  9.28 us
    ppermute x8, waiting for transfers between devices, sent(): return lax.ppermute(x, ('row', 'col'), pairs)  4.31 us
  transfers between devices with their start and end apart: 8, of which 2 were waited for; matrix products, arithmetic and copies ran while one was open for 0% of the time, Pallas kernels for 15%

profile of v12, /device:TPU:0, one launch (start us, length us, event | category | flops | bytes accessed | tf_op | source)
XLA Modules:
  0.0 35.6 jit_solution(513846348638010116)
XLA Ops:
  0.6 0.8 %pack.1 = (bf16[32,768]{1,0:T(8,128)(2,1)S(1)}, bf16[16,768]{1,0:T(8,128)(2,1)S(1)}, f32[1,768]{1,0:T(1,128)S(1)}, s32[8,2,16]{2,1,0:T(2,128)S(1)}) custom-call(bf16[16,768]{1,0:T(8,128)(2,1)} %frames_ref.1, bf16[16,768]{1,0:T(8,128)(2,1)} %vectors_in.1, f32[768]{0:T(1024)} %degrees_ref.1, s32[8,2,16]{2,1,0:T(2,128)} %bitcast.16), custom_call_target="tpu_custom_call" | custom-call | tf_op jit(solution)/shard_map/pack/pallas_call | solution.py:234
  1.4 2.4 %collective-permute-start.2 = (bf16[32,768]{1,0:T(8,128)(2,1)S(1)}, bf16[32,768]{1,0:T(8,128)(2,1)S(1)}, u32[]{:S(2)}, u32[]{:S(2)}) collective-permute-start(bf16[32,768]{1,0:T(8,128)(2,1)S(1)} %get-tuple-element.20.packed_ref), channel_id=1, source_target_pairs={{0,3},{1,2},{2,1},{3,0},{4,7},{5,6},{6,5},{7,4},{8,11},{9,10},{10,... | collective-permute-start | bytes 147464 | tf_op jit(solution)/shard_map/ppermute | solution.py:208
  3.9 2.9 %collective-permute-start = (bf16[32,768]{1,0:T(8,128)(2,1)S(1)}, bf16[32,768]{1,0:T(8,128)(2,1)S(1)}, u32[]{:S(2)}, u32[]{:S(2)}) collective-permute-start(bf16[32,768]{1,0:T(8,128)(2,1)S(1)} %get-tuple-element.20.packed_ref), channel_id=1, source_target_pairs={{0,9},{1,8},{2,11},{3,10},{4,13},{5,12},{6,15},{7,14},{8,1},{9,0},... | collective-permute-start | bytes 147464 | tf_op jit(solution)/shard_map/ppermute | solution.py:208
  6.8 1.0 %collective-permute-start.1 = (bf16[32,768]{1,0:T(8,128)(2,1)S(1)}, bf16[32,768]{1,0:T(8,128)(2,1)S(1)}, u32[]{:S(2)}, u32[]{:S(2)}) collective-permute-start(bf16[32,768]{1,0:T(8,128)(2,1)S(1)} %get-tuple-element.20.packed_ref), channel_id=1, source_target_pairs={{0,5},{1,4},{2,7},{3,6},{4,1},{5,0},{6,3},{7,2},{8,13},{9,12},{10,... | collective-permute-start | bytes 147464 | tf_op jit(solution)/shard_map/ppermute | solution.py:208
  7.8 0.9 %own.1 = (bf16[768,64]{1,0:T(8,128)(2,1)S(1)}, f32[768,16]{1,0:T(8,128)S(1)}) custom-call(bf16[32,768]{1,0:T(8,128)(2,1)S(1)} %get-tuple-element.20.packed_ref), custom_call_target="tpu_custom_call" | custom-call | tf_op jit(solution)/shard_map/own/pallas_call | solution.py:234
  8.7 0.0 collective-permute-done.2
  8.7 0.2 add_first.1.before_ref
  9.0 0.0 collective-permute-done
  9.0 1.7 %collective-permute-done.1 = bf16[32,768]{1,0:T(8,128)(2,1)S(1)} collective-permute-done((bf16[32,768]{1,0:T(8,128)(2,1)S(1)}, bf16[32,768]{1,0:T(8,128)(2,1)S(1)}, u32[]{:S(2)}, u32[]{:S(2)}) %collective-permute-start.1) | collective-permute-done | bytes 49184 | tf_op jit(solution)/shard_map/ppermute | solution.py:208
  10.7 0.2 collective-permute-start.6
  10.9 1.7 %collective-permute-start.5 = (bf16[1,32,768]{2,1,0:T(8,128)(2,1)S(1)}, bf16[1,32,768]{2,1,0:T(8,128)(2,1)S(1)}, u32[]{:S(2)}, u32[]{:S(2)}) collective-permute-start(bf16[1,32,768]{2,1,0:T(8,128)(2,1)S(1)} %bitcast.10), channel_id=1, source_target_pairs={{0,5},{1,4},{2,7},{3,6},{4,1},{5,0},{6,3},{7,2},{8,13},{9,12},{10,... | collective-permute-start | bytes 147464 | tf_op jit(solution)/shard_map/ppermute | solution.py:208
  12.6 0.7 %collective-permute-start.4 = (bf16[1,32,768]{2,1,0:T(8,128)(2,1)S(1)}, bf16[1,32,768]{2,1,0:T(8,128)(2,1)S(1)}, u32[]{:S(2)}, u32[]{:S(2)}) collective-permute-start(bf16[1,32,768]{2,1,0:T(8,128)(2,1)S(1)} %bitcast.7), channel_id=1, source_target_pairs={{0,13},{1,12},{2,15},{3,14},{4,9},{5,8},{6,11},{7,10},{8,5},{9,4},... | collective-permute-start | bytes 147464 | tf_op jit(solution)/shard_map/ppermute | solution.py:208
  13.3 0.6 %collective-permute-start.3 = (bf16[2,32,768]{2,1,0:T(8,128)(2,1)S(1)}, bf16[2,32,768]{2,1,0:T(8,128)(2,1)S(1)}, u32[]{:S(2)}, u32[]{:S(2)}) collective-permute-start(bf16[2,32,768]{2,1,0:T(8,128)(2,1)S(1)} %pad_maximum_fusion.2), channel_id=1, source_target_pairs={{0,3},{1,2},{2,1},{3,0},{4,7},{5,6},{6,5},{7,4},{8,11},{9,10},{10,... | collective-permute-start | bytes 294920 | tf_op jit(solution)/shard_map/ppermute | solution.py:208
  13.8 0.0 collective-permute-done.6
  13.9 1.6 %add_near.1.before_ref = f32[768,16]{1,0:T(8,128)S(1)} custom-call(s32[8,2,16]{2,1,0:T(2,128)S(1)} %get-tuple-element.19.table_ref, bf16[768,64]{1,0:T(8,128)(2,1)S(1)} %get-tuple-element.21.left_ref, bf16[6,32,768]{2,1,0:T(8,128)(2,1)S(1)} %pad_maximum_fusion.blocks_ref, f32[768,16]{1,0:T(8,128)S(1)} %add_first.1.before_ref), custom_call_target="tpu_custom_call", output_to_operand_aliasing={{}: (3, {})} | custom-call | tf_op jit(solution)/shard_map/add_near/pallas_call | solution.py:234
  15.5 0.0 collective-permute-done.5
  15.5 2.6 %collective-permute-done.4 = bf16[1,32,768]{2,1,0:T(8,128)(2,1)S(1)} collective-permute-done((bf16[1,32,768]{2,1,0:T(8,128)(2,1)S(1)}, bf16[1,32,768]{2,1,0:T(8,128)(2,1)S(1)}, u32[]{:S(2)}, u32[]{:S(2)}) %collective-permute-start.4) | collective-permute-done | bytes 49184 | tf_op jit(solution)/shard_map/ppermute | solution.py:208
  18.1 0.0 collective-permute-done.3
  18.1 0.2 collective-permute-start.7
  18.4 2.4 %add_across.1.before_ref = f32[768,16]{1,0:T(8,128)S(1)} custom-call(s32[8,2,16]{2,1,0:T(2,128)S(1)} %get-tuple-element.19.table_ref, bf16[768,64]{1,0:T(8,128)(2,1)S(1)} %get-tuple-element.21.left_ref, bf16[4,32,768]{2,1,0:T(8,128)(2,1)S(1)} %constant_dynamic-update-slice_fusion.blocks_ref, ...), custom_call_target="tpu_custom_call", output_to_operand_aliasing={{}: (3, {})} | custom-call | tf_op jit(solution)/shard_map/add_across/pallas_call | solution.py:234
  20.7 0.0 collective-permute-done.7.blocks_ref
  20.8 2.0 %add_far.1 = (f32[16,768]{1,0:T(8,128)S(1)}, f32[16,8,128]{2,1,0:T(8,128)S(1)}) custom-call(s32[8,2,16]{2,1,0:T(2,128)S(1)} %get-tuple-element.19.table_ref, bf16[768,64]{1,0:T(8,128)(2,1)S(1)} %get-tuple-element.21.left_ref, bf16[4,32,768]{2,1,0:T(8,128)(2,1)S(1)} %collective-permute-done.7.blocks_ref, f32[768,16]{1,0:T(8,128)S(1)} %add_across.1.before_ref, ...), custom_call_target="tpu_custom_call" | custom-call | tf_op jit(solution)/shard_map/add_far/pallas_call | solution.py:234
  22.8 11.6 %all_to_all.5.grams_ref = f32[16,8,128]{2,1,0:T(8,128)S(1)} all-to-all(f32[16,8,128]{2,1,0:T(8,128)S(1)} %get-tuple-element.34), channel_id=1, replica_groups=mesh['grp'=2,'row'=4,'col'=4] {'row','col'}, dimensions={0} | all-to-all | bytes 131072 | tf_op jit(solution)/shard_map/all_to_all | solution.py:326
  34.4 1.3 %finish.1 = (f32[16,768]{1,0:T(8,128)}, f32[16,16]{1,0:T(8,128)}) custom-call(f32[16,8,128]{2,1,0:T(8,128)S(1)} %all_to_all.5.grams_ref, f32[16,768]{1,0:T(8,128)S(1)} %get-tuple-element.35.applied_ref), custom_call_target="tpu_custom_call" | custom-call | tf_op jit(solution)/shard_map/finish/pallas_call | solution.py:234
  (6 shorter events, 0.1 us)
Async XLA Ops:
  1.4 7.3 %collective-permute-start.2 = (bf16[32,768]{1,0:T(8,128)(2,1)S(1)}, bf16[32,768]{1,0:T(8,128)(2,1)S(1)}, u32[]{:S(2)}, u32[]{:S(2)}) collective-permute-start(bf16[32,768]{1,0:T(8,128)(2,1)S(1)} %get-tuple-element.20.packed_ref), channel_id=1, source_target_pairs={{0,3},{1,2},{2,1},{3,0},{4,7},{5,6},{6,5},{7,4},{8,11},{9,10},{10,... | collective-permute-start | bytes 147464 | tf_op jit(solution)/shard_map/ppermute | solution.py:208
  3.9 5.1 %collective-permute-start = (bf16[32,768]{1,0:T(8,128)(2,1)S(1)}, bf16[32,768]{1,0:T(8,128)(2,1)S(1)}, u32[]{:S(2)}, u32[]{:S(2)}) collective-permute-start(bf16[32,768]{1,0:T(8,128)(2,1)S(1)} %get-tuple-element.20.packed_ref), channel_id=1, source_target_pairs={{0,9},{1,8},{2,11},{3,10},{4,13},{5,12},{6,15},{7,14},{8,1},{9,0},... | collective-permute-start | bytes 147464 | tf_op jit(solution)/shard_map/ppermute | solution.py:208
  6.8 3.9 %collective-permute-start.1 = (bf16[32,768]{1,0:T(8,128)(2,1)S(1)}, bf16[32,768]{1,0:T(8,128)(2,1)S(1)}, u32[]{:S(2)}, u32[]{:S(2)}) collective-permute-start(bf16[32,768]{1,0:T(8,128)(2,1)S(1)} %get-tuple-element.20.packed_ref), channel_id=1, source_target_pairs={{0,5},{1,4},{2,7},{3,6},{4,1},{5,0},{6,3},{7,2},{8,13},{9,12},{10,... | collective-permute-start | bytes 147464 | tf_op jit(solution)/shard_map/ppermute | solution.py:208
  10.7 3.1 %collective-permute-start.6 = (bf16[4,32,768]{2,1,0:T(8,128)(2,1)S(1)}, bf16[4,32,768]{2,1,0:T(8,128)(2,1)S(1)}, u32[]{:S(2)}, u32[]{:S(2)}) collective-permute-start(bf16[4,32,768]{2,1,0:T(8,128)(2,1)S(1)} %pad_maximum_fusion.1), channel_id=1, source_target_pairs={{0,1},{1,0},{2,3},{3,2},{4,5},{5,4},{6,7},{7,6},{8,9},{9,8},{10,11... | collective-permute-start | bytes 589832 | tf_op jit(solution)/shard_map/ppermute | solution.py:208
  10.9 4.6 %collective-permute-start.5 = (bf16[1,32,768]{2,1,0:T(8,128)(2,1)S(1)}, bf16[1,32,768]{2,1,0:T(8,128)(2,1)S(1)}, u32[]{:S(2)}, u32[]{:S(2)}) collective-permute-start(bf16[1,32,768]{2,1,0:T(8,128)(2,1)S(1)} %bitcast.10), channel_id=1, source_target_pairs={{0,5},{1,4},{2,7},{3,6},{4,1},{5,0},{6,3},{7,2},{8,13},{9,12},{10,... | collective-permute-start | bytes 147464 | tf_op jit(solution)/shard_map/ppermute | solution.py:208
  12.6 5.5 %collective-permute-start.4 = (bf16[1,32,768]{2,1,0:T(8,128)(2,1)S(1)}, bf16[1,32,768]{2,1,0:T(8,128)(2,1)S(1)}, u32[]{:S(2)}, u32[]{:S(2)}) collective-permute-start(bf16[1,32,768]{2,1,0:T(8,128)(2,1)S(1)} %bitcast.7), channel_id=1, source_target_pairs={{0,13},{1,12},{2,15},{3,14},{4,9},{5,8},{6,11},{7,10},{8,5},{9,4},... | collective-permute-start | bytes 147464 | tf_op jit(solution)/shard_map/ppermute | solution.py:208
  13.3 4.8 %collective-permute-start.3 = (bf16[2,32,768]{2,1,0:T(8,128)(2,1)S(1)}, bf16[2,32,768]{2,1,0:T(8,128)(2,1)S(1)}, u32[]{:S(2)}, u32[]{:S(2)}) collective-permute-start(bf16[2,32,768]{2,1,0:T(8,128)(2,1)S(1)} %pad_maximum_fusion.2), channel_id=1, source_target_pairs={{0,3},{1,2},{2,1},{3,0},{4,7},{5,6},{6,5},{7,4},{8,11},{9,10},{10,... | collective-permute-start | bytes 294920 | tf_op jit(solution)/shard_map/ppermute | solution.py:208
  18.1 2.6 %collective-permute-start.7 = (bf16[4,32,768]{2,1,0:T(8,128)(2,1)S(1)}, bf16[4,32,768]{2,1,0:T(8,128)(2,1)S(1)}, u32[]{:S(2)}, u32[]{:S(2)}) collective-permute-start(bf16[4,32,768]{2,1,0:T(8,128)(2,1)S(1)} %constant_dynamic-update-slice_fusion.blocks_ref), channel_id=1, source_target_pairs={{0,1},{1,0},{2,3},{3,2},{4,5},{5,4},{6,7},{7,6},{8,9},{9,8},{10,11... | collective-permute-start | bytes 589832 | tf_op jit(solution)/shard_map/ppermute | solution.py:208

commit v13 on v12

--- a/solution.py
+++ b/solution.py
@@ -62,28 +62,24 @@
     return jnp.concatenate([high, mid, low, edge], axis=0).T.astype(jnp.bfloat16)
 
 
-def tile_image(left_ref, kern_ref, blocks):
+def tile_image(left_ref, blocks):
     both = blocks[0] if len(blocks) == 1 else jnp.concatenate(blocks, axis=1)
     ncv = both.shape[0] // 2
     x, v = both[:ncv, :], both[ncv:, :]
     wide = x.astype(jnp.float32)
     edge = edge_rows(jnp.sum(wide * wide, axis=0, keepdims=True), False).astype(jnp.bfloat16)
     right = jnp.concatenate([x, x, x, edge], axis=0)
-    chunk, total = 256, right.shape[1]
-    for start in range(0, total, chunk):
-        power = jnp.dot(
-            left_ref[...], right[:, start : start + chunk], preferred_element_type=jnp.float32
-        )
-        kern_ref[:, start : start + chunk] = jnp.exp2(power).astype(jnp.bfloat16)
-    return lax.dot_general(kern_ref[:, :total], v, NT, preferred_element_type=jnp.float32)
-
-
-def own_kernel(packed_ref, left_ref, image_ref, kern_ref):
+    power = jnp.dot(left_ref[...], right, preferred_element_type=jnp.float32)
+    kern = jnp.exp2(power).astype(jnp.bfloat16)
+    return lax.dot_general(kern, v, NT, preferred_element_type=jnp.float32)
+
+
+def own_kernel(packed_ref, left_ref, image_ref):
     left_ref[...] = own_side(packed_ref[: packed_ref.shape[0] // 2, :])
-    image_ref[...] = tile_image(left_ref, kern_ref, [packed_ref[...]])
-
-
-def add_blocks(places, sizes, table_ref, left_ref, blocks_ref, image_ref, list_ref, kern_ref):
+    image_ref[...] = tile_image(left_ref, [packed_ref[...]])
+
+
+def add_blocks(places, sizes, table_ref, left_ref, blocks_ref, image_ref, list_ref):
     n_row, n_col = sizes
     my_row, my_col = lax.axis_index("row"), lax.axis_index("col")
     me = my_row * n_col + my_col
@@ -107,29 +103,27 @@
 
     def visit(pair, _):
         blocks = [blocks_ref[list_ref[2 * pair]], blocks_ref[list_ref[2 * pair + 1]]]
-        image_ref[...] += tile_image(left_ref, kern_ref, blocks)
+        image_ref[...] += tile_image(left_ref, blocks)
         return 0
 
     lax.fori_loop(0, count // 2, visit, 0)
 
     @pl.when(count % 2 == 1)
     def _():
-        image_ref[...] += tile_image(left_ref, kern_ref, [blocks_ref[list_ref[count - 1]]])
-
-
-def part_kernel(
-    places, sizes, table_ref, left_ref, blocks_ref, before_ref, image_ref, list_ref, kern_ref
+        image_ref[...] += tile_image(left_ref, [blocks_ref[list_ref[count - 1]]])
+
+
+def part_kernel(places, sizes, table_ref, left_ref, blocks_ref, before_ref, image_ref, list_ref):
+    image_ref[...] = before_ref[...]
+    add_blocks(places, sizes, table_ref, left_ref, blocks_ref, image_ref, list_ref)
+
+
+def last_kernel(
+    places, sizes, table_ref, left_ref, blocks_ref, before_ref, vectors_ref, root_ref,
+    applied_ref, gram_ref, image_ref, list_ref,
 ):
     image_ref[...] = before_ref[...]
-    add_blocks(places, sizes, table_ref, left_ref, blocks_ref, image_ref, list_ref, kern_ref)
-
-
-def last_kernel(
-    places, sizes, table_ref, left_ref, blocks_ref, before_ref, vectors_ref, root_ref,
-    applied_ref, gram_ref, image_ref, list_ref, kern_ref,
-):
-    image_ref[...] = before_ref[...]
-    add_blocks(places, sizes, table_ref, left_ref, blocks_ref, image_ref, list_ref, kern_ref)
+    add_blocks(places, sizes, table_ref, left_ref, blocks_ref, image_ref, list_ref)
     n = vectors_ref.shape[0]
     applied = image_ref[...].T * root_ref[...]
     applied_ref[...] = applied
@@ -214,8 +208,8 @@
 
 def exchange_plan(n_row, n_col):
     if (n_row, n_col) == (4, 4):
-        direct = [(0, 3), (2, 1), (1, 1)]
-        return direct, [((0, 3), [(1, 1), (2, 1)]), ((3, 1), [(0, 3)]), ((1, 1), [(2, 1)])]
+        direct = [(0, 3), (1, 1), (3, 1), (2, 1)]
+        return direct, [((0, 3), [(2, 1), (3, 1)]), ((1, 1), [(0, 3)])]
     lines = [(r, 1) for r in range(1, n_row)]
     chips = [(0, c) for c in range(3, n_col, 2)]
     return chips + lines, [(chip, lines) for chip in chips]
@@ -242,7 +236,6 @@
         )(*args)
 
     image_type = ((rows, nvec), jnp.float32)
-    kern_scratch = pltpu.VMEM((rows, 2 * rows), jnp.bfloat16)
 
     table = tile_table.transpose(1, 2, 0)
     packed, vectors, root, table = call(
@@ -272,7 +265,6 @@
         "own",
         [((rows, 3 * ncv + 16), jnp.bfloat16), image_type],
         packed,
-        scratch_shapes=[kern_scratch],
     )
 
     def add(name, places, blocks, image):
@@ -285,7 +277,7 @@
             blocks,
             image,
             input_output_aliases={3: 0},
-            scratch_shapes=[pltpu.SMEM((len(places) + 1,), jnp.int32), kern_scratch],
+            scratch_shapes=[pltpu.SMEM((len(places) + 1,), jnp.int32)],
         )
         return image
 
@@ -320,7 +312,6 @@
         scratch_shapes=[
             pltpu.VMEM(*image_type),
             pltpu.SMEM((len(far_places) + 1,), jnp.int32),
-            kern_scratch,
         ],
     )
     grams = lax.all_to_all(gram, ("row", "col"), 0, 0)

time: 35.3 us -> 35.2 us (level); the launches traced: 35.6 us -> 35 us
  starting transfers between devices: 9.65 us -> 7.65 us
  waiting for transfers between devices: 4.31 us -> 5.26 us
  blocking collectives: 11.6 us -> 12 us
    ppermute x8, starting transfers between devices: 9.65 us -> 7.65 us  [sent(): return lax.ppermute(x, ('row', 'col'), pairs)]
    ppermute x8, waiting for transfers between devices: 4.31 us -> 5.26 us  [sent(): return lax.ppermute(x, ('row', 'col'), pairs)]
    all_to_all x1, blocking collectives: 11.6 us -> 12 us  [per_device(): grams = lax.all_to_all(gram, ('row', 'col'), 0, 0)]
  transfers between devices with their start and end apart: 8 -> 8, of which waited for: 2 -> 3; matrix products, arithmetic and copies ran while one was open for 0% -> 0% of each run, Pallas kernels for 15% -> 16%
where the time goes in v13:
time: 35.2 us; the launch traced here: 35 us
  blocking collectives  12 us (34%)
  Pallas kernels  9.25 us (26%)
  starting transfers between devices  7.65 us (22%)
  waiting for transfers between devices  5.26 us (15%)
  between operations  0.75 us (2%)
    all_to_all x1, blocking collectives, per_device(): grams = lax.all_to_all(gram, ('row', 'col'), 0, 0)  12 us
    pallas_call x7, Pallas kernels, call(): pl.pallas_call(kernel, out_shape=shapes, in_specs=[where] * len(args), ou...  9.25 us
    ppermute x8, starting transfers between devices, sent(): return lax.ppermute(x, ('row', 'col'), pairs)  7.65 us
    ppermute x8, waiting for transfers between devices, sent(): return lax.ppermute(x, ('row', 'col'), pairs)  5.26 us
  transfers between devices with their start and end apart: 8, of which 3 were waited for; matrix products, arithmetic and copies ran while one was open for 0% of the time, Pallas kernels for 16%

profile of v13, /device:TPU:0, one launch (start us, length us, event | category | flops | bytes accessed | tf_op | source)
XLA Modules:
  0.0 35.0 jit_solution(13088186680334935845)
XLA Ops:
  0.6 0.8 %pack.1 = (bf16[32,768]{1,0:T(8,128)(2,1)S(1)}, bf16[16,768]{1,0:T(8,128)(2,1)S(1)}, f32[1,768]{1,0:T(1,128)S(1)}, s32[8,2,16]{2,1,0:T(2,128)S(1)}) custom-call(bf16[16,768]{1,0:T(8,128)(2,1)} %frames_ref.1, bf16[16,768]{1,0:T(8,128)(2,1)} %vectors_in.1, f32[768]{0:T(1024)} %degrees_ref.1, s32[8,2,16]{2,1,0:T(2,128)} %bitcast.18), custom_call_target="tpu_custom_call" | custom-call | tf_op jit(solution)/shard_map/pack/pallas_call | solution.py:228
  1.4 2.4 %collective-permute-start.3 = (bf16[32,768]{1,0:T(8,128)(2,1)S(1)}, bf16[32,768]{1,0:T(8,128)(2,1)S(1)}, u32[]{:S(2)}, u32[]{:S(2)}) collective-permute-start(bf16[32,768]{1,0:T(8,128)(2,1)S(1)} %get-tuple-element.20.packed_ref), channel_id=1, source_target_pairs={{0,3},{1,2},{2,1},{3,0},{4,7},{5,6},{6,5},{7,4},{8,11},{9,10},{10,... | collective-permute-start | bytes 147464 | tf_op jit(solution)/shard_map/ppermute | solution.py:202
  3.9 2.9 %collective-permute-start.2 = (bf16[32,768]{1,0:T(8,128)(2,1)S(1)}, bf16[32,768]{1,0:T(8,128)(2,1)S(1)}, u32[]{:S(2)}, u32[]{:S(2)}) collective-permute-start(bf16[32,768]{1,0:T(8,128)(2,1)S(1)} %get-tuple-element.20.packed_ref), channel_id=1, source_target_pairs={{0,9},{1,8},{2,11},{3,10},{4,13},{5,12},{6,15},{7,14},{8,1},{9,0},... | collective-permute-start | bytes 147464 | tf_op jit(solution)/shard_map/ppermute | solution.py:202
  6.8 1.0 %collective-permute-start.1 = (bf16[32,768]{1,0:T(8,128)(2,1)S(1)}, bf16[32,768]{1,0:T(8,128)(2,1)S(1)}, u32[]{:S(2)}, u32[]{:S(2)}) collective-permute-start(bf16[32,768]{1,0:T(8,128)(2,1)S(1)} %get-tuple-element.20.packed_ref), channel_id=1, source_target_pairs={{0,13},{1,12},{2,15},{3,14},{4,9},{5,8},{6,11},{7,10},{8,5},{9,4},... | collective-permute-start | bytes 147464 | tf_op jit(solution)/shard_map/ppermute | solution.py:202
  7.8 0.0 collective-permute-start
  7.8 0.9 %own.1 = (bf16[768,64]{1,0:T(8,128)(2,1)S(1)}, f32[768,16]{1,0:T(8,128)S(1)}) custom-call(bf16[32,768]{1,0:T(8,128)(2,1)S(1)} %get-tuple-element.20.packed_ref), custom_call_target="tpu_custom_call" | custom-call | tf_op jit(solution)/shard_map/own/pallas_call | solution.py:228
  8.7 0.0 collective-permute-done.3
  8.8 0.2 add_first.1.before_ref
  9.0 0.0 collective-permute-done.2
  9.0 3.7 %collective-permute-done.1 = bf16[32,768]{1,0:T(8,128)(2,1)S(1)} collective-permute-done((bf16[32,768]{1,0:T(8,128)(2,1)S(1)}, bf16[32,768]{1,0:T(8,128)(2,1)S(1)}, u32[]{:S(2)}, u32[]{:S(2)}) %collective-permute-start.1) | collective-permute-done | bytes 49184 | tf_op jit(solution)/shard_map/ppermute | solution.py:202
  12.7 0.0 collective-permute-done
  12.8 0.1 collective-permute-start.6
  12.9 0.7 %collective-permute-start.5 = (bf16[1,32,768]{2,1,0:T(8,128)(2,1)S(1)}, bf16[1,32,768]{2,1,0:T(8,128)(2,1)S(1)}, u32[]{:S(2)}, u32[]{:S(2)}) collective-permute-start(bf16[1,32,768]{2,1,0:T(8,128)(2,1)S(1)} %bitcast.12), channel_id=1, source_target_pairs={{0,5},{1,4},{2,7},{3,6},{4,1},{5,0},{6,3},{7,2},{8,13},{9,12},{10,... | collective-permute-start | bytes 147464 | tf_op jit(solution)/shard_map/ppermute | solution.py:202
  13.6 0.2 collective-permute-start.4
  13.9 0.5 %collective-permute-done.6 = bf16[5,32,768]{2,1,0:T(8,128)(2,1)S(1)} collective-permute-done((bf16[5,32,768]{2,1,0:T(8,128)(2,1)S(1)}, bf16[5,32,768]{2,1,0:T(8,128)(2,1)S(1)}, u32[]{:S(2)}, u32[]{:S(2)}) %collective-permute-start.6) | collective-permute-done | bytes 245792 | tf_op jit(solution)/shard_map/ppermute | solution.py:202
  14.4 3.0 %add_near.1.before_ref = f32[768,16]{1,0:T(8,128)S(1)} custom-call(s32[8,2,16]{2,1,0:T(2,128)S(1)} %get-tuple-element.19.table_ref, bf16[768,64]{1,0:T(8,128)(2,1)S(1)} %get-tuple-element.21.left_ref, bf16[8,32,768]{2,1,0:T(8,128)(2,1)S(1)} %pad_maximum_fusion.blocks_ref, f32[768,16]{1,0:T(8,128)S(1)} %add_first.1.before_ref), custom_call_target="tpu_custom_call", output_to_operand_aliasing={{}: (3, {})} | custom-call | tf_op jit(solution)/shard_map/add_near/pallas_call | solution.py:228
  17.4 0.0 collective-permute-done.5
  17.4 1.1 %collective-permute-done.4 = bf16[2,32,768]{2,1,0:T(8,128)(2,1)S(1)} collective-permute-done((bf16[2,32,768]{2,1,0:T(8,128)(2,1)S(1)}, bf16[2,32,768]{2,1,0:T(8,128)(2,1)S(1)}, u32[]{:S(2)}, u32[]{:S(2)}) %collective-permute-start.4) | collective-permute-done | bytes 98336 | tf_op jit(solution)/shard_map/ppermute | solution.py:202
  18.5 0.2 collective-permute-start.7
  18.7 1.6 %add_across.1.before_ref = f32[768,16]{1,0:T(8,128)S(1)} custom-call(s32[8,2,16]{2,1,0:T(2,128)S(1)} %get-tuple-element.19.table_ref, bf16[768,64]{1,0:T(8,128)(2,1)S(1)} %get-tuple-element.21.left_ref, bf16[3,32,768]{2,1,0:T(8,128)(2,1)S(1)} %constant_dynamic-update-slice_fusion.4.blocks_ref, ...), custom_call_target="tpu_custom_call", output_to_operand_aliasing={{}: (3, {})} | custom-call | tf_op jit(solution)/shard_map/add_across/pallas_call | solution.py:228
  20.3 0.0 collective-permute-done.7.blocks_ref
  20.3 1.4 %add_far.1 = (f32[16,768]{1,0:T(8,128)S(1)}, f32[16,8,128]{2,1,0:T(8,128)S(1)}) custom-call(s32[8,2,16]{2,1,0:T(2,128)S(1)} %get-tuple-element.19.table_ref, bf16[768,64]{1,0:T(8,128)(2,1)S(1)} %get-tuple-element.21.left_ref, bf16[3,32,768]{2,1,0:T(8,128)(2,1)S(1)} %collective-permute-done.7.blocks_ref, f32[768,16]{1,0:T(8,128)S(1)} %add_across.1.before_ref, ...), custom_call_target="tpu_custom_call" | custom-call | tf_op jit(solution)/shard_map/add_far/pallas_call | solution.py:228
  21.7 12.0 %all_to_all.5.grams_ref = f32[16,8,128]{2,1,0:T(8,128)S(1)} all-to-all(f32[16,8,128]{2,1,0:T(8,128)S(1)} %get-tuple-element.34), channel_id=1, replica_groups=mesh['grp'=2,'row'=4,'col'=4] {'row','col'}, dimensions={0} | all-to-all | bytes 131072 | tf_op jit(solution)/shard_map/all_to_all | solution.py:317
  33.7 1.3 %finish.1 = (f32[16,768]{1,0:T(8,128)}, f32[16,16]{1,0:T(8,128)}) custom-call(f32[16,8,128]{2,1,0:T(8,128)S(1)} %all_to_all.5.grams_ref, f32[16,768]{1,0:T(8,128)S(1)} %get-tuple-element.35.applied_ref), custom_call_target="tpu_custom_call" | custom-call | tf_op jit(solution)/shard_map/finish/pallas_call | solution.py:228
  (9 shorter events, 0.1 us)
Async XLA Ops:
  1.4 7.3 %collective-permute-start.3 = (bf16[32,768]{1,0:T(8,128)(2,1)S(1)}, bf16[32,768]{1,0:T(8,128)(2,1)S(1)}, u32[]{:S(2)}, u32[]{:S(2)}) collective-permute-start(bf16[32,768]{1,0:T(8,128)(2,1)S(1)} %get-tuple-element.20.packed_ref), channel_id=1, source_target_pairs={{0,3},{1,2},{2,1},{3,0},{4,7},{5,6},{6,5},{7,4},{8,11},{9,10},{10,... | collective-permute-start | bytes 147464 | tf_op jit(solution)/shard_map/ppermute | solution.py:202
  3.9 5.1 %collective-permute-start.2 = (bf16[32,768]{1,0:T(8,128)(2,1)S(1)}, bf16[32,768]{1,0:T(8,128)(2,1)S(1)}, u32[]{:S(2)}, u32[]{:S(2)}) collective-permute-start(bf16[32,768]{1,0:T(8,128)(2,1)S(1)} %get-tuple-element.20.packed_ref), channel_id=1, source_target_pairs={{0,9},{1,8},{2,11},{3,10},{4,13},{5,12},{6,15},{7,14},{8,1},{9,0},... | collective-permute-start | bytes 147464 | tf_op jit(solution)/shard_map/ppermute | solution.py:202
  6.8 6.0 %collective-permute-start.1 = (bf16[32,768]{1,0:T(8,128)(2,1)S(1)}, bf16[32,768]{1,0:T(8,128)(2,1)S(1)}, u32[]{:S(2)}, u32[]{:S(2)}) collective-permute-start(bf16[32,768]{1,0:T(8,128)(2,1)S(1)} %get-tuple-element.20.packed_ref), channel_id=1, source_target_pairs={{0,13},{1,12},{2,15},{3,14},{4,9},{5,8},{6,11},{7,10},{8,5},{9,4},... | collective-permute-start | bytes 147464 | tf_op jit(solution)/shard_map/ppermute | solution.py:202
  7.8 5.0 %collective-permute-start = (bf16[32,768]{1,0:T(8,128)(2,1)S(1)}, bf16[32,768]{1,0:T(8,128)(2,1)S(1)}, u32[]{:S(2)}, u32[]{:S(2)}) collective-permute-start(bf16[32,768]{1,0:T(8,128)(2,1)S(1)} %get-tuple-element.20.packed_ref), channel_id=1, source_target_pairs={{0,5},{1,4},{2,7},{3,6},{4,1},{5,0},{6,3},{7,2},{8,13},{9,12},{10,... | collective-permute-start | bytes 147464 | tf_op jit(solution)/shard_map/ppermute | solution.py:202
  12.8 1.6 %collective-permute-start.6 = (bf16[5,32,768]{2,1,0:T(8,128)(2,1)S(1)}, bf16[5,32,768]{2,1,0:T(8,128)(2,1)S(1)}, u32[]{:S(2)}, u32[]{:S(2)}) collective-permute-start(bf16[5,32,768]{2,1,0:T(8,128)(2,1)S(1)} %constant_dynamic-update-slice_fusion), channel_id=1, source_target_pairs={{0,1},{1,0},{2,3},{3,2},{4,5},{5,4},{6,7},{7,6},{8,9},{9,8},{10,11... | collective-permute-start | bytes 737288 | tf_op jit(solution)/shard_map/ppermute | solution.py:202
  12.9 4.5 %collective-permute-start.5 = (bf16[1,32,768]{2,1,0:T(8,128)(2,1)S(1)}, bf16[1,32,768]{2,1,0:T(8,128)(2,1)S(1)}, u32[]{:S(2)}, u32[]{:S(2)}) collective-permute-start(bf16[1,32,768]{2,1,0:T(8,128)(2,1)S(1)} %bitcast.12), channel_id=1, source_target_pairs={{0,5},{1,4},{2,7},{3,6},{4,1},{5,0},{6,3},{7,2},{8,13},{9,12},{10,... | collective-permute-start | bytes 147464 | tf_op jit(solution)/shard_map/ppermute | solution.py:202
  13.6 4.8 %collective-permute-start.4 = (bf16[2,32,768]{2,1,0:T(8,128)(2,1)S(1)}, bf16[2,32,768]{2,1,0:T(8,128)(2,1)S(1)}, u32[]{:S(2)}, u32[]{:S(2)}) collective-permute-start(bf16[2,32,768]{2,1,0:T(8,128)(2,1)S(1)} %pad_maximum_fusion.1), channel_id=1, source_target_pairs={{0,3},{1,2},{2,1},{3,0},{4,7},{5,6},{6,5},{7,4},{8,11},{9,10},{10,... | collective-permute-start | bytes 294920 | tf_op jit(solution)/shard_map/ppermute | solution.py:202
  18.5 1.8 %collective-permute-start.7 = (bf16[3,32,768]{2,1,0:T(8,128)(2,1)S(1)}, bf16[3,32,768]{2,1,0:T(8,128)(2,1)S(1)}, u32[]{:S(2)}, u32[]{:S(2)}) collective-permute-start(bf16[3,32,768]{2,1,0:T(8,128)(2,1)S(1)} %constant_dynamic-update-slice_fusion.4.blocks_ref), channel_id=1, source_target_pairs={{0,1},{1,0},{2,3},{3,2},{4,5},{5,4},{6,7},{7,6},{8,9},{9,8},{10,11... | collective-permute-start | bytes 442376 | tf_op jit(solution)/shard_map/ppermute | solution.py:202

commit v14 on v13

--- a/solution.py
+++ b/solution.py
@@ -208,7 +208,7 @@
 
 def exchange_plan(n_row, n_col):
     if (n_row, n_col) == (4, 4):
-        direct = [(0, 3), (1, 1), (3, 1), (2, 1)]
+        direct = [(0, 3), (3, 1), (1, 1), (2, 1)]
         return direct, [((0, 3), [(2, 1), (3, 1)]), ((1, 1), [(0, 3)])]
     lines = [(r, 1) for r in range(1, n_row)]
     chips = [(0, c) for c in range(3, n_col, 2)]

time: 35.2 us -> 34.7 us (0.986)
  Pallas kernels: 9.25 us -> 12 us
  blocking collectives: 12 us -> 9.49 us
  waiting for transfers between devices: 5.26 us -> 3.65 us
  starting transfers between devices: 7.65 us -> 8.32 us
    pallas_call x7, Pallas kernels: 9.25 us -> 12 us  [call(): pl.pallas_call(kernel, out_shape=shapes, in_specs=[where] * len(args), ou...]
    all_to_all x1, blocking collectives: 12 us -> 9.49 us  [per_device(): grams = lax.all_to_all(gram, ('row', 'col'), 0, 0)]
    ppermute x8, waiting for transfers between devices: 5.26 us -> 3.65 us  [sent(): return lax.ppermute(x, ('row', 'col'), pairs)]
    ppermute x8, starting transfers between devices: 7.65 us -> 8.32 us  [sent(): return lax.ppermute(x, ('row', 'col'), pairs)]
  transfers between devices with their start and end apart: 8 -> 8, of which waited for: 3 -> 3; matrix products, arithmetic and copies ran while one was open for 0% -> 0% of each run, Pallas kernels for 16% -> 23%
where the time goes in v14:
time: 34.7 us; the launch traced here: 34.3 us
  Pallas kernels  12 us (35%)
  blocking collectives  9.49 us (27%)
  starting transfers between devices  8.32 us (24%)
  waiting for transfers between devices  3.65 us (11%)
  between operations  0.76 us (2%)
    pallas_call x7, Pallas kernels, call(): pl.pallas_call(kernel, out_shape=shapes, in_specs=[where] * len(args), ou...  12 us
    all_to_all x1, blocking collectives, per_device(): grams = lax.all_to_all(gram, ('row', 'col'), 0, 0)  9.49 us
    ppermute x8, starting transfers between devices, sent(): return lax.ppermute(x, ('row', 'col'), pairs)  8.32 us
    ppermute x8, waiting for transfers between devices, sent(): return lax.ppermute(x, ('row', 'col'), pairs)  3.65 us
  transfers between devices with their start and end apart: 8, of which 3 were waited for; matrix products, arithmetic and copies ran while one was open for 0% of the time, Pallas kernels for 23%

profile of v14, /device:TPU:0, one launch (start us, length us, event | category | flops | bytes accessed | tf_op | source)
XLA Modules:
  0.0 34.3 jit_solution(6304699946827766663)
XLA Ops:
  0.6 0.8 %pack.1 = (bf16[32,768]{1,0:T(8,128)(2,1)S(1)}, bf16[16,768]{1,0:T(8,128)(2,1)S(1)}, f32[1,768]{1,0:T(1,128)S(1)}, s32[8,2,16]{2,1,0:T(2,128)S(1)}) custom-call(bf16[16,768]{1,0:T(8,128)(2,1)} %frames_ref.1, bf16[16,768]{1,0:T(8,128)(2,1)} %vectors_in.1, f32[768]{0:T(1024)} %degrees_ref.1, s32[8,2,16]{2,1,0:T(2,128)} %bitcast.18), custom_call_target="tpu_custom_call" | custom-call | tf_op jit(solution)/shard_map/pack/pallas_call | solution.py:228
  1.4 2.4 %collective-permute-start.3 = (bf16[32,768]{1,0:T(8,128)(2,1)S(1)}, bf16[32,768]{1,0:T(8,128)(2,1)S(1)}, u32[]{:S(2)}, u32[]{:S(2)}) collective-permute-start(bf16[32,768]{1,0:T(8,128)(2,1)S(1)} %get-tuple-element.20.packed_ref), channel_id=1, source_target_pairs={{0,3},{1,2},{2,1},{3,0},{4,7},{5,6},{6,5},{7,4},{8,11},{9,10},{10,... | collective-permute-start | bytes 147464 | tf_op jit(solution)/shard_map/ppermute | solution.py:202
  3.9 2.9 %collective-permute-start.2 = (bf16[32,768]{1,0:T(8,128)(2,1)S(1)}, bf16[32,768]{1,0:T(8,128)(2,1)S(1)}, u32[]{:S(2)}, u32[]{:S(2)}) collective-permute-start(bf16[32,768]{1,0:T(8,128)(2,1)S(1)} %get-tuple-element.20.packed_ref), channel_id=1, source_target_pairs={{0,9},{1,8},{2,11},{3,10},{4,13},{5,12},{6,15},{7,14},{8,1},{9,0},... | collective-permute-start | bytes 147464 | tf_op jit(solution)/shard_map/ppermute | solution.py:202
  6.8 1.0 %collective-permute-start.1 = (bf16[32,768]{1,0:T(8,128)(2,1)S(1)}, bf16[32,768]{1,0:T(8,128)(2,1)S(1)}, u32[]{:S(2)}, u32[]{:S(2)}) collective-permute-start(bf16[32,768]{1,0:T(8,128)(2,1)S(1)} %get-tuple-element.20.packed_ref), channel_id=1, source_target_pairs={{0,5},{1,4},{2,7},{3,6},{4,1},{5,0},{6,3},{7,2},{8,13},{9,12},{10,... | collective-permute-start | bytes 147464 | tf_op jit(solution)/shard_map/ppermute | solution.py:202
  7.8 0.5 %collective-permute-start = (bf16[32,768]{1,0:T(8,128)(2,1)S(1)}, bf16[32,768]{1,0:T(8,128)(2,1)S(1)}, u32[]{:S(2)}, u32[]{:S(2)}) collective-permute-start(bf16[32,768]{1,0:T(8,128)(2,1)S(1)} %get-tuple-element.20.packed_ref), channel_id=1, source_target_pairs={{0,13},{1,12},{2,15},{3,14},{4,9},{5,8},{6,11},{7,10},{8,5},{9,4},... | collective-permute-start | bytes 147464 | tf_op jit(solution)/shard_map/ppermute | solution.py:202
  8.3 0.9 %own.1 = (bf16[768,64]{1,0:T(8,128)(2,1)S(1)}, f32[768,16]{1,0:T(8,128)S(1)}) custom-call(bf16[32,768]{1,0:T(8,128)(2,1)S(1)} %get-tuple-element.20.packed_ref), custom_call_target="tpu_custom_call" | custom-call | tf_op jit(solution)/shard_map/own/pallas_call | solution.py:228
  9.2 0.0 collective-permute-done.3
  9.3 1.0 %add_first.1.before_ref = f32[768,16]{1,0:T(8,128)S(1)} custom-call(s32[8,2,16]{2,1,0:T(2,128)S(1)} %get-tuple-element.19.table_ref, bf16[768,64]{1,0:T(8,128)(2,1)S(1)} %get-tuple-element.21.left_ref, bf16[1,32,768]{2,1,0:T(8,128)(2,1)S(1)} %bitcast.11, f32[768,16]{1,0:T(8,128)S(1)} %get-tuple-element.24.before_ref), custom_call_target="tpu_custom_call", output_to_operand_aliasing={{}: (3, {})} | custom-call | tf_op jit(solution)/shard_map/add_first/pallas_call | solution.py:228
  10.3 0.0 collective-permute-done.2
  10.3 0.4 %collective-permute-done.1 = bf16[32,768]{1,0:T(8,128)(2,1)S(1)} collective-permute-done((bf16[32,768]{1,0:T(8,128)(2,1)S(1)}, bf16[32,768]{1,0:T(8,128)(2,1)S(1)}, u32[]{:S(2)}, u32[]{:S(2)}) %collective-permute-start.1) | collective-permute-done | bytes 49184 | tf_op jit(solution)/shard_map/ppermute | solution.py:202
  10.7 2.4 %collective-permute-done = bf16[32,768]{1,0:T(8,128)(2,1)S(1)} collective-permute-done((bf16[32,768]{1,0:T(8,128)(2,1)S(1)}, bf16[32,768]{1,0:T(8,128)(2,1)S(1)}, u32[]{:S(2)}, u32[]{:S(2)}) %collective-permute-start) | collective-permute-done | bytes 49184 | tf_op jit(solution)/shard_map/ppermute | solution.py:202
  13.1 0.7 %collective-permute-start.6 = (bf16[5,32,768]{2,1,0:T(8,128)(2,1)S(1)}, bf16[5,32,768]{2,1,0:T(8,128)(2,1)S(1)}, u32[]{:S(2)}, u32[]{:S(2)}) collective-permute-start(bf16[5,32,768]{2,1,0:T(8,128)(2,1)S(1)} %constant_dynamic-update-slice_fusion), channel_id=1, source_target_pairs={{0,1},{1,0},{2,3},{3,2},{4,5},{5,4},{6,7},{7,6},{8,9},{9,8},{10,11... | collective-permute-start | bytes 737288 | tf_op jit(solution)/shard_map/ppermute | solution.py:202
  13.9 0.0 collective-permute-start.5
  13.9 0.3 collective-permute-start.4
  14.2 0.8 %collective-permute-done.6 = bf16[5,32,768]{2,1,0:T(8,128)(2,1)S(1)} collective-permute-done((bf16[5,32,768]{2,1,0:T(8,128)(2,1)S(1)}, bf16[5,32,768]{2,1,0:T(8,128)(2,1)S(1)}, u32[]{:S(2)}, u32[]{:S(2)}) %collective-permute-start.6) | collective-permute-done | bytes 245792 | tf_op jit(solution)/shard_map/ppermute | solution.py:202
  15.0 4.4 %add_near.1.before_ref = f32[768,16]{1,0:T(8,128)S(1)} custom-call(s32[8,2,16]{2,1,0:T(2,128)S(1)} %get-tuple-element.19.table_ref, bf16[768,64]{1,0:T(8,128)(2,1)S(1)} %get-tuple-element.21.left_ref, bf16[8,32,768]{2,1,0:T(8,128)(2,1)S(1)} %pad_maximum_fusion.blocks_ref, f32[768,16]{1,0:T(8,128)S(1)} %add_first.1.before_ref), custom_call_target="tpu_custom_call", output_to_operand_aliasing={{}: (3, {})} | custom-call | tf_op jit(solution)/shard_map/add_near/pallas_call | solution.py:228
  19.4 0.0 collective-permute-done.5
  19.4 0.0 collective-permute-done.4
  19.5 0.5 %collective-permute-start.7 = (bf16[3,32,768]{2,1,0:T(8,128)(2,1)S(1)}, bf16[3,32,768]{2,1,0:T(8,128)(2,1)S(1)}, u32[]{:S(2)}, u32[]{:S(2)}) collective-permute-start(bf16[3,32,768]{2,1,0:T(8,128)(2,1)S(1)} %constant_dynamic-update-slice_fusion.4.blocks_ref), channel_id=1, source_target_pairs={{0,1},{1,0},{2,3},{3,2},{4,5},{5,4},{6,7},{7,6},{8,9},{9,8},{10,11... | collective-permute-start | bytes 442376 | tf_op jit(solution)/shard_map/ppermute | solution.py:202
  19.9 1.6 %add_across.1.before_ref = f32[768,16]{1,0:T(8,128)S(1)} custom-call(s32[8,2,16]{2,1,0:T(2,128)S(1)} %get-tuple-element.19.table_ref, bf16[768,64]{1,0:T(8,128)(2,1)S(1)} %get-tuple-element.21.left_ref, bf16[3,32,768]{2,1,0:T(8,128)(2,1)S(1)} %constant_dynamic-update-slice_fusion.4.blocks_ref, ...), custom_call_target="tpu_custom_call", output_to_operand_aliasing={{}: (3, {})} | custom-call | tf_op jit(solution)/shard_map/add_across/pallas_call | solution.py:228
  21.5 0.0 collective-permute-done.7.blocks_ref
  21.5 2.0 %add_far.1 = (f32[16,768]{1,0:T(8,128)S(1)}, f32[16,8,128]{2,1,0:T(8,128)S(1)}) custom-call(s32[8,2,16]{2,1,0:T(2,128)S(1)} %get-tuple-element.19.table_ref, bf16[768,64]{1,0:T(8,128)(2,1)S(1)} %get-tuple-element.21.left_ref, bf16[3,32,768]{2,1,0:T(8,128)(2,1)S(1)} %collective-permute-done.7.blocks_ref, f32[768,16]{1,0:T(8,128)S(1)} %add_across.1.before_ref, ...), custom_call_target="tpu_custom_call" | custom-call | tf_op jit(solution)/shard_map/add_far/pallas_call | solution.py:228
  23.5 9.5 %all_to_all.5.grams_ref = f32[16,8,128]{2,1,0:T(8,128)S(1)} all-to-all(f32[16,8,128]{2,1,0:T(8,128)S(1)} %get-tuple-element.34), channel_id=1, replica_groups=mesh['grp'=2,'row'=4,'col'=4] {'row','col'}, dimensions={0} | all-to-all | bytes 131072 | tf_op jit(solution)/shard_map/all_to_all | solution.py:317
  33.0 1.3 %finish.1 = (f32[16,768]{1,0:T(8,128)}, f32[16,16]{1,0:T(8,128)}) custom-call(f32[16,8,128]{2,1,0:T(8,128)S(1)} %all_to_all.5.grams_ref, f32[16,768]{1,0:T(8,128)S(1)} %get-tuple-element.35.applied_ref), custom_call_target="tpu_custom_call" | custom-call | tf_op jit(solution)/shard_map/finish/pallas_call | solution.py:228
  (9 shorter events, 0.1 us)
Async XLA Ops:
  1.4 7.8 %collective-permute-start.3 = (bf16[32,768]{1,0:T(8,128)(2,1)S(1)}, bf16[32,768]{1,0:T(8,128)(2,1)S(1)}, u32[]{:S(2)}, u32[]{:S(2)}) collective-permute-start(bf16[32,768]{1,0:T(8,128)(2,1)S(1)} %get-tuple-element.20.packed_ref), channel_id=1, source_target_pairs={{0,3},{1,2},{2,1},{3,0},{4,7},{5,6},{6,5},{7,4},{8,11},{9,10},{10,... | collective-permute-start | bytes 147464 | tf_op jit(solution)/shard_map/ppermute | solution.py:202
  3.9 6.4 %collective-permute-start.2 = (bf16[32,768]{1,0:T(8,128)(2,1)S(1)}, bf16[32,768]{1,0:T(8,128)(2,1)S(1)}, u32[]{:S(2)}, u32[]{:S(2)}) collective-permute-start(bf16[32,768]{1,0:T(8,128)(2,1)S(1)} %get-tuple-element.20.packed_ref), channel_id=1, source_target_pairs={{0,9},{1,8},{2,11},{3,10},{4,13},{5,12},{6,15},{7,14},{8,1},{9,0},... | collective-permute-start | bytes 147464 | tf_op jit(solution)/shard_map/ppermute | solution.py:202
  6.8 3.9 %collective-permute-start.1 = (bf16[32,768]{1,0:T(8,128)(2,1)S(1)}, bf16[32,768]{1,0:T(8,128)(2,1)S(1)}, u32[]{:S(2)}, u32[]{:S(2)}) collective-permute-start(bf16[32,768]{1,0:T(8,128)(2,1)S(1)} %get-tuple-element.20.packed_ref), channel_id=1, source_target_pairs={{0,5},{1,4},{2,7},{3,6},{4,1},{5,0},{6,3},{7,2},{8,13},{9,12},{10,... | collective-permute-start | bytes 147464 | tf_op jit(solution)/shard_map/ppermute | solution.py:202
  7.8 5.3 %collective-permute-start = (bf16[32,768]{1,0:T(8,128)(2,1)S(1)}, bf16[32,768]{1,0:T(8,128)(2,1)S(1)}, u32[]{:S(2)}, u32[]{:S(2)}) collective-permute-start(bf16[32,768]{1,0:T(8,128)(2,1)S(1)} %get-tuple-element.20.packed_ref), channel_id=1, source_target_pairs={{0,13},{1,12},{2,15},{3,14},{4,9},{5,8},{6,11},{7,10},{8,5},{9,4},... | collective-permute-start | bytes 147464 | tf_op jit(solution)/shard_map/ppermute | solution.py:202
  13.1 1.9 %collective-permute-start.6 = (bf16[5,32,768]{2,1,0:T(8,128)(2,1)S(1)}, bf16[5,32,768]{2,1,0:T(8,128)(2,1)S(1)}, u32[]{:S(2)}, u32[]{:S(2)}) collective-permute-start(bf16[5,32,768]{2,1,0:T(8,128)(2,1)S(1)} %constant_dynamic-update-slice_fusion), channel_id=1, source_target_pairs={{0,1},{1,0},{2,3},{3,2},{4,5},{5,4},{6,7},{7,6},{8,9},{9,8},{10,11... | collective-permute-start | bytes 737288 | tf_op jit(solution)/shard_map/ppermute | solution.py:202
  13.9 5.6 %collective-permute-start.5 = (bf16[1,32,768]{2,1,0:T(8,128)(2,1)S(1)}, bf16[1,32,768]{2,1,0:T(8,128)(2,1)S(1)}, u32[]{:S(2)}, u32[]{:S(2)}) collective-permute-start(bf16[1,32,768]{2,1,0:T(8,128)(2,1)S(1)} %bitcast.12), channel_id=1, source_target_pairs={{0,5},{1,4},{2,7},{3,6},{4,1},{5,0},{6,3},{7,2},{8,13},{9,12},{10,... | collective-permute-start | bytes 147464 | tf_op jit(solution)/shard_map/ppermute | solution.py:202
  13.9 5.6 %collective-permute-start.4 = (bf16[2,32,768]{2,1,0:T(8,128)(2,1)S(1)}, bf16[2,32,768]{2,1,0:T(8,128)(2,1)S(1)}, u32[]{:S(2)}, u32[]{:S(2)}) collective-permute-start(bf16[2,32,768]{2,1,0:T(8,128)(2,1)S(1)} %pad_maximum_fusion.1), channel_id=1, source_target_pairs={{0,3},{1,2},{2,1},{3,0},{4,7},{5,6},{6,5},{7,4},{8,11},{9,10},{10,... | collective-permute-start | bytes 294920 | tf_op jit(solution)/shard_map/ppermute | solution.py:202
  19.5 2.0 %collective-permute-start.7 = (bf16[3,32,768]{2,1,0:T(8,128)(2,1)S(1)}, bf16[3,32,768]{2,1,0:T(8,128)(2,1)S(1)}, u32[]{:S(2)}, u32[]{:S(2)}) collective-permute-start(bf16[3,32,768]{2,1,0:T(8,128)(2,1)S(1)} %constant_dynamic-update-slice_fusion.4.blocks_ref), channel_id=1, source_target_pairs={{0,1},{1,0},{2,3},{3,2},{4,5},{5,4},{6,7},{7,6},{8,9},{9,8},{10,11... | collective-permute-start | bytes 442376 | tf_op jit(solution)/shard_map/ppermute | solution.py:202
